TPU v7x, 32 devices: a whole 2x2x4 slice. The times are simulated.
32 devices in a mesh: groups: 2 (over y), row: 8 (over z, core), col: 2 (over x).
Axes of the slice: x: 2, y: 2, z: 4, core: 2. Of those that a mesh axis runs over, the one named last changes fastest.
Arguments:
- slab: bfloat16 [64, 512, 2048], P(('groups', 'col'), 'row'), parts along dimension 0, may hold values from -32 to 32
- factor_one: bfloat16 [2048, 128], replicated, may hold values from -0.125 to 0.125
- factor_two: bfloat16 [512, 128], P('row'), may hold values from -0.25 to 0.25
Outputs:
- gram: float32 [64, 32], P(('groups', 'col'), 'row'), parts along dimension 0
There are 2 independent parts, one for each index of `groups`. A program takes and returns all parts, laid end to end along the dimension named above; an argument that names none is the same for every part. Nothing has to cross between parts.
All inputs are finite; a program needn't handle non-finite values.
Results may differ from a plain program's by a relative error of at most 0.0003.
Values sent between devices are 32-bit elements; how exact they have to be, the bound alone decides.
No kernel may reach another device: no remote copies, remote signals or barrier semaphores. Data moves between devices by JAX's collectives and lax.ppermute only.
A program may use at most 64 MiB of HBM per device.

v0:
```python
import jax
import jax.numpy as jnp
from jax import lax
from jax.sharding import PartitionSpec as P

R1 = 128
R2 = 128


def per_device(slab, factor_one, factor_two):
    first = jnp.einsum("kji,ir->rkj", slab, factor_one, preferred_element_type=jnp.float32).astype(
        jnp.bfloat16
    )
    partial_value = jnp.einsum("rkj,js->rks", first, factor_two, preferred_element_type=jnp.float32)
    core_share = lax.psum_scatter(partial_value, "row", scatter_dimension=0, tiled=True)
    gram_rows = jnp.einsum(
        "rks,rls->kl",
        core_share,
        lax.all_gather(core_share, "col", axis=1, tiled=True),
        precision=lax.Precision.HIGHEST,
    )
    summed = lax.psum_scatter(gram_rows, "row", scatter_dimension=1, tiled=True)
    return summed / float(R1 * R2)


def solution(mesh):
    in_specs = (P(("groups", "col"), "row", None), P(), P("row", None))
    out_specs = P(("groups", "col"), "row")
    return jax.shard_map(
        per_device, mesh=mesh, in_specs=in_specs, out_specs=out_specs, check_vma=False
    )
```

profile of v0, /device:TPU:0, one launch (start us, length us, event | category | flops | bytes accessed | tf_op | source)
XLA Modules:
  0.0 88.3 jit_solution(11832498037244615819)
XLA Ops:
  6.5 0.0 copy-start
  6.5 0.0 copy-start.1
  6.5 0.0 reduce-scatter.2.cloned.1.call-start
  6.5 1.0 %copy-done = bf16[2048,128]{1,0:T(8,128)(2,1)S(1)} copy-done((bf16[2048,128]{1,0:T(8,128)(2,1)S(1)}, bf16[2048,128]{1,0:T(8,128)(2,1)}, u32[]{:S(2)}) %copy-start) | copy-done | bytes 524312
  7.6 4.8 %fusion = f32[128,16,128]{2,0,1:T(8,128)} fusion(bf16[16,64,2048]{2,1,0:T(8,128)(2,1)} %param.3, bf16[2048,128]{1,0:T(8,128)(2,1)S(1)} %copy-done, bf16[64,128]{1,0:T(8,128)(2,1)} %param.5), kind=kOutput, calls=%fused_computation.1 | convolution fusion | flops 570556416 | bytes 5783552 | tf_op jit(solution)/shard_map/rkj,js->rks/dot_general | solution.py:14
  12.3 0.0 reduce-scatter.2.cloned.1.call-update
  12.4 0.0 copy-done.1
  12.4 0.6 dynamic-slice
  13.6 33.9 %reduce-scatter.2.cloned.1.call-done = f32[16,16,128]{2,0,1:T(8,128)} async-done(((f32[128,16,128]{2,0,1:T(8,128)}), f32[16,16,128]{2,0,1:T(8,128)}) %reduce-scatter.2.cloned.1.call-update) | async-done | bytes 131088 | tf_op jit(solution)/shard_map/reduce_scatter | solution.py:15
  47.5 5.8 %all_gather.3 = f32[16,32,128]{2,0,1:T(8,128)S(1)} all-gather(f32[16,16,128]{2,0,1:T(8,128)} %reduce-scatter.2.cloned.1.call-done), channel_id=1, replica_groups=mesh['groups'=2,'row'=8,'col'=2] {'col'}, dimensions={1}, use_global_device_ids=true | all-gather | bytes 393216 | tf_op jit(solution)/shard_map/all_gather | solution.py:19
  53.4 1.3 %convolution_bitcast_fusion = f32[16,32]{0,1:T(8,128)S(1)} fusion(f32[16,32,128]{2,0,1:T(8,128)S(1)} %all_gather.3, f32[16,16,128]{2,0,1:T(8,128)} %reduce-scatter.2.cloned.1.call-done), kind=kOutput, calls=%fused_computation.2 | convolution fusion | flops 12582912 | bytes 395264 | tf_op jit(solution)/shard_map/rks,rls->kl/dot_general | solution.py:16
  54.7 26.2 %all-reduce = f32[16,32]{0,1:T(8,128)S(1)} all-reduce(f32[16,32]{0,1:T(8,128)S(1)} %convolution_bitcast_fusion), channel_id=3, replica_groups=mesh['groups'=2,'row'=8,'col'=2] {'row'}, use_global_device_ids=true, to_apply=%region_1.0.clone | all-reduce | flops 512 | bytes 4096
  80.9 0.6 dynamic-slice_multiply_fusion
Async XLA Ops:
  6.5 1.0 %copy-start = (bf16[2048,128]{1,0:T(8,128)(2,1)S(1)}, bf16[2048,128]{1,0:T(8,128)(2,1)}, u32[]{:S(2)}) copy-start(bf16[2048,128]{1,0:T(8,128)(2,1)} %param.4) | copy-start | bytes 1572868
  6.5 5.8 %copy-start.1 = (u32[32]{0:T(128)S(1)}, u32[32]{0:T(128)}, u32[]{:S(2)}) copy-start(u32[32]{0:T(128)} %constant.5) | copy-start | bytes 388
  6.5 41.0 %reduce-scatter.2.cloned.1.call-start = ((), (), s32[]{:S(2)}) async-start(), calls=%async_computation.1 | async-start | bytes 1179648 | tf_op jit(solution)/shard_map/reduce_scatter | solution.py:15
Sparse Core Ops, SparseCore 0:
  12.5 35.0 reduce-scatter.1
where the time goes:
time: 88.5 us; the launch traced here: 88.3 us
  waiting for transfers between devices  33.9 us (38%)
  blocking collectives  32 us (36%)
  between operations  14.1 us (16%)
  matrix products  6.07 us (7%)
  local copies, waits for them, and re-layouts  1.63 us (2%)
    reduce_scatter x1, waiting for transfers between devices, per_device(): lax.psum_scatter(partial_value, 'row', scatter_dimension=0, tiled=True)  33.9 us
    unnamed x1, blocking collectives  26.2 us
    all_gather x1, blocking collectives, per_device(): lax.all_gather(core_share, 'col', axis=1, tiled=True)  5.84 us
    dot_general x1, matrix products, per_device(): jnp.einsum('rkj,js->rks', first, factor_two, preferred_element_type=jnp.f...  4.76 us
  transfers between devices with their start and end apart: 1, of which 1 were waited for; matrix products, arithmetic and copies ran while one was open for 1% of the time, Pallas kernels for 0%

commit v1 on v0

v1 whole, which is shorter than its diff:
```python
import functools

import jax
import jax.numpy as jnp
from jax import lax
from jax.experimental import pallas as pl
from jax.experimental.pallas import tpu as pltpu
from jax.sharding import Mesh, PartitionSpec as P

TILE = 8
CORES = 2
CHUNK = 4


def project_kernel(chunk, slab_ref, one_ref, two_ref, own_ref, other_ref, slab_buf, one_buf, turned, sems):
    depth, width, _ = slab_ref.shape
    chunks = depth // chunk
    half = turned.shape[0] // CORES
    one_copy = pltpu.make_async_copy(one_ref, one_buf, sems.at[chunks])
    one_copy.start()
    copies = []
    for c in range(chunks):
        part = pl.ds(c * chunk, chunk)
        copies.append(pltpu.make_async_copy(slab_ref.at[part], slab_buf.at[part], sems.at[c]))
        copies[-1].start()
    turned[...] = two_ref[...].astype(jnp.float32).T
    core = lax.axis_index("core")
    two_own = turned[pl.ds(pl.multiple_of(core * half, half), half), :].astype(jnp.bfloat16)
    two_other = turned[pl.ds(pl.multiple_of((1 - core) * half, half), half), :].astype(jnp.bfloat16)
    one_copy.wait()
    for c in range(chunks):
        copies[c].wait()
        rows = slab_buf[pl.ds(c * chunk, chunk)].reshape(chunk * width, -1)
        first = jnp.dot(rows, one_buf[...], preferred_element_type=jnp.float32).astype(jnp.bfloat16)
        for q in range(chunk):
            k = c * chunk + q
            piece = first[q * width : (q + 1) * width]
            for two, out in ((two_other, other_ref), (two_own, own_ref)):
                core_part = jnp.dot(two, piece, preferred_element_type=jnp.float32)
                out[:, k] = core_part.reshape(half // TILE, TILE, -1)


def project(slab, factor_one, factor_two):
    depth, width, length = slab.shape
    r1, r2 = factor_one.shape[1], factor_two.shape[1]
    half = r2 // CORES
    chunk = CHUNK if depth % CHUNK == 0 else 1
    out = jax.ShapeDtypeStruct((half // TILE, depth, TILE, r1), jnp.float32)
    return pl.pallas_call(
        functools.partial(project_kernel, chunk),
        out_shape=(out, out),
        in_specs=[
            pl.BlockSpec(memory_space=pl.ANY),
            pl.BlockSpec(memory_space=pl.ANY),
            pl.BlockSpec(memory_space=pltpu.VMEM),
        ],
        out_specs=[pl.BlockSpec(memory_space=pltpu.VMEM)] * 2,
        scratch_shapes=[
            pltpu.VMEM(slab.shape, slab.dtype),
            pltpu.VMEM(factor_one.shape, factor_one.dtype),
            pltpu.VMEM((r2, width), jnp.float32),
            pltpu.SemaphoreType.DMA((depth // chunk + 1,)),
        ],
        compiler_params=pltpu.CompilerParams(vmem_limit_bytes=32 * 2**20),
        cost_estimate=pl.CostEstimate(
            flops=2 * depth * width * r1 * (length + r2),
            bytes_accessed=2 * (slab.size + factor_one.size) + 8 * depth * half * r1,
            transcendentals=0,
        ),
    )(slab, factor_one, factor_two)


def gram_kernel(cols, scale, parts_ref, out_ref, total):
    sources, depth, tile, _ = parts_ref.shape
    for x in range(cols):
        value = parts_ref[x]
        for z in range(1, sources // cols):
            value = value + parts_ref[z * cols + x]
        total[pl.ds(x * depth * tile, depth * tile), :] = value.reshape(depth * tile, -1)
    full = cols * depth
    gram = jnp.zeros((full, full), jnp.float32)
    for s in range(tile):
        rows = total[pl.ds(s, full, stride=tile), :]
        gram = gram + lax.dot_general(
            rows,
            rows,
            (((1,), (1,)), ((), ())),
            precision=lax.Precision.HIGHEST,
            preferred_element_type=jnp.float32,
        )
    gram = gram * scale
    devices = out_ref.shape[0]
    share = full // (devices // cols)
    for d in range(devices):
        x = d % cols
        start = d // cols * share
        out_ref[d, 0:share, 0:depth] = gram[start : start + share, x * depth : (x + 1) * depth]


def gram_blocks(parts, cols, rows, scale):
    _, depth, tile, r1 = parts.shape
    full = cols * depth
    return pl.pallas_call(
        functools.partial(gram_kernel, cols, scale),
        out_shape=jax.ShapeDtypeStruct((rows * cols, TILE, 128), jnp.float32),
        in_specs=[pl.BlockSpec(memory_space=pltpu.VMEM)],
        out_specs=pl.BlockSpec(memory_space=pltpu.VMEM),
        scratch_shapes=[pltpu.VMEM((full * tile, r1), jnp.float32)],
        cost_estimate=pl.CostEstimate(
            flops=2 * full * full * tile * r1, bytes_accessed=4 * parts.size, transcendentals=0
        ),
    )(parts)


def per_device(sizes, slab, factor_one, factor_two):
    zs, cols = sizes
    depth = slab.shape[0]
    r1, r2 = factor_one.shape[1], factor_two.shape[1]
    scale = 1.0 / (r1 * r2)
    own, other = project(slab, factor_one, factor_two)
    own = own + lax.ppermute(other, "core", [(0, 1), (1, 0)])
    pieces = zs * cols
    full = cols * depth
    rows = zs * CORES
    if own.shape[0] == pieces and full % rows == 0 and full // rows <= TILE and depth <= 128:
        parts = lax.all_to_all(own, ("z", "col"), 0, 0, tiled=True)
        blocks = gram_blocks(parts, cols, rows, scale)
        blocks = lax.all_to_all(blocks, ("z", "core", "col"), 0, 0, tiled=True)
        return blocks[:, : full // rows, :depth].sum(0).T
    own = own.transpose(0, 2, 1, 3).reshape(r2 // CORES, depth, r1)
    share = lax.psum_scatter(own, "z", scatter_dimension=0, tiled=True)
    whole = lax.all_gather(share, "col", axis=1, tiled=True)
    gram = jnp.einsum("skr,slr->kl", share, whole, precision=lax.Precision.HIGHEST)
    return lax.psum_scatter(gram, ("z", "core"), scatter_dimension=1, tiled=True) * scale


def solution(mesh):
    groups, rows, cols = mesh.devices.shape
    zs = rows // CORES
    fine = Mesh(mesh.devices.reshape(groups, zs, CORES, cols), ("groups", "z", "core", "col"))
    row = ("z", "core")
    return jax.shard_map(
        functools.partial(per_device, (zs, cols)),
        mesh=fine,
        in_specs=(P(("groups", "col"), row, None), P(), P(row, None)),
        out_specs=P(("groups", "col"), row),
        check_vma=False,
    )
```

time: 88.5 us -> 44.2 us (0.50)
  waiting for transfers between devices: 33.9 us -> 1.54 us
  between operations: 14.1 us -> 0.02 us
  matrix products: 6.07 us -> 0 us
  Pallas kernels: 0 us -> 4.83 us
  local copies, waits for them, and re-layouts: 1.63 us -> 3.95 us
    reduce_scatter x1 -> x0, waiting for transfers between devices: 33.9 us -> none  [per_device(): lax.psum_scatter(partial_value, 'row', scatter_dimension=0, tiled=True)]
    all_to_all x0 -> x2, blocking collectives: none -> 32.3 us  [the longest x1 21.9 us: per_device(): parts = lax.all_to_all(own, ('z', 'col'), 0, 0, tiled=True)]
    unnamed x1 -> x0, blocking collectives: 26.2 us -> none
    dot_general x2 -> x0, matrix products: 6.07 us -> none  [the longest x1 4.76 us: per_device(): jnp.einsum('rkj,js->rks', first, factor_two, preferred_element_type=jnp.f...]
    all_gather x1 -> x0, blocking collectives: 5.84 us -> none  [per_device(): lax.all_gather(core_share, 'col', axis=1, tiled=True)]
    pallas_call x0 -> x2, Pallas kernels: none -> 4.83 us  [the longest x1 2.73 us: project(): pl.pallas_call(functools.partial(project_kernel, chunk), out_shape=(out,...]
    unnamed x5 -> x6, local copies, waits for them, and re-layouts: 1.63 us -> 3.95 us
    ppermute x0 -> x1, waiting for transfers between devices: none -> 1.54 us  [per_device(): own = own + lax.ppermute(other, 'core', [(0, 1), (1, 0)])]
  transfers between devices with their start and end apart: 1 -> 1, of which waited for: 1 -> 1; matrix products, arithmetic and copies ran while one was open for 1% -> 0% of each run, Pallas kernels for 0% -> 0%
where the time goes in v1:
time: 44.2 us; the launch traced here: 43.8 us
  blocking collectives  32.3 us (73%)
  Pallas kernels  4.83 us (11%)
  local copies, waits for them, and re-layouts  3.95 us (9%)
  waiting for transfers between devices  1.54 us (3%)
  other arithmetic  0.68 us (2%)
  starting transfers between devices  0.52 us (1%)
    all_to_all x1, blocking collectives, per_device(): parts = lax.all_to_all(own, ('z', 'col'), 0, 0, tiled=True)  21.9 us
    all_to_all x1, blocking collectives, per_device(): blocks = lax.all_to_all(blocks, ('z', 'core', 'col'), 0, 0, tiled=True)  10.4 us
    unnamed x6, local copies, waits for them, and re-layouts  3.95 us
    pallas_call x1, Pallas kernels, project(): pl.pallas_call(functools.partial(project_kernel, chunk), out_shape=(out,...  2.73 us
    pallas_call x1, Pallas kernels, gram_blocks(): pl.pallas_call(functools.partial(gram_kernel, cols, scale), out_shape=jax...  2.09 us
    ppermute x1, waiting for transfers between devices, per_device(): own = own + lax.ppermute(other, 'core', [(0, 1), (1, 0)])  1.54 us
  transfers between devices with their start and end apart: 1, of which 1 were waited for; matrix products, arithmetic and copies ran while one was open for 0% of the time, Pallas kernels for 0%

profile of v1, /device:TPU:0, one launch (start us, length us, event | category | flops | bytes accessed | tf_op | source)
XLA Modules:
  0.0 43.8 jit_solution(6374908249483950048)
XLA Ops:
  0.0 0.0 copy-start
  0.0 2.2 %copy-done = bf16[16,64,2048]{2,1,0:T(8,128)(2,1)S(1)} copy-done((bf16[16,64,2048]{2,1,0:T(8,128)(2,1)S(1)}, bf16[16,64,2048]{2,1,0:T(8,128)(2,1)}, u32[]{:S(2)}) %copy-start) | copy-done | bytes 4194328
  2.2 0.0 copy-start.1
  2.2 1.0 %copy-done.1 = bf16[2048,128]{1,0:T(8,128)(2,1)S(1)} copy-done((bf16[2048,128]{1,0:T(8,128)(2,1)S(1)}, bf16[2048,128]{1,0:T(8,128)(2,1)}, u32[]{:S(2)}) %copy-start.1) | copy-done | bytes 524312
  3.2 0.0 copy-start.2
  3.2 0.7 %copy-done.2 = bf16[64,128]{1,0:T(8,128)(2,1)S(1)} copy-done((bf16[64,128]{1,0:T(8,128)(2,1)S(1)}, bf16[64,128]{1,0:T(8,128)(2,1)}, u32[]{:S(2)}) %copy-start.2) | copy-done | bytes 16408
  3.9 2.7 %shard_map.37 = (f32[8,16,8,128]{3,2,1,0:T(8,128)S(1)}, f32[8,16,8,128]{3,2,1,0:T(8,128)S(1)}) custom-call(bf16[16,64,2048]{2,1,0:T(8,128)(2,1)S(1)} %copy-done, bf16[2048,128]{1,0:T(8,128)(2,1)S(1)} %copy-done.1, bf16[64,128]{1,0:T(8,128)(2,1)S(1)} %copy-done.2), custom_call_target="tpu_custom_call" | custom-call | flops 570425344 | bytes 5767168 | tf_op jit(solution)/shard_map/pallas_call | solution.py:49
  6.7 0.5 %collective-permute-start = (f32[8,16,8,128]{3,2,1,0:T(8,128)S(1)}, f32[8,16,8,128]{3,2,1,0:T(8,128)S(1)}, u32[]{:S(2)}, u32[]{:S(2)}) collective-permute-start(f32[8,16,8,128]{3,2,1,0:T(8,128)S(1)} %get-tuple-element.8), channel_id=1, source_target_pairs={{0,2},{2,0},{1,3},{3,1},{4,6},{6,4},{5,7},{7,5},{8,10},{10,8},{9,1... | collective-permute-start | bytes 1572872 | tf_op jit(solution)/shard_map/ppermute | solution.py:121
  7.2 1.5 %collective-permute-done = f32[8,16,8,128]{3,2,1,0:T(8,128)S(1)} collective-permute-done((f32[8,16,8,128]{3,2,1,0:T(8,128)S(1)}, f32[8,16,8,128]{3,2,1,0:T(8,128)S(1)}, u32[]{:S(2)}, u32[]{:S(2)}) %collective-permute-start) | collective-permute-done | bytes 524320 | tf_op jit(solution)/shard_map/ppermute | solution.py:121
  8.7 0.1 add.3
  8.8 21.9 %all_to_all.10.parts_ref = f32[8,16,8,128]{3,2,1,0:T(8,128)} all-to-all(f32[8,16,8,128]{3,2,1,0:T(8,128)S(1)} %add.3), channel_id=1, replica_groups=mesh['groups'=2,'z'=4,'core'=2,'col'=2] {'z','col'}, dimensions={0} | all-to-all | bytes 1048576 | tf_op jit(solution)/shard_map/all_to_all | solution.py:126
  30.7 2.1 %shard_map.38 = f32[16,8,128]{2,1,0:T(8,128)} custom-call(f32[8,16,8,128]{3,2,1,0:T(8,128)} %all_to_all.10.parts_ref), custom_call_target="tpu_custom_call" | custom-call | flops 2097152 | bytes 524288 | tf_op jit(solution)/shard_map/pallas_call | solution.py:103
  32.8 10.4 %all_to_all.11 = f32[16,8,128]{2,1,0:T(8,128)S(1)} all-to-all(f32[16,8,128]{2,1,0:T(8,128)} %shard_map.38), channel_id=1, replica_groups=mesh['groups'=2,'z'=4,'core'=2,'col'=2] {'z','core','col'}, dimensions={0} | all-to-all | bytes 131072 | tf_op jit(solution)/shard_map/all_to_all | solution.py:128
  43.2 0.6 %slice_reduce_fusion = f32[4,16]{1,0:T(4,128)} fusion(f32[16,8,128]{2,1,0:T(8,128)S(1)} %all_to_all.11), kind=kLoop, calls=%fused_computation | loop fusion | flops 960 | bytes 4352 | tf_op jit(solution)/shard_map/reduce_sum | solution.py:129
Async XLA Ops:
  0.0 2.2 %copy-start = (bf16[16,64,2048]{2,1,0:T(8,128)(2,1)S(1)}, bf16[16,64,2048]{2,1,0:T(8,128)(2,1)}, u32[]{:S(2)}) copy-start(bf16[16,64,2048]{2,1,0:T(8,128)(2,1)} %slab_ref.1) | copy-start | bytes 12582916
  2.2 1.0 %copy-start.1 = (bf16[2048,128]{1,0:T(8,128)(2,1)S(1)}, bf16[2048,128]{1,0:T(8,128)(2,1)}, u32[]{:S(2)}) copy-start(bf16[2048,128]{1,0:T(8,128)(2,1)} %one_ref.1) | copy-start | bytes 1572868
  3.2 0.7 %copy-start.2 = (bf16[64,128]{1,0:T(8,128)(2,1)S(1)}, bf16[64,128]{1,0:T(8,128)(2,1)}, u32[]{:S(2)}) copy-start(bf16[64,128]{1,0:T(8,128)(2,1)} %two_ref.1) | copy-start | bytes 49156
  6.7 2.1 %collective-permute-start = (f32[8,16,8,128]{3,2,1,0:T(8,128)S(1)}, f32[8,16,8,128]{3,2,1,0:T(8,128)S(1)}, u32[]{:S(2)}, u32[]{:S(2)}) collective-permute-start(f32[8,16,8,128]{3,2,1,0:T(8,128)S(1)} %get-tuple-element.8), channel_id=1, source_target_pairs={{0,2},{2,0},{1,3},{3,1},{4,6},{6,4},{5,7},{7,5},{8,10},{10,8},{9,1... | collective-permute-start | bytes 1572872 | tf_op jit(solution)/shard_map/ppermute | solution.py:121

commit v2 on v1

--- a/solution.py
+++ b/solution.py
@@ -12,18 +12,21 @@
 CHUNK = 4
 
 
-def project_kernel(chunk, slab_ref, one_ref, two_ref, own_ref, other_ref, slab_buf, one_buf, turned, sems):
+def project_kernel(chunk, slab_ref, one_ref, two_ref, own_ref, other_ref, slab_buf, one_buf, two_buf, turned, sems):
     depth, width, _ = slab_ref.shape
     chunks = depth // chunk
     half = turned.shape[0] // CORES
     one_copy = pltpu.make_async_copy(one_ref, one_buf, sems.at[chunks])
     one_copy.start()
+    two_copy = pltpu.make_async_copy(two_ref, two_buf, sems.at[chunks + 1])
+    two_copy.start()
     copies = []
     for c in range(chunks):
         part = pl.ds(c * chunk, chunk)
         copies.append(pltpu.make_async_copy(slab_ref.at[part], slab_buf.at[part], sems.at[c]))
         copies[-1].start()
-    turned[...] = two_ref[...].astype(jnp.float32).T
+    two_copy.wait()
+    turned[...] = two_buf[...].astype(jnp.float32).T
     core = lax.axis_index("core")
     two_own = turned[pl.ds(pl.multiple_of(core * half, half), half), :].astype(jnp.bfloat16)
     two_other = turned[pl.ds(pl.multiple_of((1 - core) * half, half), half), :].astype(jnp.bfloat16)
@@ -45,21 +48,22 @@
     r1, r2 = factor_one.shape[1], factor_two.shape[1]
     half = r2 // CORES
     chunk = CHUNK if depth % CHUNK == 0 else 1
-    out = jax.ShapeDtypeStruct((half // TILE, depth, TILE, r1), jnp.float32)
+    out = pltpu.VMEM((half // TILE, depth, TILE, r1), jnp.float32)
     return pl.pallas_call(
         functools.partial(project_kernel, chunk),
         out_shape=(out, out),
         in_specs=[
-            pl.BlockSpec(memory_space=pl.ANY),
-            pl.BlockSpec(memory_space=pl.ANY),
-            pl.BlockSpec(memory_space=pltpu.VMEM),
+            pl.BlockSpec(memory_space=pltpu.HBM),
+            pl.BlockSpec(memory_space=pltpu.HBM),
+            pl.BlockSpec(memory_space=pltpu.HBM),
         ],
         out_specs=[pl.BlockSpec(memory_space=pltpu.VMEM)] * 2,
         scratch_shapes=[
             pltpu.VMEM(slab.shape, slab.dtype),
             pltpu.VMEM(factor_one.shape, factor_one.dtype),
+            pltpu.VMEM(factor_two.shape, factor_two.dtype),
             pltpu.VMEM((r2, width), jnp.float32),
-            pltpu.SemaphoreType.DMA((depth // chunk + 1,)),
+            pltpu.SemaphoreType.DMA((depth // chunk + 2,)),
         ],
         compiler_params=pltpu.CompilerParams(vmem_limit_bytes=32 * 2**20),
         cost_estimate=pl.CostEstimate(
@@ -67,7 +71,7 @@
             bytes_accessed=2 * (slab.size + factor_one.size) + 8 * depth * half * r1,
             transcendentals=0,
         ),
-    )(slab, factor_one, factor_two)
+    )(*(pltpu.with_memory_space_constraint(a, pltpu.HBM) for a in (slab, factor_one, factor_two)))
 
 
 def gram_kernel(cols, scale, parts_ref, out_ref, total):
@@ -102,7 +106,7 @@
     full = cols * depth
     return pl.pallas_call(
         functools.partial(gram_kernel, cols, scale),
-        out_shape=jax.ShapeDtypeStruct((rows * cols, TILE, 128), jnp.float32),
+        out_shape=pltpu.VMEM((rows * cols, TILE, 128), jnp.float32),
         in_specs=[pl.BlockSpec(memory_space=pltpu.VMEM)],
         out_specs=pl.BlockSpec(memory_space=pltpu.VMEM),
         scratch_shapes=[pltpu.VMEM((full * tile, r1), jnp.float32)],

time: 44.2 us -> 40.2 us (0.910)
  local copies, waits for them, and re-layouts: 3.95 us -> 0 us
    unnamed x6 -> x0, local copies, waits for them, and re-layouts: 3.95 us -> none
    pallas_call x1, Pallas kernels: 2.73 us -> 3.72 us  [project(): pl.pallas_call(functools.partial(project_kernel, chunk), out_shape=(out,...]
    pallas_call x1, Pallas kernels: 2.09 us -> 1.45 us  [gram_blocks(): pl.pallas_call(functools.partial(gram_kernel, cols, scale), out_shape=plt...]
where the time goes in v2:
time: 40.2 us; the launch traced here: 40 us
  blocking collectives  32.1 us (80%)
  Pallas kernels  5.17 us (13%)
  waiting for transfers between devices  1.54 us (4%)
  other arithmetic  0.68 us (2%)
  starting transfers between devices  0.52 us (1%)
    all_to_all x1, blocking collectives, per_device(): parts = lax.all_to_all(own, ('z', 'col'), 0, 0, tiled=True)  21.9 us
    all_to_all x1, blocking collectives, per_device(): blocks = lax.all_to_all(blocks, ('z', 'core', 'col'), 0, 0, tiled=True)  10.2 us
    pallas_call x1, Pallas kernels, project(): pl.pallas_call(functools.partial(project_kernel, chunk), out_shape=(out,...  3.72 us
    ppermute x1, waiting for transfers between devices, per_device(): own = own + lax.ppermute(other, 'core', [(0, 1), (1, 0)])  1.54 us
    pallas_call x1, Pallas kernels, gram_blocks(): pl.pallas_call(functools.partial(gram_kernel, cols, scale), out_shape=plt...  1.45 us
  transfers between devices with their start and end apart: 1, of which 1 were waited for; matrix products, arithmetic and copies ran while one was open for 0% of the time, Pallas kernels for 0%

profile of v2, /device:TPU:0, one launch (start us, length us, event | category | flops | bytes accessed | tf_op | source)
XLA Modules:
  0.0 40.0 jit_solution(8460073451999454366)
XLA Ops:
  0.0 3.7 %shard_map.37 = (f32[8,16,8,128]{3,2,1,0:T(8,128)S(1)}, f32[8,16,8,128]{3,2,1,0:T(8,128)S(1)}) custom-call(bf16[16,64,2048]{2,1,0:T(8,128)(2,1)} %slab_ref.1, bf16[2048,128]{1,0:T(8,128)(2,1)} %one_ref.1, bf16[64,128]{1,0:T(8,128)(2,1)} %two_ref.1), custom_call_target="tpu_custom_call" | custom-call | flops 570425344 | bytes 5767168 | tf_op jit(solution)/shard_map/pallas_call | solution.py:52
  3.7 0.5 %collective-permute-start = (f32[8,16,8,128]{3,2,1,0:T(8,128)S(1)}, f32[8,16,8,128]{3,2,1,0:T(8,128)S(1)}, u32[]{:S(2)}, u32[]{:S(2)}) collective-permute-start(f32[8,16,8,128]{3,2,1,0:T(8,128)S(1)} %get-tuple-element.8), channel_id=1, source_target_pairs={{0,2},{2,0},{1,3},{3,1},{4,6},{6,4},{5,7},{7,5},{8,10},{10,8},{9,1... | collective-permute-start | bytes 1572872 | tf_op jit(solution)/shard_map/ppermute | solution.py:125
  4.2 1.5 %collective-permute-done = f32[8,16,8,128]{3,2,1,0:T(8,128)S(1)} collective-permute-done((f32[8,16,8,128]{3,2,1,0:T(8,128)S(1)}, f32[8,16,8,128]{3,2,1,0:T(8,128)S(1)}, u32[]{:S(2)}, u32[]{:S(2)}) %collective-permute-start) | collective-permute-done | bytes 524320 | tf_op jit(solution)/shard_map/ppermute | solution.py:125
  5.8 0.1 add.3
  5.9 21.9 %all_to_all.10.parts_ref = f32[8,16,8,128]{3,2,1,0:T(8,128)} all-to-all(f32[8,16,8,128]{3,2,1,0:T(8,128)S(1)} %add.3), channel_id=1, replica_groups=mesh['groups'=2,'z'=4,'core'=2,'col'=2] {'z','col'}, dimensions={0} | all-to-all | bytes 1048576 | tf_op jit(solution)/shard_map/all_to_all | solution.py:130
  27.7 1.5 %shard_map.38 = f32[16,8,128]{2,1,0:T(8,128)S(1)} custom-call(f32[8,16,8,128]{3,2,1,0:T(8,128)} %all_to_all.10.parts_ref), custom_call_target="tpu_custom_call" | custom-call | flops 2097152 | bytes 524288 | tf_op jit(solution)/shard_map/pallas_call | solution.py:107
  29.2 10.2 %all_to_all.11 = f32[16,8,128]{2,1,0:T(8,128)S(1)} all-to-all(f32[16,8,128]{2,1,0:T(8,128)S(1)} %shard_map.38), channel_id=1, replica_groups=mesh['groups'=2,'z'=4,'core'=2,'col'=2] {'z','core','col'}, dimensions={0} | all-to-all | bytes 131072 | tf_op jit(solution)/shard_map/all_to_all | solution.py:132
  39.4 0.6 %slice_reduce_fusion = f32[4,16]{1,0:T(4,128)} fusion(f32[16,8,128]{2,1,0:T(8,128)S(1)} %all_to_all.11), kind=kLoop, calls=%fused_computation | loop fusion | flops 960 | bytes 4352 | tf_op jit(solution)/shard_map/reduce_sum | solution.py:133
Async XLA Ops:
  3.7 2.1 %collective-permute-start = (f32[8,16,8,128]{3,2,1,0:T(8,128)S(1)}, f32[8,16,8,128]{3,2,1,0:T(8,128)S(1)}, u32[]{:S(2)}, u32[]{:S(2)}) collective-permute-start(f32[8,16,8,128]{3,2,1,0:T(8,128)S(1)} %get-tuple-element.8), channel_id=1, source_target_pairs={{0,2},{2,0},{1,3},{3,1},{4,6},{6,4},{5,7},{7,5},{8,10},{10,8},{9,1... | collective-permute-start | bytes 1572872 | tf_op jit(solution)/shard_map/ppermute | solution.py:125

commit v3 on v2

v3 whole, which is shorter than its diff:
```python
import functools

import jax
import jax.numpy as jnp
from jax import lax
from jax.experimental import pallas as pl
from jax.experimental.pallas import tpu as pltpu
from jax.sharding import Mesh, PartitionSpec as P

TILE = 8
CORES = 2
CHUNK = 4
RING = 4
FIRST = 1
SECOND = 3


def project_kernel(chunk, starts, slab_ref, one_ref, two_ref, *rest):
    outs, (slab_buf, one_buf, two_buf, turned, sems) = rest[:-5], rest[-5:]
    depth, width, _ = slab_ref.shape
    chunks = depth // chunk
    one_copy = pltpu.make_async_copy(one_ref, one_buf, sems.at[chunks])
    one_copy.start()
    two_copy = pltpu.make_async_copy(two_ref, two_buf, sems.at[chunks + 1])
    two_copy.start()
    copies = []
    for c in range(chunks):
        part = pl.ds(c * chunk, chunk)
        copies.append(pltpu.make_async_copy(slab_ref.at[part], slab_buf.at[part], sems.at[c]))
        copies[-1].start()
    two_copy.wait()
    turned[...] = two_buf[...].astype(jnp.float32).T
    pieces = [turned[pl.ds(pl.multiple_of(s, TILE), TILE), :] for s in starts()]
    two = jnp.concatenate(pieces, axis=0).astype(jnp.bfloat16)
    share = two.shape[0] // len(outs)

    def second(c, first):
        for q in range(chunk):
            core_part = jnp.dot(two, first[q * width : (q + 1) * width], preferred_element_type=jnp.float32)
            for o, out in enumerate(outs):
                piece = core_part[o * share : (o + 1) * share]
                out[:, c * chunk + q] = piece.reshape(share // TILE, TILE, -1)

    one_copy.wait()
    late = None
    for c in range(chunks):
        copies[c].wait()
        rows = slab_buf[pl.ds(c * chunk, chunk)].reshape(chunk * width, -1)
        first = jnp.dot(rows, one_buf[...], preferred_element_type=jnp.float32).astype(jnp.bfloat16)
        if late is not None:
            second(c - 1, late)
        late = first
    second(chunks - 1, late)


def project(slab, factor_one, factor_two, starts, outputs):
    depth, width, length = slab.shape
    r1, r2 = factor_one.shape[1], factor_two.shape[1]
    chunk = CHUNK if depth % CHUNK == 0 else 1
    out = pltpu.VMEM((r2 // TILE // outputs, depth, TILE, r1), jnp.float32)
    return pl.pallas_call(
        functools.partial(project_kernel, chunk, starts),
        out_shape=(out,) * outputs,
        in_specs=[pl.BlockSpec(memory_space=pltpu.HBM)] * 3,
        out_specs=[pl.BlockSpec(memory_space=pltpu.VMEM)] * outputs,
        scratch_shapes=[
            pltpu.VMEM(slab.shape, slab.dtype),
            pltpu.VMEM(factor_one.shape, factor_one.dtype),
            pltpu.VMEM(factor_two.shape, factor_two.dtype),
            pltpu.VMEM((r2, width), jnp.float32),
            pltpu.SemaphoreType.DMA((depth // chunk + 2,)),
        ],
        compiler_params=pltpu.CompilerParams(vmem_limit_bytes=32 * 2**20),
        cost_estimate=pl.CostEstimate(
            flops=2 * depth * width * r1 * (length + r2),
            bytes_accessed=2 * (slab.size + factor_one.size) + 4 * depth * r2 * r1,
            transcendentals=0,
        ),
    )(*(pltpu.with_memory_space_constraint(a, pltpu.HBM) for a in (slab, factor_one, factor_two)))


def gram_kernel(scale, own_ref, far_ref, out_ref, flag_ref, total, gram):
    groups, depth, tile, _ = own_ref.shape
    z, core, x = (lax.axis_index(name) for name in ("z", "core", "col"))
    chips, share, _ = out_ref.shape
    size = depth * tile
    value = jnp.zeros((2 * depth, depth), jnp.float32)
    for g in range(groups):
        total[g, pl.ds(pl.multiple_of(x * size, size), size), :] = own_ref[g].reshape(size, -1)
        total[g, pl.ds(pl.multiple_of((1 - x) * size, size), size), :] = far_ref[g].reshape(size, -1)
    for g in range(groups):
        for s in range(tile):
            rows = total[g, pl.ds(s, 2 * depth, stride=tile), :]
            own = total[g, pl.ds(x * size + s, depth, stride=tile), :]
            value = value + lax.dot_general(
                rows,
                own,
                (((1,), (1,)), ((), ())),
                precision=lax.Precision.HIGHEST,
                preferred_element_type=jnp.float32,
            )
    gram[:, 0:depth] = value * scale
    for slot, hops in enumerate(((), (SECOND,), (FIRST,), (FIRST, SECOND))):
        to_z = z
        for hop in hops:
            to_z = jnp.bitwise_xor(to_z, hop)
        out_ref[slot] = gram[pl.ds(pl.multiple_of(to_z * share, TILE), share), :]
    flag_ref[...] = jnp.full(flag_ref.shape, core, jnp.int32)


def gram_blocks(own, far, chips, scale):
    groups, depth, tile, r1 = own.shape
    full = 2 * depth
    return pl.pallas_call(
        functools.partial(gram_kernel, scale),
        out_shape=(pltpu.VMEM((chips, full // chips, 128), jnp.float32), pltpu.VMEM((TILE, 128), jnp.int32)),
        in_specs=[pl.BlockSpec(memory_space=pltpu.VMEM)] * 2,
        out_specs=[pl.BlockSpec(memory_space=pltpu.VMEM)] * 2,
        scratch_shapes=[
            pltpu.VMEM((groups, full * tile, r1), jnp.float32),
            pltpu.VMEM((full, 128), jnp.float32),
        ],
        cost_estimate=pl.CostEstimate(
            flops=2 * groups * full * depth * tile * r1, bytes_accessed=8 * own.size, transcendentals=0
        ),
    )(*(pltpu.with_memory_space_constraint(a, pltpu.VMEM) for a in (own, far)))


def send(value, zs, step, cross=0):
    pairs = [(z * CORES + core, step(z) * CORES + (core ^ cross)) for z in range(zs) for core in range(CORES)]
    return lax.ppermute(value, ("z", "core"), pairs)


def swap(value, axis):
    return lax.ppermute(value, axis, [(0, 1), (1, 0)])


RING_STEPS = (2, 1, -1, 0)


def ring_starts(zs, half, width):
    z, core = lax.axis_index("z"), lax.axis_index("core")
    starts = []
    for side in (1 - core, core):
        for step in RING_STEPS:
            to_z = lax.rem(z + step + zs, zs)
            starts += [side * half + to_z * width + s for s in range(0, width, TILE)]
    return starts


def ring_plan(zs, scale, slab, factor_one, factor_two):
    half = factor_two.shape[1] // CORES
    starts = functools.partial(ring_starts, zs, half, half // zs)
    parts = project(slab, factor_one, factor_two, starts, 2 * zs)
    others, owns = parts[:zs], parts[zs:]
    swapped = [swap(other, "core") for other in others]
    chip = [own + got for own, got in zip(owns, swapped)]
    got = [send(value, zs, lambda z, step=step: (z + step) % zs) for value, step in zip(chip[:-1], RING_STEPS)]
    own = chip[-1] + got[0] + got[1] + got[2]
    blocks, flag = gram_blocks(own, swap(own, "col"), zs, scale)
    blocks = blocks + swap(blocks, "core")
    pair = blocks[:2] + send(blocks[2:], zs, lambda z: z ^ FIRST, cross=1)
    last = pair[0] + send(pair[1], zs, lambda z: z ^ SECOND, cross=1)
    depth, rows = slab.shape[0], last.shape[0] // CORES
    return jnp.where(flag[:rows, :depth] == 1, last[rows:, :depth], last[:rows, :depth]).T


def general_plan(scale, slab, factor_one, factor_two):
    depth = slab.shape[0]
    r1, r2 = factor_one.shape[1], factor_two.shape[1]
    half = r2 // CORES

    def starts():
        core = lax.axis_index("core")
        return [side * half + s for side in (1 - core, core) for s in range(0, half, TILE)]

    other, own = project(slab, factor_one, factor_two, starts, 2)
    own = own + swap(other, "core")
    own = own.transpose(0, 2, 1, 3).reshape(half, depth, r1)
    share = lax.psum_scatter(own, "z", scatter_dimension=0, tiled=True)
    whole = lax.all_gather(share, "col", axis=1, tiled=True)
    gram = jnp.einsum("skr,slr->kl", share, whole, precision=lax.Precision.HIGHEST)
    return lax.psum_scatter(gram, ("z", "core"), scatter_dimension=1, tiled=True) * scale


def per_device(zs, cols, slab, factor_one, factor_two):
    r1, r2 = factor_one.shape[1], factor_two.shape[1]
    scale = 1.0 / (r1 * r2)
    depth = slab.shape[0]
    if zs == RING and cols == 2 and r2 % (CORES * zs * TILE) == 0 and cols * depth == zs * TILE:
        return ring_plan(zs, scale, slab, factor_one, factor_two)
    return general_plan(scale, slab, factor_one, factor_two)


def solution(mesh):
    groups, rows, cols = mesh.devices.shape
    zs = rows // CORES
    fine = Mesh(mesh.devices.reshape(groups, zs, CORES, cols), ("groups", "z", "core", "col"))
    row = ("z", "core")
    return jax.shard_map(
        functools.partial(per_device, zs, cols),
        mesh=fine,
        in_specs=(P(("groups", "col"), row, None), P(), P(row, None)),
        out_specs=P(("groups", "col"), row),
        check_vma=False,
    )
```

time: 40.2 us -> 35.9 us (0.89)
  blocking collectives: 32.1 us -> 0 us
  starting transfers between devices: 0.52 us -> 16 us
  waiting for transfers between devices: 1.54 us -> 15.1 us
  Pallas kernels: 5.17 us -> 3.83 us
    all_to_all x2 -> x0, blocking collectives: 32.1 us -> none  [the longest x1 21.9 us: per_device(): parts = lax.all_to_all(own, ('z', 'col'), 0, 0, tiled=True)]
    ppermute x1 -> x11, starting transfers between devices: 0.52 us -> 16 us  [the longest x5 13.3 us: send(): return lax.ppermute(value, ('z', 'core'), pairs)]
    ppermute x1 -> x11, waiting for transfers between devices: 1.54 us -> 15.1 us  [the longest x5 10.1 us: send(): return lax.ppermute(value, ('z', 'core'), pairs)]
    pallas_call x2, Pallas kernels: 5.17 us -> 3.83 us  [the longest x1 3.35 us: project(): pl.pallas_call(functools.partial(project_kernel, chunk, starts), out_shap...]
    reduce_sum x1 -> x0, other arithmetic: 0.6 us -> none  [per_device(): return blocks[:, :full // rows, :depth].sum(0).T]
    transpose x0 -> x1, other arithmetic: none -> 0.58 us  [ring_plan(): jnp.where(flag[:rows, :depth] == 1, last[rows:, :depth], last[:rows, :dep...]
  transfers between devices with their start and end apart: 1 -> 11, of which waited for: 1 -> 7; matrix products, arithmetic and copies ran while one was open for 0% -> 0% of each run, Pallas kernels for 0% -> 0%
where the time goes in v3:
time: 35.9 us; the launch traced here: 35.7 us
  starting transfers between devices  16 us (45%)
  waiting for transfers between devices  15.1 us (42%)
  Pallas kernels  3.83 us (11%)
  other arithmetic  0.7 us (2%)
    ppermute x5, starting transfers between devices, send(): return lax.ppermute(value, ('z', 'core'), pairs)  13.3 us
    ppermute x5, waiting for transfers between devices, send(): return lax.ppermute(value, ('z', 'core'), pairs)  10.1 us
    ppermute x6, waiting for transfers between devices, swap(): return lax.ppermute(value, axis, [(0, 1), (1, 0)])  5 us
    pallas_call x1, Pallas kernels, project(): pl.pallas_call(functools.partial(project_kernel, chunk, starts), out_shap...  3.35 us
    ppermute x6, starting transfers between devices, swap(): return lax.ppermute(value, axis, [(0, 1), (1, 0)])  2.78 us
  transfers between devices with their start and end apart: 11, of which 7 were waited for; matrix products, arithmetic and copies ran while one was open for 0% of the time, Pallas kernels for 0%

profile of v3, /device:TPU:0, one launch (start us, length us, event | category | flops | bytes accessed | tf_op | source)
XLA Modules:
  0.0 35.7 jit_solution(9879174151893930346)
XLA Ops:
  0.0 3.3 %shard_map.37 = (f32[2,16,8,128]{3,2,1,0:T(8,128)S(1)}, f32[2,16,8,128]{3,2,1,0:T(8,128)S(1)}, f32[2,16,8,128]{3,2,1,0:T(8,128)S(1)}, f32[2,16,8,128]{3,2,1,0:T(...) custom-call(bf16[16,64,2048]{2,1,0:T(8,128)(2,1)} %slab_ref.1, ...), custom_call_target="tpu_custom_call" | custom-call | flops 570425344 | bytes 5767168 | tf_op jit(solution)/shard_map/pallas_call | solution.py:61
  3.4 0.5 %collective-permute-start.1 = (f32[2,16,8,128]{3,2,1,0:T(8,128)S(1)}, f32[2,16,8,128]{3,2,1,0:T(8,128)S(1)}, u32[]{:S(2)}, u32[]{:S(2)}) collective-permute-start(f32[2,16,8,128]{3,2,1,0:T(8,128)S(1)} %get-tuple-element.18), channel_id=1, source_target_pairs={{0,2},{2,0},{1,3},{3,1},{4,6},{6,4},{5,7},{7,5},{8,10},{10,8},{9,1... | collective-permute-start | bytes 393224 | tf_op jit(solution)/shard_map/ppermute | solution.py:135
  3.9 0.1 collective-permute-start.3
  4.0 0.4 %collective-permute-start.5 = (f32[2,16,8,128]{3,2,1,0:T(8,128)S(1)}, f32[2,16,8,128]{3,2,1,0:T(8,128)S(1)}, u32[]{:S(2)}, u32[]{:S(2)}) collective-permute-start(f32[2,16,8,128]{3,2,1,0:T(8,128)S(1)} %get-tuple-element.22), channel_id=1, source_target_pairs={{0,2},{2,0},{1,3},{3,1},{4,6},{6,4},{5,7},{7,5},{8,10},{10,8},{9,1... | collective-permute-start | bytes 393224 | tf_op jit(solution)/shard_map/ppermute | solution.py:135
  4.4 0.1 collective-permute-start
  4.5 0.4 %collective-permute-done.1 = f32[2,16,8,128]{3,2,1,0:T(8,128)S(1)} collective-permute-done((f32[2,16,8,128]{3,2,1,0:T(8,128)S(1)}, f32[2,16,8,128]{3,2,1,0:T(8,128)S(1)}, u32[]{:S(2)}, u32[]{:S(2)}) %collective-permute-start.1) | collective-permute-done | bytes 131104 | tf_op jit(solution)/shard_map/ppermute | solution.py:135
  4.9 4.0 %collective-permute-start.2 = (f32[2,16,8,128]{3,2,1,0:T(8,128)S(1)}, f32[2,16,8,128]{3,2,1,0:T(8,128)S(1)}, u32[]{:S(2)}, u32[]{:S(2)}) collective-permute-start(f32[2,16,8,128]{3,2,1,0:T(8,128)S(1)} %add.31), channel_id=1, source_target_pairs={{0,8},{2,10},{4,12},{6,14},{8,0},{10,2},{12,4},{14,6},{1,9},{3,11}... | collective-permute-start | bytes 393224 | tf_op jit(solution)/shard_map/ppermute | solution.py:131
  8.9 0.0 collective-permute-done.3
  8.9 1.6 %collective-permute-start.4 = (f32[2,16,8,128]{3,2,1,0:T(8,128)S(1)}, f32[2,16,8,128]{3,2,1,0:T(8,128)S(1)}, u32[]{:S(2)}, u32[]{:S(2)}) collective-permute-start(f32[2,16,8,128]{3,2,1,0:T(8,128)S(1)} %add.33), channel_id=1, source_target_pairs={{0,4},{2,6},{4,8},{6,10},{8,12},{10,14},{12,0},{14,2},{1,5},{3,7},... | collective-permute-start | bytes 393224 | tf_op jit(solution)/shard_map/ppermute | solution.py:131
  10.6 0.0 collective-permute-done.5
  10.6 2.3 %collective-permute-start.6 = (f32[2,16,8,128]{3,2,1,0:T(8,128)S(1)}, f32[2,16,8,128]{3,2,1,0:T(8,128)S(1)}, u32[]{:S(2)}, u32[]{:S(2)}) collective-permute-start(f32[2,16,8,128]{3,2,1,0:T(8,128)S(1)} %add.35), channel_id=1, source_target_pairs={{0,12},{2,14},{4,0},{6,2},{8,4},{10,6},{12,8},{14,10},{1,13},{3,15... | collective-permute-start | bytes 393224 | tf_op jit(solution)/shard_map/ppermute | solution.py:131
  12.9 0.0 collective-permute-done
  12.9 6.0 %collective-permute-done.2 = f32[2,16,8,128]{3,2,1,0:T(8,128)S(1)} collective-permute-done((f32[2,16,8,128]{3,2,1,0:T(8,128)S(1)}, f32[2,16,8,128]{3,2,1,0:T(8,128)S(1)}, u32[]{:S(2)}, u32[]{:S(2)}) %collective-permute-start.2) | collective-permute-done | bytes 131104 | tf_op jit(solution)/shard_map/ppermute | solution.py:131
  18.8 0.0 collective-permute-done.4
  18.8 1.2 %collective-permute-done.6 = f32[2,16,8,128]{3,2,1,0:T(8,128)S(1)} collective-permute-done((f32[2,16,8,128]{3,2,1,0:T(8,128)S(1)}, f32[2,16,8,128]{3,2,1,0:T(8,128)S(1)}, u32[]{:S(2)}, u32[]{:S(2)}) %collective-permute-start.6) | collective-permute-done | bytes 131104 | tf_op jit(solution)/shard_map/ppermute | solution.py:131
  20.1 1.6 %collective-permute-start.7 = (f32[2,16,8,128]{3,2,1,0:T(8,128)S(1)}, f32[2,16,8,128]{3,2,1,0:T(8,128)S(1)}, u32[]{:S(2)}, u32[]{:S(2)}) collective-permute-start(f32[2,16,8,128]{3,2,1,0:T(8,128)S(1)} %add_add_fusion.own_ref), channel_id=1, source_target_pairs={{0,1},{1,0},{2,3},{3,2},{4,5},{5,4},{6,7},{7,6},{8,9},{9,8},{10,11... | collective-permute-start | bytes 393224 | tf_op jit(solution)/shard_map/ppermute | solution.py:135
  21.7 3.4 %collective-permute-done.7.far_ref = f32[2,16,8,128]{3,2,1,0:T(8,128)S(1)} collective-permute-done((f32[2,16,8,128]{3,2,1,0:T(8,128)S(1)}, f32[2,16,8,128]{3,2,1,0:T(8,128)S(1)}, u32[]{:S(2)}, u32[]{:S(2)}) %collective-permute-start.7) | collective-permute-done | bytes 131104 | tf_op jit(solution)/shard_map/ppermute | solution.py:135
  25.2 0.5 %shard_map.38 = (f32[4,8,128]{2,1,0:T(8,128)S(1)}, s32[8,128]{1,0:T(8,128)S(1)}) custom-call(f32[2,16,8,128]{3,2,1,0:T(8,128)S(1)} %add_add_fusion.own_ref, f32[2,16,8,128]{3,2,1,0:T(8,128)S(1)} %collective-permute-done.7.far_ref), custom_call_target="tpu_custom_call" | custom-call | flops 2097152 | bytes 262144 | tf_op jit(solution)/shard_map/pallas_call | solution.py:114
  25.6 0.1 collective-permute-start.8
  25.7 1.2 %collective-permute-done.8 = f32[4,8,128]{2,1,0:T(8,128)S(1)} collective-permute-done((f32[4,8,128]{2,1,0:T(8,128)S(1)}, f32[4,8,128]{2,1,0:T(8,128)S(1)}, u32[]{:S(2)}, u32[]{:S(2)}) %collective-permute-start.8) | collective-permute-done | bytes 16416 | tf_op jit(solution)/shard_map/ppermute | solution.py:135
  26.9 2.0 %collective-permute-start.9 = (f32[2,8,128]{2,1,0:T(8,128)S(1)}, f32[2,8,128]{2,1,0:T(8,128)S(1)}, u32[]{:S(2)}, u32[]{:S(2)}) collective-permute-start(f32[2,8,128]{2,1,0:T(8,128)S(1)} %slice.29), channel_id=1, source_target_pairs={{0,6},{2,4},{4,2},{6,0},{8,14},{10,12},{12,10},{14,8},{1,7},{3,5},... | collective-permute-start | bytes 24584 | tf_op jit(solution)/shard_map/ppermute | solution.py:131
  28.9 1.4 %collective-permute-done.9 = f32[2,8,128]{2,1,0:T(8,128)S(1)} collective-permute-done((f32[2,8,128]{2,1,0:T(8,128)S(1)}, f32[2,8,128]{2,1,0:T(8,128)S(1)}, u32[]{:S(2)}, u32[]{:S(2)}) %collective-permute-start.9) | collective-permute-done | bytes 8224 | tf_op jit(solution)/shard_map/ppermute | solution.py:131
  30.3 3.3 %collective-permute-start.10 = (f32[8,128]{1,0:T(8,128)S(1)}, f32[8,128]{1,0:T(8,128)S(1)}, u32[]{:S(2)}, u32[]{:S(2)}) collective-permute-start(f32[8,128]{1,0:T(8,128)S(1)} %slice_bitcast_fusion), channel_id=1, source_target_pairs={{0,14},{2,12},{4,10},{6,8},{8,6},{10,4},{12,2},{14,0},{1,15},{3,13... | collective-permute-start | bytes 12296 | tf_op jit(solution)/shard_map/ppermute | solution.py:131
  33.6 1.5 %collective-permute-done.10 = f32[8,128]{1,0:T(8,128)S(1)} collective-permute-done((f32[8,128]{1,0:T(8,128)S(1)}, f32[8,128]{1,0:T(8,128)S(1)}, u32[]{:S(2)}, u32[]{:S(2)}) %collective-permute-start.10) | collective-permute-done | bytes 4128 | tf_op jit(solution)/shard_map/ppermute | solution.py:131
  35.1 0.6 %select_bitcast_fusion = f32[16,4]{0,1:T(4,128)} fusion(f32[8,128]{1,0:T(8,128)S(1)} %fusion, s32[8,128]{1,0:T(8,128)S(1)} %get-tuple-element.23), kind=kLoop, calls=%fused_computation.5 | loop fusion | flops 128 | bytes 1024 | tf_op jit(solution)/shard_map/transpose | solution.py:165
  (9 shorter events, 0.1 us)
Async XLA Ops:
  3.4 1.5 %collective-permute-start.1 = (f32[2,16,8,128]{3,2,1,0:T(8,128)S(1)}, f32[2,16,8,128]{3,2,1,0:T(8,128)S(1)}, u32[]{:S(2)}, u32[]{:S(2)}) collective-permute-start(f32[2,16,8,128]{3,2,1,0:T(8,128)S(1)} %get-tuple-element.18), channel_id=1, source_target_pairs={{0,2},{2,0},{1,3},{3,1},{4,6},{6,4},{5,7},{7,5},{8,10},{10,8},{9,1... | collective-permute-start | bytes 393224 | tf_op jit(solution)/shard_map/ppermute | solution.py:135
  3.9 5.0 %collective-permute-start.3 = (f32[2,16,8,128]{3,2,1,0:T(8,128)S(1)}, f32[2,16,8,128]{3,2,1,0:T(8,128)S(1)}, u32[]{:S(2)}, u32[]{:S(2)}) collective-permute-start(f32[2,16,8,128]{3,2,1,0:T(8,128)S(1)} %get-tuple-element.20), channel_id=1, source_target_pairs={{0,2},{2,0},{1,3},{3,1},{4,6},{6,4},{5,7},{7,5},{8,10},{10,8},{9,1... | collective-permute-start | bytes 393224 | tf_op jit(solution)/shard_map/ppermute | solution.py:135
  4.0 6.6 %collective-permute-start.5 = (f32[2,16,8,128]{3,2,1,0:T(8,128)S(1)}, f32[2,16,8,128]{3,2,1,0:T(8,128)S(1)}, u32[]{:S(2)}, u32[]{:S(2)}) collective-permute-start(f32[2,16,8,128]{3,2,1,0:T(8,128)S(1)} %get-tuple-element.22), channel_id=1, source_target_pairs={{0,2},{2,0},{1,3},{3,1},{4,6},{6,4},{5,7},{7,5},{8,10},{10,8},{9,1... | collective-permute-start | bytes 393224 | tf_op jit(solution)/shard_map/ppermute | solution.py:135
  4.4 8.5 %collective-permute-start = (f32[2,16,8,128]{3,2,1,0:T(8,128)S(1)}, f32[2,16,8,128]{3,2,1,0:T(8,128)S(1)}, u32[]{:S(2)}, u32[]{:S(2)}) collective-permute-start(f32[2,16,8,128]{3,2,1,0:T(8,128)S(1)} %get-tuple-element.16), channel_id=1, source_target_pairs={{0,2},{2,0},{1,3},{3,1},{4,6},{6,4},{5,7},{7,5},{8,10},{10,8},{9,1... | collective-permute-start | bytes 393224 | tf_op jit(solution)/shard_map/ppermute | solution.py:135
  4.9 14.0 %collective-permute-start.2 = (f32[2,16,8,128]{3,2,1,0:T(8,128)S(1)}, f32[2,16,8,128]{3,2,1,0:T(8,128)S(1)}, u32[]{:S(2)}, u32[]{:S(2)}) collective-permute-start(f32[2,16,8,128]{3,2,1,0:T(8,128)S(1)} %add.31), channel_id=1, source_target_pairs={{0,8},{2,10},{4,12},{6,14},{8,0},{10,2},{12,4},{14,6},{1,9},{3,11}... | collective-permute-start | bytes 393224 | tf_op jit(solution)/shard_map/ppermute | solution.py:131
  8.9 9.9 %collective-permute-start.4 = (f32[2,16,8,128]{3,2,1,0:T(8,128)S(1)}, f32[2,16,8,128]{3,2,1,0:T(8,128)S(1)}, u32[]{:S(2)}, u32[]{:S(2)}) collective-permute-start(f32[2,16,8,128]{3,2,1,0:T(8,128)S(1)} %add.33), channel_id=1, source_target_pairs={{0,4},{2,6},{4,8},{6,10},{8,12},{10,14},{12,0},{14,2},{1,5},{3,7},... | collective-permute-start | bytes 393224 | tf_op jit(solution)/shard_map/ppermute | solution.py:131
  10.6 9.5 %collective-permute-start.6 = (f32[2,16,8,128]{3,2,1,0:T(8,128)S(1)}, f32[2,16,8,128]{3,2,1,0:T(8,128)S(1)}, u32[]{:S(2)}, u32[]{:S(2)}) collective-permute-start(f32[2,16,8,128]{3,2,1,0:T(8,128)S(1)} %add.35), channel_id=1, source_target_pairs={{0,12},{2,14},{4,0},{6,2},{8,4},{10,6},{12,8},{14,10},{1,13},{3,15... | collective-permute-start | bytes 393224 | tf_op jit(solution)/shard_map/ppermute | solution.py:131
  20.1 5.0 %collective-permute-start.7 = (f32[2,16,8,128]{3,2,1,0:T(8,128)S(1)}, f32[2,16,8,128]{3,2,1,0:T(8,128)S(1)}, u32[]{:S(2)}, u32[]{:S(2)}) collective-permute-start(f32[2,16,8,128]{3,2,1,0:T(8,128)S(1)} %add_add_fusion.own_ref), channel_id=1, source_target_pairs={{0,1},{1,0},{2,3},{3,2},{4,5},{5,4},{6,7},{7,6},{8,9},{9,8},{10,11... | collective-permute-start | bytes 393224 | tf_op jit(solution)/shard_map/ppermute | solution.py:135
  25.6 1.2 %collective-permute-start.8 = (f32[4,8,128]{2,1,0:T(8,128)S(1)}, f32[4,8,128]{2,1,0:T(8,128)S(1)}, u32[]{:S(2)}, u32[]{:S(2)}) collective-permute-start(f32[4,8,128]{2,1,0:T(8,128)S(1)} %get-tuple-element.24), channel_id=1, source_target_pairs={{0,2},{2,0},{1,3},{3,1},{4,6},{6,4},{5,7},{7,5},{8,10},{10,8},{9,1... | collective-permute-start | bytes 49160 | tf_op jit(solution)/shard_map/ppermute | solution.py:135
  26.9 3.4 %collective-permute-start.9 = (f32[2,8,128]{2,1,0:T(8,128)S(1)}, f32[2,8,128]{2,1,0:T(8,128)S(1)}, u32[]{:S(2)}, u32[]{:S(2)}) collective-permute-start(f32[2,8,128]{2,1,0:T(8,128)S(1)} %slice.29), channel_id=1, source_target_pairs={{0,6},{2,4},{4,2},{6,0},{8,14},{10,12},{12,10},{14,8},{1,7},{3,5},... | collective-permute-start | bytes 24584 | tf_op jit(solution)/shard_map/ppermute | solution.py:131
  30.3 4.8 %collective-permute-start.10 = (f32[8,128]{1,0:T(8,128)S(1)}, f32[8,128]{1,0:T(8,128)S(1)}, u32[]{:S(2)}, u32[]{:S(2)}) collective-permute-start(f32[8,128]{1,0:T(8,128)S(1)} %slice_bitcast_fusion), channel_id=1, source_target_pairs={{0,14},{2,12},{4,10},{6,8},{8,6},{10,4},{12,2},{14,0},{1,15},{3,13... | collective-permute-start | bytes 12296 | tf_op jit(solution)/shard_map/ppermute | solution.py:131

commit v4 on v3

--- a/solution.py
+++ b/solution.py
@@ -12,7 +12,7 @@
 CHUNK = 4
 RING = 4
 FIRST = 1
-SECOND = 3
+SECOND = 2
 
 
 def project_kernel(chunk, starts, slab_ref, one_ref, two_ref, *rest):
@@ -126,8 +126,10 @@
     )(*(pltpu.with_memory_space_constraint(a, pltpu.VMEM) for a in (own, far)))
 
 
-def send(value, zs, step, cross=0):
-    pairs = [(z * CORES + core, step(z) * CORES + (core ^ cross)) for z in range(zs) for core in range(CORES)]
+def hop(value, zs, masks, cross=0):
+    pairs = [
+        (z * CORES + core, (z ^ masks[core]) * CORES + (core ^ cross)) for z in range(zs) for core in range(CORES)
+    ]
     return lax.ppermute(value, ("z", "core"), pairs)
 
 
@@ -135,32 +137,32 @@
     return lax.ppermute(value, axis, [(0, 1), (1, 0)])
 
 
-RING_STEPS = (2, 1, -1, 0)
-
-
-def ring_starts(zs, half, width):
+FIRST_HOP = (FIRST, SECOND)
+SECOND_HOP = (SECOND, FIRST)
+
+
+def ring_starts(half, width):
     z, core = lax.axis_index("z"), lax.axis_index("core")
     starts = []
-    for side in (1 - core, core):
-        for step in RING_STEPS:
-            to_z = lax.rem(z + step + zs, zs)
-            starts += [side * half + to_z * width + s for s in range(0, width, TILE)]
+    for to_core in (1 - core, core):
+        one, two = (to_core * (hops[1] - hops[0]) + hops[0] for hops in (FIRST_HOP, SECOND_HOP))
+        for mask in (FIRST ^ SECOND, one, two, 0):
+            starts += [to_core * half + jnp.bitwise_xor(z, mask) * width + s for s in range(0, width, TILE)]
     return starts
 
 
 def ring_plan(zs, scale, slab, factor_one, factor_two):
     half = factor_two.shape[1] // CORES
-    starts = functools.partial(ring_starts, zs, half, half // zs)
+    starts = functools.partial(ring_starts, half, half // zs)
     parts = project(slab, factor_one, factor_two, starts, 2 * zs)
-    others, owns = parts[:zs], parts[zs:]
-    swapped = [swap(other, "core") for other in others]
-    chip = [own + got for own, got in zip(owns, swapped)]
-    got = [send(value, zs, lambda z, step=step: (z + step) % zs) for value, step in zip(chip[:-1], RING_STEPS)]
-    own = chip[-1] + got[0] + got[1] + got[2]
+    passed, given, across, own = (o + swap(t, "core") for t, o in zip(parts[:zs], parts[zs:]))
+    arrived = hop(passed, zs, FIRST_HOP)
+    beside = hop(given, zs, FIRST_HOP)
+    own = own + beside + hop(across + arrived, zs, SECOND_HOP)
     blocks, flag = gram_blocks(own, swap(own, "col"), zs, scale)
     blocks = blocks + swap(blocks, "core")
-    pair = blocks[:2] + send(blocks[2:], zs, lambda z: z ^ FIRST, cross=1)
-    last = pair[0] + send(pair[1], zs, lambda z: z ^ SECOND, cross=1)
+    pair = blocks[:2] + hop(blocks[2:], zs, (FIRST, FIRST), cross=1)
+    last = pair[0] + hop(pair[1], zs, (SECOND, SECOND), cross=1)
     depth, rows = slab.shape[0], last.shape[0] // CORES
     return jnp.where(flag[:rows, :depth] == 1, last[rows:, :depth], last[:rows, :depth]).T
 

time: 35.9 us -> 33.6 us (0.936)
  waiting for transfers between devices: 15.1 us -> 12.1 us
  starting transfers between devices: 16 us -> 16.8 us
    ppermute x5, waiting for transfers between devices: 10.1 us -> 7.45 us  [hop(): return lax.ppermute(value, ('z', 'core'), pairs)]
    ppermute x6, starting transfers between devices: 2.78 us -> 4.61 us  [swap(): return lax.ppermute(value, axis, [(0, 1), (1, 0)])]
    ppermute x5, starting transfers between devices: 13.3 us -> 12.2 us  [hop(): return lax.ppermute(value, ('z', 'core'), pairs)]
    ppermute x6, waiting for transfers between devices: 5 us -> 4.6 us  [swap(): return lax.ppermute(value, axis, [(0, 1), (1, 0)])]
  transfers between devices with their start and end apart: 11 -> 11, of which waited for: 7 -> 8; matrix products, arithmetic and copies ran while one was open for 0% -> 0% of each run, Pallas kernels for 0% -> 0%
where the time goes in v4:
time: 33.6 us; the launch traced here: 33.4 us
  starting transfers between devices  16.8 us (50%)
  waiting for transfers between devices  12.1 us (36%)
  Pallas kernels  3.83 us (11%)
  other arithmetic  0.69 us (2%)
    ppermute x5, starting transfers between devices, hop(): return lax.ppermute(value, ('z', 'core'), pairs)  12.2 us
    ppermute x5, waiting for transfers between devices, hop(): return lax.ppermute(value, ('z', 'core'), pairs)  7.45 us
    ppermute x6, starting transfers between devices, swap(): return lax.ppermute(value, axis, [(0, 1), (1, 0)])  4.61 us
    ppermute x6, waiting for transfers between devices, swap(): return lax.ppermute(value, axis, [(0, 1), (1, 0)])  4.6 us
    pallas_call x1, Pallas kernels, project(): pl.pallas_call(functools.partial(project_kernel, chunk, starts), out_shap...  3.35 us
  transfers between devices with their start and end apart: 11, of which 8 were waited for; matrix products, arithmetic and copies ran while one was open for 0% of the time, Pallas kernels for 0%

profile of v4, /device:TPU:0, one launch (start us, length us, event | category | flops | bytes accessed | tf_op | source)
XLA Modules:
  0.0 33.4 jit_solution(16450793448182629351)
XLA Ops:
  0.0 3.3 %shard_map.37 = (f32[2,16,8,128]{3,2,1,0:T(8,128)S(1)}, f32[2,16,8,128]{3,2,1,0:T(8,128)S(1)}, f32[2,16,8,128]{3,2,1,0:T(8,128)S(1)}, f32[2,16,8,128]{3,2,1,0:T(...) custom-call(bf16[16,64,2048]{2,1,0:T(8,128)(2,1)} %slab_ref.1, ...), custom_call_target="tpu_custom_call" | custom-call | flops 570425344 | bytes 5767168 | tf_op jit(solution)/shard_map/pallas_call | solution.py:61
  3.4 0.5 %collective-permute-start.4 = (f32[2,16,8,128]{3,2,1,0:T(8,128)S(1)}, f32[2,16,8,128]{3,2,1,0:T(8,128)S(1)}, u32[]{:S(2)}, u32[]{:S(2)}) collective-permute-start(f32[2,16,8,128]{3,2,1,0:T(8,128)S(1)} %get-tuple-element.22), channel_id=1, source_target_pairs={{0,2},{2,0},{1,3},{3,1},{4,6},{6,4},{5,7},{7,5},{8,10},{10,8},{9,1... | collective-permute-start | bytes 393224 | tf_op jit(solution)/shard_map/ppermute | solution.py:137
  3.9 0.1 collective-permute-start.1
  4.0 0.4 %collective-permute-start.3 = (f32[2,16,8,128]{3,2,1,0:T(8,128)S(1)}, f32[2,16,8,128]{3,2,1,0:T(8,128)S(1)}, u32[]{:S(2)}, u32[]{:S(2)}) collective-permute-start(f32[2,16,8,128]{3,2,1,0:T(8,128)S(1)} %get-tuple-element.20), channel_id=1, source_target_pairs={{0,2},{2,0},{1,3},{3,1},{4,6},{6,4},{5,7},{7,5},{8,10},{10,8},{9,1... | collective-permute-start | bytes 393224 | tf_op jit(solution)/shard_map/ppermute | solution.py:137
  4.4 0.5 %collective-permute-done.4 = f32[2,16,8,128]{3,2,1,0:T(8,128)S(1)} collective-permute-done((f32[2,16,8,128]{3,2,1,0:T(8,128)S(1)}, f32[2,16,8,128]{3,2,1,0:T(8,128)S(1)}, u32[]{:S(2)}, u32[]{:S(2)}) %collective-permute-start.4) | collective-permute-done | bytes 131104 | tf_op jit(solution)/shard_map/ppermute | solution.py:137
  4.9 3.0 %collective-permute-start.5 = (f32[2,16,8,128]{3,2,1,0:T(8,128)S(1)}, f32[2,16,8,128]{3,2,1,0:T(8,128)S(1)}, u32[]{:S(2)}, u32[]{:S(2)}) collective-permute-start(f32[2,16,8,128]{3,2,1,0:T(8,128)S(1)} %add.34), channel_id=1, source_target_pairs={{0,4},{2,10},{4,0},{6,14},{8,12},{10,2},{12,8},{14,6},{1,5},{3,11}... | collective-permute-start | bytes 393224 | tf_op jit(solution)/shard_map/ppermute | solution.py:133
  7.9 0.9 %collective-permute-start = (f32[2,16,8,128]{3,2,1,0:T(8,128)S(1)}, f32[2,16,8,128]{3,2,1,0:T(8,128)S(1)}, u32[]{:S(2)}, u32[]{:S(2)}) collective-permute-start(f32[2,16,8,128]{3,2,1,0:T(8,128)S(1)} %get-tuple-element.16), channel_id=1, source_target_pairs={{0,2},{2,0},{1,3},{3,1},{4,6},{6,4},{5,7},{7,5},{8,10},{10,8},{9,1... | collective-permute-start | bytes 393224 | tf_op jit(solution)/shard_map/ppermute | solution.py:137
  8.8 0.0 collective-permute-done.1
  8.8 1.6 %collective-permute-start.2 = (f32[2,16,8,128]{3,2,1,0:T(8,128)S(1)}, f32[2,16,8,128]{3,2,1,0:T(8,128)S(1)}, u32[]{:S(2)}, u32[]{:S(2)}) collective-permute-start(f32[2,16,8,128]{3,2,1,0:T(8,128)S(1)} %add.31), channel_id=1, source_target_pairs={{0,4},{2,10},{4,0},{6,14},{8,12},{10,2},{12,8},{14,6},{1,5},{3,11}... | collective-permute-start | bytes 393224 | tf_op jit(solution)/shard_map/ppermute | solution.py:133
  10.4 0.0 collective-permute-done.3
  10.4 1.5 %collective-permute-done.5 = f32[2,16,8,128]{3,2,1,0:T(8,128)S(1)} collective-permute-done((f32[2,16,8,128]{3,2,1,0:T(8,128)S(1)}, f32[2,16,8,128]{3,2,1,0:T(8,128)S(1)}, u32[]{:S(2)}, u32[]{:S(2)}) %collective-permute-start.5) | collective-permute-done | bytes 131104 | tf_op jit(solution)/shard_map/ppermute | solution.py:133
  12.0 2.8 %collective-permute-start.6 = (f32[2,16,8,128]{3,2,1,0:T(8,128)S(1)}, f32[2,16,8,128]{3,2,1,0:T(8,128)S(1)}, u32[]{:S(2)}, u32[]{:S(2)}) collective-permute-start(f32[2,16,8,128]{3,2,1,0:T(8,128)S(1)} %add_add_fusion), channel_id=1, source_target_pairs={{0,8},{2,6},{4,12},{6,2},{8,0},{10,14},{12,4},{14,10},{1,9},{3,7},... | collective-permute-start | bytes 393224 | tf_op jit(solution)/shard_map/ppermute | solution.py:133
  14.8 0.0 collective-permute-done
  14.8 0.7 %collective-permute-done.2 = f32[2,16,8,128]{3,2,1,0:T(8,128)S(1)} collective-permute-done((f32[2,16,8,128]{3,2,1,0:T(8,128)S(1)}, f32[2,16,8,128]{3,2,1,0:T(8,128)S(1)}, u32[]{:S(2)}, u32[]{:S(2)}) %collective-permute-start.2) | collective-permute-done | bytes 131104 | tf_op jit(solution)/shard_map/ppermute | solution.py:133
  15.5 2.6 %collective-permute-done.6 = f32[2,16,8,128]{3,2,1,0:T(8,128)S(1)} collective-permute-done((f32[2,16,8,128]{3,2,1,0:T(8,128)S(1)}, f32[2,16,8,128]{3,2,1,0:T(8,128)S(1)}, u32[]{:S(2)}, u32[]{:S(2)}) %collective-permute-start.6) | collective-permute-done | bytes 131104 | tf_op jit(solution)/shard_map/ppermute | solution.py:133
  18.0 2.6 %collective-permute-start.7 = (f32[2,16,8,128]{3,2,1,0:T(8,128)S(1)}, f32[2,16,8,128]{3,2,1,0:T(8,128)S(1)}, u32[]{:S(2)}, u32[]{:S(2)}) collective-permute-start(f32[2,16,8,128]{3,2,1,0:T(8,128)S(1)} %add_add_fusion.1.own_ref), channel_id=1, source_target_pairs={{0,1},{1,0},{2,3},{3,2},{4,5},{5,4},{6,7},{7,6},{8,9},{9,8},{10,11... | collective-permute-start | bytes 393224 | tf_op jit(solution)/shard_map/ppermute | solution.py:137
  20.7 2.9 %collective-permute-done.7.far_ref = f32[2,16,8,128]{3,2,1,0:T(8,128)S(1)} collective-permute-done((f32[2,16,8,128]{3,2,1,0:T(8,128)S(1)}, f32[2,16,8,128]{3,2,1,0:T(8,128)S(1)}, u32[]{:S(2)}, u32[]{:S(2)}) %collective-permute-start.7) | collective-permute-done | bytes 131104 | tf_op jit(solution)/shard_map/ppermute | solution.py:137
  23.6 0.5 %shard_map.38 = (f32[4,8,128]{2,1,0:T(8,128)S(1)}, s32[8,128]{1,0:T(8,128)S(1)}) custom-call(f32[2,16,8,128]{3,2,1,0:T(8,128)S(1)} %add_add_fusion.1.own_ref, f32[2,16,8,128]{3,2,1,0:T(8,128)S(1)} %collective-permute-done.7.far_ref), custom_call_target="tpu_custom_call" | custom-call | flops 2097152 | bytes 262144 | tf_op jit(solution)/shard_map/pallas_call | solution.py:114
  24.1 0.1 collective-permute-start.8
  24.2 1.2 %collective-permute-done.8 = f32[4,8,128]{2,1,0:T(8,128)S(1)} collective-permute-done((f32[4,8,128]{2,1,0:T(8,128)S(1)}, f32[4,8,128]{2,1,0:T(8,128)S(1)}, u32[]{:S(2)}, u32[]{:S(2)}) %collective-permute-start.8) | collective-permute-done | bytes 16416 | tf_op jit(solution)/shard_map/ppermute | solution.py:137
  25.4 1.9 %collective-permute-start.9 = (f32[2,8,128]{2,1,0:T(8,128)S(1)}, f32[2,8,128]{2,1,0:T(8,128)S(1)}, u32[]{:S(2)}, u32[]{:S(2)}) collective-permute-start(f32[2,8,128]{2,1,0:T(8,128)S(1)} %slice.29), channel_id=1, source_target_pairs={{0,6},{2,4},{4,2},{6,0},{8,14},{10,12},{12,10},{14,8},{1,7},{3,5},... | collective-permute-start | bytes 24584 | tf_op jit(solution)/shard_map/ppermute | solution.py:133
  27.2 1.4 %collective-permute-done.9 = f32[2,8,128]{2,1,0:T(8,128)S(1)} collective-permute-done((f32[2,8,128]{2,1,0:T(8,128)S(1)}, f32[2,8,128]{2,1,0:T(8,128)S(1)}, u32[]{:S(2)}, u32[]{:S(2)}) %collective-permute-start.9) | collective-permute-done | bytes 8224 | tf_op jit(solution)/shard_map/ppermute | solution.py:133
  28.6 2.9 %collective-permute-start.10 = (f32[8,128]{1,0:T(8,128)S(1)}, f32[8,128]{1,0:T(8,128)S(1)}, u32[]{:S(2)}, u32[]{:S(2)}) collective-permute-start(f32[8,128]{1,0:T(8,128)S(1)} %slice_bitcast_fusion), channel_id=1, source_target_pairs={{0,10},{2,8},{4,14},{6,12},{8,2},{10,0},{12,6},{14,4},{1,11},{3,9}... | collective-permute-start | bytes 12296 | tf_op jit(solution)/shard_map/ppermute | solution.py:133
  31.5 1.3 %collective-permute-done.10 = f32[8,128]{1,0:T(8,128)S(1)} collective-permute-done((f32[8,128]{1,0:T(8,128)S(1)}, f32[8,128]{1,0:T(8,128)S(1)}, u32[]{:S(2)}, u32[]{:S(2)}) %collective-permute-start.10) | collective-permute-done | bytes 4128 | tf_op jit(solution)/shard_map/ppermute | solution.py:133
  32.8 0.6 %select_bitcast_fusion = f32[16,4]{0,1:T(4,128)} fusion(f32[8,128]{1,0:T(8,128)S(1)} %fusion, s32[8,128]{1,0:T(8,128)S(1)} %get-tuple-element.23), kind=kLoop, calls=%fused_computation.6 | loop fusion | flops 128 | bytes 1024 | tf_op jit(solution)/shard_map/transpose | solution.py:167
  (9 shorter events, 0.1 us)
Async XLA Ops:
  3.4 1.5 %collective-permute-start.4 = (f32[2,16,8,128]{3,2,1,0:T(8,128)S(1)}, f32[2,16,8,128]{3,2,1,0:T(8,128)S(1)}, u32[]{:S(2)}, u32[]{:S(2)}) collective-permute-start(f32[2,16,8,128]{3,2,1,0:T(8,128)S(1)} %get-tuple-element.22), channel_id=1, source_target_pairs={{0,2},{2,0},{1,3},{3,1},{4,6},{6,4},{5,7},{7,5},{8,10},{10,8},{9,1... | collective-permute-start | bytes 393224 | tf_op jit(solution)/shard_map/ppermute | solution.py:137
  3.9 4.9 %collective-permute-start.1 = (f32[2,16,8,128]{3,2,1,0:T(8,128)S(1)}, f32[2,16,8,128]{3,2,1,0:T(8,128)S(1)}, u32[]{:S(2)}, u32[]{:S(2)}) collective-permute-start(f32[2,16,8,128]{3,2,1,0:T(8,128)S(1)} %get-tuple-element.18), channel_id=1, source_target_pairs={{0,2},{2,0},{1,3},{3,1},{4,6},{6,4},{5,7},{7,5},{8,10},{10,8},{9,1... | collective-permute-start | bytes 393224 | tf_op jit(solution)/shard_map/ppermute | solution.py:137
  4.0 6.5 %collective-permute-start.3 = (f32[2,16,8,128]{3,2,1,0:T(8,128)S(1)}, f32[2,16,8,128]{3,2,1,0:T(8,128)S(1)}, u32[]{:S(2)}, u32[]{:S(2)}) collective-permute-start(f32[2,16,8,128]{3,2,1,0:T(8,128)S(1)} %get-tuple-element.20), channel_id=1, source_target_pairs={{0,2},{2,0},{1,3},{3,1},{4,6},{6,4},{5,7},{7,5},{8,10},{10,8},{9,1... | collective-permute-start | bytes 393224 | tf_op jit(solution)/shard_map/ppermute | solution.py:137
  4.9 7.1 %collective-permute-start.5 = (f32[2,16,8,128]{3,2,1,0:T(8,128)S(1)}, f32[2,16,8,128]{3,2,1,0:T(8,128)S(1)}, u32[]{:S(2)}, u32[]{:S(2)}) collective-permute-start(f32[2,16,8,128]{3,2,1,0:T(8,128)S(1)} %add.34), channel_id=1, source_target_pairs={{0,4},{2,10},{4,0},{6,14},{8,12},{10,2},{12,8},{14,6},{1,5},{3,11}... | collective-permute-start | bytes 393224 | tf_op jit(solution)/shard_map/ppermute | solution.py:133
  7.9 6.9 %collective-permute-start = (f32[2,16,8,128]{3,2,1,0:T(8,128)S(1)}, f32[2,16,8,128]{3,2,1,0:T(8,128)S(1)}, u32[]{:S(2)}, u32[]{:S(2)}) collective-permute-start(f32[2,16,8,128]{3,2,1,0:T(8,128)S(1)} %get-tuple-element.16), channel_id=1, source_target_pairs={{0,2},{2,0},{1,3},{3,1},{4,6},{6,4},{5,7},{7,5},{8,10},{10,8},{9,1... | collective-permute-start | bytes 393224 | tf_op jit(solution)/shard_map/ppermute | solution.py:137
  8.8 6.7 %collective-permute-start.2 = (f32[2,16,8,128]{3,2,1,0:T(8,128)S(1)}, f32[2,16,8,128]{3,2,1,0:T(8,128)S(1)}, u32[]{:S(2)}, u32[]{:S(2)}) collective-permute-start(f32[2,16,8,128]{3,2,1,0:T(8,128)S(1)} %add.31), channel_id=1, source_target_pairs={{0,4},{2,10},{4,0},{6,14},{8,12},{10,2},{12,8},{14,6},{1,5},{3,11}... | collective-permute-start | bytes 393224 | tf_op jit(solution)/shard_map/ppermute | solution.py:133
  12.0 6.0 %collective-permute-start.6 = (f32[2,16,8,128]{3,2,1,0:T(8,128)S(1)}, f32[2,16,8,128]{3,2,1,0:T(8,128)S(1)}, u32[]{:S(2)}, u32[]{:S(2)}) collective-permute-start(f32[2,16,8,128]{3,2,1,0:T(8,128)S(1)} %add_add_fusion), channel_id=1, source_target_pairs={{0,8},{2,6},{4,12},{6,2},{8,0},{10,14},{12,4},{14,10},{1,9},{3,7},... | collective-permute-start | bytes 393224 | tf_op jit(solution)/shard_map/ppermute | solution.py:133
  18.0 5.6 %collective-permute-start.7 = (f32[2,16,8,128]{3,2,1,0:T(8,128)S(1)}, f32[2,16,8,128]{3,2,1,0:T(8,128)S(1)}, u32[]{:S(2)}, u32[]{:S(2)}) collective-permute-start(f32[2,16,8,128]{3,2,1,0:T(8,128)S(1)} %add_add_fusion.1.own_ref), channel_id=1, source_target_pairs={{0,1},{1,0},{2,3},{3,2},{4,5},{5,4},{6,7},{7,6},{8,9},{9,8},{10,11... | collective-permute-start | bytes 393224 | tf_op jit(solution)/shard_map/ppermute | solution.py:137
  24.1 1.2 %collective-permute-start.8 = (f32[4,8,128]{2,1,0:T(8,128)S(1)}, f32[4,8,128]{2,1,0:T(8,128)S(1)}, u32[]{:S(2)}, u32[]{:S(2)}) collective-permute-start(f32[4,8,128]{2,1,0:T(8,128)S(1)} %get-tuple-element.24), channel_id=1, source_target_pairs={{0,2},{2,0},{1,3},{3,1},{4,6},{6,4},{5,7},{7,5},{8,10},{10,8},{9,1... | collective-permute-start | bytes 49160 | tf_op jit(solution)/shard_map/ppermute | solution.py:137
  25.4 3.2 %collective-permute-start.9 = (f32[2,8,128]{2,1,0:T(8,128)S(1)}, f32[2,8,128]{2,1,0:T(8,128)S(1)}, u32[]{:S(2)}, u32[]{:S(2)}) collective-permute-start(f32[2,8,128]{2,1,0:T(8,128)S(1)} %slice.29), channel_id=1, source_target_pairs={{0,6},{2,4},{4,2},{6,0},{8,14},{10,12},{12,10},{14,8},{1,7},{3,5},... | collective-permute-start | bytes 24584 | tf_op jit(solution)/shard_map/ppermute | solution.py:133
  28.6 4.2 %collective-permute-start.10 = (f32[8,128]{1,0:T(8,128)S(1)}, f32[8,128]{1,0:T(8,128)S(1)}, u32[]{:S(2)}, u32[]{:S(2)}) collective-permute-start(f32[8,128]{1,0:T(8,128)S(1)} %slice_bitcast_fusion), channel_id=1, source_target_pairs={{0,10},{2,8},{4,14},{6,12},{8,2},{10,0},{12,6},{14,4},{1,11},{3,9}... | collective-permute-start | bytes 12296 | tf_op jit(solution)/shard_map/ppermute | solution.py:133

commit v5 on v4

--- a/solution.py
+++ b/solution.py
@@ -79,15 +79,15 @@
     )(*(pltpu.with_memory_space_constraint(a, pltpu.HBM) for a in (slab, factor_one, factor_two)))
 
 
-def gram_kernel(scale, own_ref, far_ref, out_ref, flag_ref, total, gram):
+def gram_kernel(scale, own_ref, own_add, far_ref, far_add, out_ref, flag_ref, total, gram):
     groups, depth, tile, _ = own_ref.shape
     z, core, x = (lax.axis_index(name) for name in ("z", "core", "col"))
     chips, share, _ = out_ref.shape
     size = depth * tile
     value = jnp.zeros((2 * depth, depth), jnp.float32)
     for g in range(groups):
-        total[g, pl.ds(pl.multiple_of(x * size, size), size), :] = own_ref[g].reshape(size, -1)
-        total[g, pl.ds(pl.multiple_of((1 - x) * size, size), size), :] = far_ref[g].reshape(size, -1)
+        total[g, pl.ds(pl.multiple_of(x * size, size), size), :] = (own_ref[g] + own_add[g]).reshape(size, -1)
+        total[g, pl.ds(pl.multiple_of((1 - x) * size, size), size), :] = (far_ref[g] + far_add[g]).reshape(size, -1)
     for g in range(groups):
         for s in range(tile):
             rows = total[g, pl.ds(s, 2 * depth, stride=tile), :]
@@ -109,28 +109,31 @@
 
 
 def gram_blocks(own, far, chips, scale):
-    groups, depth, tile, r1 = own.shape
+    groups, depth, tile, r1 = own[0].shape
     full = 2 * depth
     return pl.pallas_call(
         functools.partial(gram_kernel, scale),
         out_shape=(pltpu.VMEM((chips, full // chips, 128), jnp.float32), pltpu.VMEM((TILE, 128), jnp.int32)),
-        in_specs=[pl.BlockSpec(memory_space=pltpu.VMEM)] * 2,
+        in_specs=[pl.BlockSpec(memory_space=pltpu.VMEM)] * 4,
         out_specs=[pl.BlockSpec(memory_space=pltpu.VMEM)] * 2,
         scratch_shapes=[
             pltpu.VMEM((groups, full * tile, r1), jnp.float32),
             pltpu.VMEM((full, 128), jnp.float32),
         ],
         cost_estimate=pl.CostEstimate(
-            flops=2 * groups * full * depth * tile * r1, bytes_accessed=8 * own.size, transcendentals=0
+            flops=2 * groups * full * depth * tile * r1, bytes_accessed=16 * own[0].size, transcendentals=0
         ),
-    )(*(pltpu.with_memory_space_constraint(a, pltpu.VMEM) for a in (own, far)))
-
-
-def hop(value, zs, masks, cross=0):
-    pairs = [
-        (z * CORES + core, (z ^ masks[core]) * CORES + (core ^ cross)) for z in range(zs) for core in range(CORES)
-    ]
-    return lax.ppermute(value, ("z", "core"), pairs)
+    )(*(pltpu.with_memory_space_constraint(a, pltpu.VMEM) for a in own + far))
+
+
+def hop(value, zs, masks, cross=0, flip=0):
+    pairs = []
+    for z in range(zs):
+        for core in range(CORES):
+            for x in range(2):
+                to = ((z ^ masks[core]) * CORES + (core ^ cross)) * 2 + (x ^ flip)
+                pairs.append(((z * CORES + core) * 2 + x, to))
+    return lax.ppermute(value, ("z", "core", "col"), pairs)
 
 
 def swap(value, axis):
@@ -158,8 +161,11 @@
     passed, given, across, own = (o + swap(t, "core") for t, o in zip(parts[:zs], parts[zs:]))
     arrived = hop(passed, zs, FIRST_HOP)
     beside = hop(given, zs, FIRST_HOP)
-    own = own + beside + hop(across + arrived, zs, SECOND_HOP)
-    blocks, flag = gram_blocks(own, swap(own, "col"), zs, scale)
+    onward = across + arrived
+    far_add = hop(onward, zs, SECOND_HOP, flip=1)
+    own_add = hop(onward, zs, SECOND_HOP)
+    own = lax.optimization_barrier((own, onward))[0] + beside
+    blocks, flag = gram_blocks((own, own_add), (swap(own, "col"), far_add), zs, scale)
     blocks = blocks + swap(blocks, "core")
     pair = blocks[:2] + hop(blocks[2:], zs, (FIRST, FIRST), cross=1)
     last = pair[0] + hop(pair[1], zs, (SECOND, SECOND), cross=1)

time: 33.6 us -> 32.5 us (0.967)
  starting transfers between devices: 16.8 us -> 13.5 us
  waiting for transfers between devices: 12.1 us -> 14.3 us
    ppermute x5 -> x6, waiting for transfers between devices: 7.45 us -> 12.7 us  [hop(): return lax.ppermute(value, ('z', 'core', 'col'), pairs)]
    ppermute x6, waiting for transfers between devices: 4.6 us -> 1.58 us  [swap(): return lax.ppermute(value, axis, [(0, 1), (1, 0)])]
    ppermute x6, starting transfers between devices: 4.61 us -> 1.96 us  [swap(): return lax.ppermute(value, axis, [(0, 1), (1, 0)])]
    ppermute x5 -> x6, starting transfers between devices: 12.2 us -> 11.5 us  [hop(): return lax.ppermute(value, ('z', 'core', 'col'), pairs)]
  transfers between devices with their start and end apart: 11 -> 12, of which waited for: 8 -> 7; matrix products, arithmetic and copies ran while one was open for 0% -> 0% of each run, Pallas kernels for 0% -> 0%
where the time goes in v5:
time: 32.5 us; the launch traced here: 32.4 us
  waiting for transfers between devices  14.3 us (44%)
  starting transfers between devices  13.5 us (42%)
  Pallas kernels  3.86 us (12%)
  other arithmetic  0.7 us (2%)
    ppermute x6, waiting for transfers between devices, hop(): return lax.ppermute(value, ('z', 'core', 'col'), pairs)  12.7 us
    ppermute x6, starting transfers between devices, hop(): return lax.ppermute(value, ('z', 'core', 'col'), pairs)  11.5 us
    pallas_call x1, Pallas kernels, project(): pl.pallas_call(functools.partial(project_kernel, chunk, starts), out_shap...  3.35 us
    ppermute x6, starting transfers between devices, swap(): return lax.ppermute(value, axis, [(0, 1), (1, 0)])  1.96 us
    ppermute x6, waiting for transfers between devices, swap(): return lax.ppermute(value, axis, [(0, 1), (1, 0)])  1.58 us
  transfers between devices with their start and end apart: 12, of which 7 were waited for; matrix products, arithmetic and copies ran while one was open for 0% of the time, Pallas kernels for 0%

profile of v5, /device:TPU:0, one launch (start us, length us, event | category | flops | bytes accessed | tf_op | source)
XLA Modules:
  0.0 32.4 jit_solution(11860649553126826371)
XLA Ops:
  0.0 3.3 %shard_map.37 = (f32[2,16,8,128]{3,2,1,0:T(8,128)S(1)}, f32[2,16,8,128]{3,2,1,0:T(8,128)S(1)}, f32[2,16,8,128]{3,2,1,0:T(8,128)S(1)}, f32[2,16,8,128]{3,2,1,0:T(...) custom-call(bf16[16,64,2048]{2,1,0:T(8,128)(2,1)} %slab_ref.1, ...), custom_call_target="tpu_custom_call" | custom-call | flops 570425344 | bytes 5767168 | tf_op jit(solution)/shard_map/pallas_call | solution.py:61
  3.4 0.5 %collective-permute-start.2 = (f32[2,16,8,128]{3,2,1,0:T(8,128)S(1)}, f32[2,16,8,128]{3,2,1,0:T(8,128)S(1)}, u32[]{:S(2)}, u32[]{:S(2)}) collective-permute-start(f32[2,16,8,128]{3,2,1,0:T(8,128)S(1)} %get-tuple-element.21), channel_id=1, source_target_pairs={{0,2},{2,0},{1,3},{3,1},{4,6},{6,4},{5,7},{7,5},{8,10},{10,8},{9,1... | collective-permute-start | bytes 393224 | tf_op jit(solution)/shard_map/ppermute | solution.py:140
  3.9 0.1 collective-permute-start.4
  4.0 0.4 %collective-permute-start = (f32[2,16,8,128]{3,2,1,0:T(8,128)S(1)}, f32[2,16,8,128]{3,2,1,0:T(8,128)S(1)}, u32[]{:S(2)}, u32[]{:S(2)}) collective-permute-start(f32[2,16,8,128]{3,2,1,0:T(8,128)S(1)} %get-tuple-element.17), channel_id=1, source_target_pairs={{0,2},{2,0},{1,3},{3,1},{4,6},{6,4},{5,7},{7,5},{8,10},{10,8},{9,1... | collective-permute-start | bytes 393224 | tf_op jit(solution)/shard_map/ppermute | solution.py:140
  4.4 0.1 collective-permute-start.1
  4.5 0.4 %collective-permute-done.2 = f32[2,16,8,128]{3,2,1,0:T(8,128)S(1)} collective-permute-done((f32[2,16,8,128]{3,2,1,0:T(8,128)S(1)}, f32[2,16,8,128]{3,2,1,0:T(8,128)S(1)}, u32[]{:S(2)}, u32[]{:S(2)}) %collective-permute-start.2) | collective-permute-done | bytes 131104 | tf_op jit(solution)/shard_map/ppermute | solution.py:140
  4.9 3.0 %collective-permute-start.3 = (f32[2,16,8,128]{3,2,1,0:T(8,128)S(1)}, f32[2,16,8,128]{3,2,1,0:T(8,128)S(1)}, u32[]{:S(2)}, u32[]{:S(2)}) collective-permute-start(f32[2,16,8,128]{3,2,1,0:T(8,128)S(1)} %add.29), channel_id=1, source_target_pairs={{0,4},{1,5},{2,10},{3,11},{4,0},{5,1},{6,14},{7,15},{8,12},{9,13},... | collective-permute-start | bytes 393224 | tf_op jit(solution)/shard_map/ppermute | solution.py:136
  7.9 0.0 collective-permute-done.4
  7.9 0.2 collective-permute-start.5
  8.1 0.0 collective-permute-done
  8.1 0.0 collective-permute-done.1
  8.1 3.8 %collective-permute-done.3 = f32[2,16,8,128]{3,2,1,0:T(8,128)S(1)} collective-permute-done((f32[2,16,8,128]{3,2,1,0:T(8,128)S(1)}, f32[2,16,8,128]{3,2,1,0:T(8,128)S(1)}, u32[]{:S(2)}, u32[]{:S(2)}) %collective-permute-start.3) | collective-permute-done | bytes 131104 | tf_op jit(solution)/shard_map/ppermute | solution.py:136
  12.0 3.7 %collective-permute-start.8 = (f32[2,16,8,128]{3,2,1,0:T(8,128)S(1)}, f32[2,16,8,128]{3,2,1,0:T(8,128)S(1)}, u32[]{:S(2)}, u32[]{:S(2)}) collective-permute-start(f32[2,16,8,128]{3,2,1,0:T(8,128)S(1)} %add_add_fusion), channel_id=1, source_target_pairs={{0,9},{1,8},{2,7},{3,6},{4,13},{5,12},{6,3},{7,2},{8,1},{9,0},{10,... | collective-permute-start | bytes 393224 | tf_op jit(solution)/shard_map/ppermute | solution.py:136
  15.7 0.8 %collective-permute-start.6 = (f32[2,16,8,128]{3,2,1,0:T(8,128)S(1)}, f32[2,16,8,128]{3,2,1,0:T(8,128)S(1)}, u32[]{:S(2)}, u32[]{:S(2)}) collective-permute-start(f32[2,16,8,128]{3,2,1,0:T(8,128)S(1)} %add_add_fusion), channel_id=1, source_target_pairs={{0,8},{1,9},{2,6},{3,7},{4,12},{5,13},{6,2},{7,3},{8,0},{9,1},{10,... | collective-permute-start | bytes 393224 | tf_op jit(solution)/shard_map/ppermute | solution.py:136
  16.5 0.0 collective-permute-done.5
  16.6 0.8 %collective-permute-start.7 = (f32[2,16,8,128]{3,2,1,0:T(8,128)S(1)}, f32[2,16,8,128]{3,2,1,0:T(8,128)S(1)}, u32[]{:S(2)}, u32[]{:S(2)}) collective-permute-start(f32[2,16,8,128]{3,2,1,0:T(8,128)S(1)} %add.32.own_ref), channel_id=1, source_target_pairs={{0,1},{1,0},{2,3},{3,2},{4,5},{5,4},{6,7},{7,6},{8,9},{9,8},{10,11... | collective-permute-start | bytes 393224 | tf_op jit(solution)/shard_map/ppermute | solution.py:140
  17.3 1.7 %collective-permute-done.8.far_add = f32[2,16,8,128]{3,2,1,0:T(8,128)S(1)} collective-permute-done((f32[2,16,8,128]{3,2,1,0:T(8,128)S(1)}, f32[2,16,8,128]{3,2,1,0:T(8,128)S(1)}, u32[]{:S(2)}, u32[]{:S(2)}) %collective-permute-start.8) | collective-permute-done | bytes 131104 | tf_op jit(solution)/shard_map/ppermute | solution.py:136
  19.0 4.0 %collective-permute-done.6.own_add = f32[2,16,8,128]{3,2,1,0:T(8,128)S(1)} collective-permute-done((f32[2,16,8,128]{3,2,1,0:T(8,128)S(1)}, f32[2,16,8,128]{3,2,1,0:T(8,128)S(1)}, u32[]{:S(2)}, u32[]{:S(2)}) %collective-permute-start.6) | collective-permute-done | bytes 131104 | tf_op jit(solution)/shard_map/ppermute | solution.py:136
  23.0 0.0 collective-permute-done.7.far_ref
  23.0 0.5 %shard_map.38 = (f32[4,8,128]{2,1,0:T(8,128)S(1)}, s32[8,128]{1,0:T(8,128)S(1)}) custom-call(f32[2,16,8,128]{3,2,1,0:T(8,128)S(1)} %add.32.own_ref, f32[2,16,8,128]{3,2,1,0:T(8,128)S(1)} %collective-permute-done.6.own_add, f32[2,16,8,128]{3,2,1,0:T(8,128)S(1)} %collective-permute-done.7.far_ref, f32[2,16,8,128]{3,2,1,0:T(8,128)S(1)} %collective-permute-done.8.far_add), custom_call_target="tpu_custom_call" | custom-call | flops 2097152 | bytes 524288 | tf_op jit(solution)/shard_map/pallas_call | solution.py:114
  23.5 0.1 collective-permute-start.9
  23.6 1.2 %collective-permute-done.9 = f32[4,8,128]{2,1,0:T(8,128)S(1)} collective-permute-done((f32[4,8,128]{2,1,0:T(8,128)S(1)}, f32[4,8,128]{2,1,0:T(8,128)S(1)}, u32[]{:S(2)}, u32[]{:S(2)}) %collective-permute-start.9) | collective-permute-done | bytes 16416 | tf_op jit(solution)/shard_map/ppermute | solution.py:140
  24.8 1.2 %collective-permute-start.10 = (f32[2,8,128]{2,1,0:T(8,128)S(1)}, f32[2,8,128]{2,1,0:T(8,128)S(1)}, u32[]{:S(2)}, u32[]{:S(2)}) collective-permute-start(f32[2,8,128]{2,1,0:T(8,128)S(1)} %slice.29), channel_id=1, source_target_pairs={{0,6},{1,7},{2,4},{3,5},{4,2},{5,3},{6,0},{7,1},{8,14},{9,15},{10,... | collective-permute-start | bytes 24584 | tf_op jit(solution)/shard_map/ppermute | solution.py:136
  25.9 1.9 %collective-permute-done.10 = f32[2,8,128]{2,1,0:T(8,128)S(1)} collective-permute-done((f32[2,8,128]{2,1,0:T(8,128)S(1)}, f32[2,8,128]{2,1,0:T(8,128)S(1)}, u32[]{:S(2)}, u32[]{:S(2)}) %collective-permute-start.10) | collective-permute-done | bytes 8224 | tf_op jit(solution)/shard_map/ppermute | solution.py:136
  27.8 2.6 %collective-permute-start.11 = (f32[8,128]{1,0:T(8,128)S(1)}, f32[8,128]{1,0:T(8,128)S(1)}, u32[]{:S(2)}, u32[]{:S(2)}) collective-permute-start(f32[8,128]{1,0:T(8,128)S(1)} %slice_bitcast_fusion), channel_id=1, source_target_pairs={{0,10},{1,11},{2,8},{3,9},{4,14},{5,15},{6,12},{7,13},{8,2},{9,3},... | collective-permute-start | bytes 12296 | tf_op jit(solution)/shard_map/ppermute | solution.py:136
  30.5 1.3 %collective-permute-done.11 = f32[8,128]{1,0:T(8,128)S(1)} collective-permute-done((f32[8,128]{1,0:T(8,128)S(1)}, f32[8,128]{1,0:T(8,128)S(1)}, u32[]{:S(2)}, u32[]{:S(2)}) %collective-permute-start.11) | collective-permute-done | bytes 4128 | tf_op jit(solution)/shard_map/ppermute | solution.py:136
  31.8 0.6 %select_bitcast_fusion = f32[16,4]{0,1:T(4,128)} fusion(f32[8,128]{1,0:T(8,128)S(1)} %fusion, s32[8,128]{1,0:T(8,128)S(1)} %get-tuple-element.25), kind=kLoop, calls=%fused_computation.5 | loop fusion | flops 128 | bytes 1024 | tf_op jit(solution)/shard_map/transpose | solution.py:173
  (10 shorter events, 0.1 us)
Async XLA Ops:
  3.4 1.5 %collective-permute-start.2 = (f32[2,16,8,128]{3,2,1,0:T(8,128)S(1)}, f32[2,16,8,128]{3,2,1,0:T(8,128)S(1)}, u32[]{:S(2)}, u32[]{:S(2)}) collective-permute-start(f32[2,16,8,128]{3,2,1,0:T(8,128)S(1)} %get-tuple-element.21), channel_id=1, source_target_pairs={{0,2},{2,0},{1,3},{3,1},{4,6},{6,4},{5,7},{7,5},{8,10},{10,8},{9,1... | collective-permute-start | bytes 393224 | tf_op jit(solution)/shard_map/ppermute | solution.py:140
  3.9 4.0 %collective-permute-start.4 = (f32[2,16,8,128]{3,2,1,0:T(8,128)S(1)}, f32[2,16,8,128]{3,2,1,0:T(8,128)S(1)}, u32[]{:S(2)}, u32[]{:S(2)}) collective-permute-start(f32[2,16,8,128]{3,2,1,0:T(8,128)S(1)} %get-tuple-element.24), channel_id=1, source_target_pairs={{0,2},{2,0},{1,3},{3,1},{4,6},{6,4},{5,7},{7,5},{8,10},{10,8},{9,1... | collective-permute-start | bytes 393224 | tf_op jit(solution)/shard_map/ppermute | solution.py:140
  4.0 4.1 %collective-permute-start = (f32[2,16,8,128]{3,2,1,0:T(8,128)S(1)}, f32[2,16,8,128]{3,2,1,0:T(8,128)S(1)}, u32[]{:S(2)}, u32[]{:S(2)}) collective-permute-start(f32[2,16,8,128]{3,2,1,0:T(8,128)S(1)} %get-tuple-element.17), channel_id=1, source_target_pairs={{0,2},{2,0},{1,3},{3,1},{4,6},{6,4},{5,7},{7,5},{8,10},{10,8},{9,1... | collective-permute-start | bytes 393224 | tf_op jit(solution)/shard_map/ppermute | solution.py:140
  4.4 3.7 %collective-permute-start.1 = (f32[2,16,8,128]{3,2,1,0:T(8,128)S(1)}, f32[2,16,8,128]{3,2,1,0:T(8,128)S(1)}, u32[]{:S(2)}, u32[]{:S(2)}) collective-permute-start(f32[2,16,8,128]{3,2,1,0:T(8,128)S(1)} %get-tuple-element.19), channel_id=1, source_target_pairs={{0,2},{2,0},{1,3},{3,1},{4,6},{6,4},{5,7},{7,5},{8,10},{10,8},{9,1... | collective-permute-start | bytes 393224 | tf_op jit(solution)/shard_map/ppermute | solution.py:140
  4.9 7.1 %collective-permute-start.3 = (f32[2,16,8,128]{3,2,1,0:T(8,128)S(1)}, f32[2,16,8,128]{3,2,1,0:T(8,128)S(1)}, u32[]{:S(2)}, u32[]{:S(2)}) collective-permute-start(f32[2,16,8,128]{3,2,1,0:T(8,128)S(1)} %add.29), channel_id=1, source_target_pairs={{0,4},{1,5},{2,10},{3,11},{4,0},{5,1},{6,14},{7,15},{8,12},{9,13},... | collective-permute-start | bytes 393224 | tf_op jit(solution)/shard_map/ppermute | solution.py:136
  7.9 8.6 %collective-permute-start.5 = (f32[2,16,8,128]{3,2,1,0:T(8,128)S(1)}, f32[2,16,8,128]{3,2,1,0:T(8,128)S(1)}, u32[]{:S(2)}, u32[]{:S(2)}) collective-permute-start(f32[2,16,8,128]{3,2,1,0:T(8,128)S(1)} %add.31), channel_id=1, source_target_pairs={{0,4},{1,5},{2,10},{3,11},{4,0},{5,1},{6,14},{7,15},{8,12},{9,13},... | collective-permute-start | bytes 393224 | tf_op jit(solution)/shard_map/ppermute | solution.py:136
  12.0 7.0 %collective-permute-start.8 = (f32[2,16,8,128]{3,2,1,0:T(8,128)S(1)}, f32[2,16,8,128]{3,2,1,0:T(8,128)S(1)}, u32[]{:S(2)}, u32[]{:S(2)}) collective-permute-start(f32[2,16,8,128]{3,2,1,0:T(8,128)S(1)} %add_add_fusion), channel_id=1, source_target_pairs={{0,9},{1,8},{2,7},{3,6},{4,13},{5,12},{6,3},{7,2},{8,1},{9,0},{10,... | collective-permute-start | bytes 393224 | tf_op jit(solution)/shard_map/ppermute | solution.py:136
  15.7 7.3 %collective-permute-start.6 = (f32[2,16,8,128]{3,2,1,0:T(8,128)S(1)}, f32[2,16,8,128]{3,2,1,0:T(8,128)S(1)}, u32[]{:S(2)}, u32[]{:S(2)}) collective-permute-start(f32[2,16,8,128]{3,2,1,0:T(8,128)S(1)} %add_add_fusion), channel_id=1, source_target_pairs={{0,8},{1,9},{2,6},{3,7},{4,12},{5,13},{6,2},{7,3},{8,0},{9,1},{10,... | collective-permute-start | bytes 393224 | tf_op jit(solution)/shard_map/ppermute | solution.py:136
  16.6 6.4 %collective-permute-start.7 = (f32[2,16,8,128]{3,2,1,0:T(8,128)S(1)}, f32[2,16,8,128]{3,2,1,0:T(8,128)S(1)}, u32[]{:S(2)}, u32[]{:S(2)}) collective-permute-start(f32[2,16,8,128]{3,2,1,0:T(8,128)S(1)} %add.32.own_ref), channel_id=1, source_target_pairs={{0,1},{1,0},{2,3},{3,2},{4,5},{5,4},{6,7},{7,6},{8,9},{9,8},{10,11... | collective-permute-start | bytes 393224 | tf_op jit(solution)/shard_map/ppermute | solution.py:140
  23.5 1.2 %collective-permute-start.9 = (f32[4,8,128]{2,1,0:T(8,128)S(1)}, f32[4,8,128]{2,1,0:T(8,128)S(1)}, u32[]{:S(2)}, u32[]{:S(2)}) collective-permute-start(f32[4,8,128]{2,1,0:T(8,128)S(1)} %get-tuple-element.26), channel_id=1, source_target_pairs={{0,2},{2,0},{1,3},{3,1},{4,6},{6,4},{5,7},{7,5},{8,10},{10,8},{9,1... | collective-permute-start | bytes 49160 | tf_op jit(solution)/shard_map/ppermute | solution.py:140
  24.8 3.1 %collective-permute-start.10 = (f32[2,8,128]{2,1,0:T(8,128)S(1)}, f32[2,8,128]{2,1,0:T(8,128)S(1)}, u32[]{:S(2)}, u32[]{:S(2)}) collective-permute-start(f32[2,8,128]{2,1,0:T(8,128)S(1)} %slice.29), channel_id=1, source_target_pairs={{0,6},{1,7},{2,4},{3,5},{4,2},{5,3},{6,0},{7,1},{8,14},{9,15},{10,... | collective-permute-start | bytes 24584 | tf_op jit(solution)/shard_map/ppermute | solution.py:136
  27.8 4.0 %collective-permute-start.11 = (f32[8,128]{1,0:T(8,128)S(1)}, f32[8,128]{1,0:T(8,128)S(1)}, u32[]{:S(2)}, u32[]{:S(2)}) collective-permute-start(f32[8,128]{1,0:T(8,128)S(1)} %slice_bitcast_fusion), channel_id=1, source_target_pairs={{0,10},{1,11},{2,8},{3,9},{4,14},{5,15},{6,12},{7,13},{8,2},{9,3},... | collective-permute-start | bytes 12296 | tf_op jit(solution)/shard_map/ppermute | solution.py:136

commit v6 on v5

--- a/solution.py
+++ b/solution.py
@@ -19,15 +19,17 @@
     outs, (slab_buf, one_buf, two_buf, turned, sems) = rest[:-5], rest[-5:]
     depth, width, _ = slab_ref.shape
     chunks = depth // chunk
+    copies = []
+    for c in range(chunks):
+        part = pl.ds(c * chunk, chunk)
+        copies.append(pltpu.make_async_copy(slab_ref.at[part], slab_buf.at[part], sems.at[c]))
+    copies[0].start()
     one_copy = pltpu.make_async_copy(one_ref, one_buf, sems.at[chunks])
     one_copy.start()
     two_copy = pltpu.make_async_copy(two_ref, two_buf, sems.at[chunks + 1])
     two_copy.start()
-    copies = []
-    for c in range(chunks):
-        part = pl.ds(c * chunk, chunk)
-        copies.append(pltpu.make_async_copy(slab_ref.at[part], slab_buf.at[part], sems.at[c]))
-        copies[-1].start()
+    for copy in copies[1:]:
+        copy.start()
     two_copy.wait()
     turned[...] = two_buf[...].astype(jnp.float32).T
     pieces = [turned[pl.ds(pl.multiple_of(s, TILE), TILE), :] for s in starts()]
@@ -46,7 +48,10 @@
     for c in range(chunks):
         copies[c].wait()
         rows = slab_buf[pl.ds(c * chunk, chunk)].reshape(chunk * width, -1)
-        first = jnp.dot(rows, one_buf[...], preferred_element_type=jnp.float32).astype(jnp.bfloat16)
+        middle = rows.shape[1] // 2
+        first = jnp.dot(rows[:, :middle], one_buf[:middle], preferred_element_type=jnp.float32)
+        first = first + jnp.dot(rows[:, middle:], one_buf[middle:], preferred_element_type=jnp.float32)
+        first = first.astype(jnp.bfloat16)
         if late is not None:
             second(c - 1, late)
         late = first

time: 32.5 us -> 32.5 us (level)
  no operation moved by 1% of the time
where the time goes in v6:
time: 32.5 us; the launch traced here: 32.3 us
  waiting for transfers between devices  14.3 us (44%)
  starting transfers between devices  13.5 us (42%)
  Pallas kernels  3.81 us (12%)
  other arithmetic  0.7 us (2%)
    ppermute x6, waiting for transfers between devices, hop(): return lax.ppermute(value, ('z', 'core', 'col'), pairs)  12.7 us
    ppermute x6, starting transfers between devices, hop(): return lax.ppermute(value, ('z', 'core', 'col'), pairs)  11.5 us
    pallas_call x1, Pallas kernels, project(): pl.pallas_call(functools.partial(project_kernel, chunk, starts), out_shap...  3.31 us
    ppermute x6, starting transfers between devices, swap(): return lax.ppermute(value, axis, [(0, 1), (1, 0)])  1.96 us
    ppermute x6, waiting for transfers between devices, swap(): return lax.ppermute(value, axis, [(0, 1), (1, 0)])  1.58 us
  transfers between devices with their start and end apart: 12, of which 7 were waited for; matrix products, arithmetic and copies ran while one was open for 0% of the time, Pallas kernels for 0%

profile of v6, /device:TPU:0, one launch (start us, length us, event | category | flops | bytes accessed | tf_op | source)
XLA Modules:
  0.0 32.3 jit_solution(12193958747501558309)
XLA Ops:
  0.0 3.3 %shard_map.37 = (f32[2,16,8,128]{3,2,1,0:T(8,128)S(1)}, f32[2,16,8,128]{3,2,1,0:T(8,128)S(1)}, f32[2,16,8,128]{3,2,1,0:T(8,128)S(1)}, f32[2,16,8,128]{3,2,1,0:T(...) custom-call(bf16[16,64,2048]{2,1,0:T(8,128)(2,1)} %slab_ref.1, ...), custom_call_target="tpu_custom_call" | custom-call | flops 570425344 | bytes 5767168 | tf_op jit(solution)/shard_map/pallas_call | solution.py:66
  3.3 0.5 %collective-permute-start.2 = (f32[2,16,8,128]{3,2,1,0:T(8,128)S(1)}, f32[2,16,8,128]{3,2,1,0:T(8,128)S(1)}, u32[]{:S(2)}, u32[]{:S(2)}) collective-permute-start(f32[2,16,8,128]{3,2,1,0:T(8,128)S(1)} %get-tuple-element.21), channel_id=1, source_target_pairs={{0,2},{2,0},{1,3},{3,1},{4,6},{6,4},{5,7},{7,5},{8,10},{10,8},{9,1... | collective-permute-start | bytes 393224 | tf_op jit(solution)/shard_map/ppermute | solution.py:145
  3.8 0.1 collective-permute-start.4
  3.9 0.4 %collective-permute-start = (f32[2,16,8,128]{3,2,1,0:T(8,128)S(1)}, f32[2,16,8,128]{3,2,1,0:T(8,128)S(1)}, u32[]{:S(2)}, u32[]{:S(2)}) collective-permute-start(f32[2,16,8,128]{3,2,1,0:T(8,128)S(1)} %get-tuple-element.17), channel_id=1, source_target_pairs={{0,2},{2,0},{1,3},{3,1},{4,6},{6,4},{5,7},{7,5},{8,10},{10,8},{9,1... | collective-permute-start | bytes 393224 | tf_op jit(solution)/shard_map/ppermute | solution.py:145
  4.3 0.1 collective-permute-start.1
  4.4 0.4 %collective-permute-done.2 = f32[2,16,8,128]{3,2,1,0:T(8,128)S(1)} collective-permute-done((f32[2,16,8,128]{3,2,1,0:T(8,128)S(1)}, f32[2,16,8,128]{3,2,1,0:T(8,128)S(1)}, u32[]{:S(2)}, u32[]{:S(2)}) %collective-permute-start.2) | collective-permute-done | bytes 131104 | tf_op jit(solution)/shard_map/ppermute | solution.py:145
  4.8 3.0 %collective-permute-start.3 = (f32[2,16,8,128]{3,2,1,0:T(8,128)S(1)}, f32[2,16,8,128]{3,2,1,0:T(8,128)S(1)}, u32[]{:S(2)}, u32[]{:S(2)}) collective-permute-start(f32[2,16,8,128]{3,2,1,0:T(8,128)S(1)} %add.29), channel_id=1, source_target_pairs={{0,4},{1,5},{2,10},{3,11},{4,0},{5,1},{6,14},{7,15},{8,12},{9,13},... | collective-permute-start | bytes 393224 | tf_op jit(solution)/shard_map/ppermute | solution.py:141
  7.8 0.0 collective-permute-done.4
  7.9 0.2 collective-permute-start.5
  8.0 0.0 collective-permute-done
  8.0 0.0 collective-permute-done.1
  8.1 3.8 %collective-permute-done.3 = f32[2,16,8,128]{3,2,1,0:T(8,128)S(1)} collective-permute-done((f32[2,16,8,128]{3,2,1,0:T(8,128)S(1)}, f32[2,16,8,128]{3,2,1,0:T(8,128)S(1)}, u32[]{:S(2)}, u32[]{:S(2)}) %collective-permute-start.3) | collective-permute-done | bytes 131104 | tf_op jit(solution)/shard_map/ppermute | solution.py:141
  11.9 3.7 %collective-permute-start.8 = (f32[2,16,8,128]{3,2,1,0:T(8,128)S(1)}, f32[2,16,8,128]{3,2,1,0:T(8,128)S(1)}, u32[]{:S(2)}, u32[]{:S(2)}) collective-permute-start(f32[2,16,8,128]{3,2,1,0:T(8,128)S(1)} %add_add_fusion), channel_id=1, source_target_pairs={{0,9},{1,8},{2,7},{3,6},{4,13},{5,12},{6,3},{7,2},{8,1},{9,0},{10,... | collective-permute-start | bytes 393224 | tf_op jit(solution)/shard_map/ppermute | solution.py:141
  15.7 0.8 %collective-permute-start.6 = (f32[2,16,8,128]{3,2,1,0:T(8,128)S(1)}, f32[2,16,8,128]{3,2,1,0:T(8,128)S(1)}, u32[]{:S(2)}, u32[]{:S(2)}) collective-permute-start(f32[2,16,8,128]{3,2,1,0:T(8,128)S(1)} %add_add_fusion), channel_id=1, source_target_pairs={{0,8},{1,9},{2,6},{3,7},{4,12},{5,13},{6,2},{7,3},{8,0},{9,1},{10,... | collective-permute-start | bytes 393224 | tf_op jit(solution)/shard_map/ppermute | solution.py:141
  16.5 0.0 collective-permute-done.5
  16.5 0.8 %collective-permute-start.7 = (f32[2,16,8,128]{3,2,1,0:T(8,128)S(1)}, f32[2,16,8,128]{3,2,1,0:T(8,128)S(1)}, u32[]{:S(2)}, u32[]{:S(2)}) collective-permute-start(f32[2,16,8,128]{3,2,1,0:T(8,128)S(1)} %add.32.own_ref), channel_id=1, source_target_pairs={{0,1},{1,0},{2,3},{3,2},{4,5},{5,4},{6,7},{7,6},{8,9},{9,8},{10,11... | collective-permute-start | bytes 393224 | tf_op jit(solution)/shard_map/ppermute | solution.py:145
  17.3 1.7 %collective-permute-done.8.far_add = f32[2,16,8,128]{3,2,1,0:T(8,128)S(1)} collective-permute-done((f32[2,16,8,128]{3,2,1,0:T(8,128)S(1)}, f32[2,16,8,128]{3,2,1,0:T(8,128)S(1)}, u32[]{:S(2)}, u32[]{:S(2)}) %collective-permute-start.8) | collective-permute-done | bytes 131104 | tf_op jit(solution)/shard_map/ppermute | solution.py:141
  19.0 4.0 %collective-permute-done.6.own_add = f32[2,16,8,128]{3,2,1,0:T(8,128)S(1)} collective-permute-done((f32[2,16,8,128]{3,2,1,0:T(8,128)S(1)}, f32[2,16,8,128]{3,2,1,0:T(8,128)S(1)}, u32[]{:S(2)}, u32[]{:S(2)}) %collective-permute-start.6) | collective-permute-done | bytes 131104 | tf_op jit(solution)/shard_map/ppermute | solution.py:141
  22.9 0.0 collective-permute-done.7.far_ref
  22.9 0.5 %shard_map.38 = (f32[4,8,128]{2,1,0:T(8,128)S(1)}, s32[8,128]{1,0:T(8,128)S(1)}) custom-call(f32[2,16,8,128]{3,2,1,0:T(8,128)S(1)} %add.32.own_ref, f32[2,16,8,128]{3,2,1,0:T(8,128)S(1)} %collective-permute-done.6.own_add, f32[2,16,8,128]{3,2,1,0:T(8,128)S(1)} %collective-permute-done.7.far_ref, f32[2,16,8,128]{3,2,1,0:T(8,128)S(1)} %collective-permute-done.8.far_add), custom_call_target="tpu_custom_call" | custom-call | flops 2097152 | bytes 524288 | tf_op jit(solution)/shard_map/pallas_call | solution.py:119
  23.5 0.1 collective-permute-start.9
  23.5 1.2 %collective-permute-done.9 = f32[4,8,128]{2,1,0:T(8,128)S(1)} collective-permute-done((f32[4,8,128]{2,1,0:T(8,128)S(1)}, f32[4,8,128]{2,1,0:T(8,128)S(1)}, u32[]{:S(2)}, u32[]{:S(2)}) %collective-permute-start.9) | collective-permute-done | bytes 16416 | tf_op jit(solution)/shard_map/ppermute | solution.py:145
  24.7 1.2 %collective-permute-start.10 = (f32[2,8,128]{2,1,0:T(8,128)S(1)}, f32[2,8,128]{2,1,0:T(8,128)S(1)}, u32[]{:S(2)}, u32[]{:S(2)}) collective-permute-start(f32[2,8,128]{2,1,0:T(8,128)S(1)} %slice.29), channel_id=1, source_target_pairs={{0,6},{1,7},{2,4},{3,5},{4,2},{5,3},{6,0},{7,1},{8,14},{9,15},{10,... | collective-permute-start | bytes 24584 | tf_op jit(solution)/shard_map/ppermute | solution.py:141
  25.9 1.9 %collective-permute-done.10 = f32[2,8,128]{2,1,0:T(8,128)S(1)} collective-permute-done((f32[2,8,128]{2,1,0:T(8,128)S(1)}, f32[2,8,128]{2,1,0:T(8,128)S(1)}, u32[]{:S(2)}, u32[]{:S(2)}) %collective-permute-start.10) | collective-permute-done | bytes 8224 | tf_op jit(solution)/shard_map/ppermute | solution.py:141
  27.8 2.6 %collective-permute-start.11 = (f32[8,128]{1,0:T(8,128)S(1)}, f32[8,128]{1,0:T(8,128)S(1)}, u32[]{:S(2)}, u32[]{:S(2)}) collective-permute-start(f32[8,128]{1,0:T(8,128)S(1)} %slice_bitcast_fusion), channel_id=1, source_target_pairs={{0,10},{1,11},{2,8},{3,9},{4,14},{5,15},{6,12},{7,13},{8,2},{9,3},... | collective-permute-start | bytes 12296 | tf_op jit(solution)/shard_map/ppermute | solution.py:141
  30.4 1.3 %collective-permute-done.11 = f32[8,128]{1,0:T(8,128)S(1)} collective-permute-done((f32[8,128]{1,0:T(8,128)S(1)}, f32[8,128]{1,0:T(8,128)S(1)}, u32[]{:S(2)}, u32[]{:S(2)}) %collective-permute-start.11) | collective-permute-done | bytes 4128 | tf_op jit(solution)/shard_map/ppermute | solution.py:141
  31.8 0.6 %select_bitcast_fusion = f32[16,4]{0,1:T(4,128)} fusion(f32[8,128]{1,0:T(8,128)S(1)} %fusion, s32[8,128]{1,0:T(8,128)S(1)} %get-tuple-element.25), kind=kLoop, calls=%fused_computation.5 | loop fusion | flops 128 | bytes 1024 | tf_op jit(solution)/shard_map/transpose | solution.py:178
  (10 shorter events, 0.1 us)
Async XLA Ops:
  3.3 1.5 %collective-permute-start.2 = (f32[2,16,8,128]{3,2,1,0:T(8,128)S(1)}, f32[2,16,8,128]{3,2,1,0:T(8,128)S(1)}, u32[]{:S(2)}, u32[]{:S(2)}) collective-permute-start(f32[2,16,8,128]{3,2,1,0:T(8,128)S(1)} %get-tuple-element.21), channel_id=1, source_target_pairs={{0,2},{2,0},{1,3},{3,1},{4,6},{6,4},{5,7},{7,5},{8,10},{10,8},{9,1... | collective-permute-start | bytes 393224 | tf_op jit(solution)/shard_map/ppermute | solution.py:145
  3.8 4.0 %collective-permute-start.4 = (f32[2,16,8,128]{3,2,1,0:T(8,128)S(1)}, f32[2,16,8,128]{3,2,1,0:T(8,128)S(1)}, u32[]{:S(2)}, u32[]{:S(2)}) collective-permute-start(f32[2,16,8,128]{3,2,1,0:T(8,128)S(1)} %get-tuple-element.24), channel_id=1, source_target_pairs={{0,2},{2,0},{1,3},{3,1},{4,6},{6,4},{5,7},{7,5},{8,10},{10,8},{9,1... | collective-permute-start | bytes 393224 | tf_op jit(solution)/shard_map/ppermute | solution.py:145
  3.9 4.1 %collective-permute-start = (f32[2,16,8,128]{3,2,1,0:T(8,128)S(1)}, f32[2,16,8,128]{3,2,1,0:T(8,128)S(1)}, u32[]{:S(2)}, u32[]{:S(2)}) collective-permute-start(f32[2,16,8,128]{3,2,1,0:T(8,128)S(1)} %get-tuple-element.17), channel_id=1, source_target_pairs={{0,2},{2,0},{1,3},{3,1},{4,6},{6,4},{5,7},{7,5},{8,10},{10,8},{9,1... | collective-permute-start | bytes 393224 | tf_op jit(solution)/shard_map/ppermute | solution.py:145
  4.3 3.7 %collective-permute-start.1 = (f32[2,16,8,128]{3,2,1,0:T(8,128)S(1)}, f32[2,16,8,128]{3,2,1,0:T(8,128)S(1)}, u32[]{:S(2)}, u32[]{:S(2)}) collective-permute-start(f32[2,16,8,128]{3,2,1,0:T(8,128)S(1)} %get-tuple-element.19), channel_id=1, source_target_pairs={{0,2},{2,0},{1,3},{3,1},{4,6},{6,4},{5,7},{7,5},{8,10},{10,8},{9,1... | collective-permute-start | bytes 393224 | tf_op jit(solution)/shard_map/ppermute | solution.py:145
  4.8 7.1 %collective-permute-start.3 = (f32[2,16,8,128]{3,2,1,0:T(8,128)S(1)}, f32[2,16,8,128]{3,2,1,0:T(8,128)S(1)}, u32[]{:S(2)}, u32[]{:S(2)}) collective-permute-start(f32[2,16,8,128]{3,2,1,0:T(8,128)S(1)} %add.29), channel_id=1, source_target_pairs={{0,4},{1,5},{2,10},{3,11},{4,0},{5,1},{6,14},{7,15},{8,12},{9,13},... | collective-permute-start | bytes 393224 | tf_op jit(solution)/shard_map/ppermute | solution.py:141
  7.9 8.6 %collective-permute-start.5 = (f32[2,16,8,128]{3,2,1,0:T(8,128)S(1)}, f32[2,16,8,128]{3,2,1,0:T(8,128)S(1)}, u32[]{:S(2)}, u32[]{:S(2)}) collective-permute-start(f32[2,16,8,128]{3,2,1,0:T(8,128)S(1)} %add.31), channel_id=1, source_target_pairs={{0,4},{1,5},{2,10},{3,11},{4,0},{5,1},{6,14},{7,15},{8,12},{9,13},... | collective-permute-start | bytes 393224 | tf_op jit(solution)/shard_map/ppermute | solution.py:141
  11.9 7.0 %collective-permute-start.8 = (f32[2,16,8,128]{3,2,1,0:T(8,128)S(1)}, f32[2,16,8,128]{3,2,1,0:T(8,128)S(1)}, u32[]{:S(2)}, u32[]{:S(2)}) collective-permute-start(f32[2,16,8,128]{3,2,1,0:T(8,128)S(1)} %add_add_fusion), channel_id=1, source_target_pairs={{0,9},{1,8},{2,7},{3,6},{4,13},{5,12},{6,3},{7,2},{8,1},{9,0},{10,... | collective-permute-start | bytes 393224 | tf_op jit(solution)/shard_map/ppermute | solution.py:141
  15.7 7.3 %collective-permute-start.6 = (f32[2,16,8,128]{3,2,1,0:T(8,128)S(1)}, f32[2,16,8,128]{3,2,1,0:T(8,128)S(1)}, u32[]{:S(2)}, u32[]{:S(2)}) collective-permute-start(f32[2,16,8,128]{3,2,1,0:T(8,128)S(1)} %add_add_fusion), channel_id=1, source_target_pairs={{0,8},{1,9},{2,6},{3,7},{4,12},{5,13},{6,2},{7,3},{8,0},{9,1},{10,... | collective-permute-start | bytes 393224 | tf_op jit(solution)/shard_map/ppermute | solution.py:141
  16.5 6.4 %collective-permute-start.7 = (f32[2,16,8,128]{3,2,1,0:T(8,128)S(1)}, f32[2,16,8,128]{3,2,1,0:T(8,128)S(1)}, u32[]{:S(2)}, u32[]{:S(2)}) collective-permute-start(f32[2,16,8,128]{3,2,1,0:T(8,128)S(1)} %add.32.own_ref), channel_id=1, source_target_pairs={{0,1},{1,0},{2,3},{3,2},{4,5},{5,4},{6,7},{7,6},{8,9},{9,8},{10,11... | collective-permute-start | bytes 393224 | tf_op jit(solution)/shard_map/ppermute | solution.py:145
  23.5 1.2 %collective-permute-start.9 = (f32[4,8,128]{2,1,0:T(8,128)S(1)}, f32[4,8,128]{2,1,0:T(8,128)S(1)}, u32[]{:S(2)}, u32[]{:S(2)}) collective-permute-start(f32[4,8,128]{2,1,0:T(8,128)S(1)} %get-tuple-element.26), channel_id=1, source_target_pairs={{0,2},{2,0},{1,3},{3,1},{4,6},{6,4},{5,7},{7,5},{8,10},{10,8},{9,1... | collective-permute-start | bytes 49160 | tf_op jit(solution)/shard_map/ppermute | solution.py:145
  24.7 3.1 %collective-permute-start.10 = (f32[2,8,128]{2,1,0:T(8,128)S(1)}, f32[2,8,128]{2,1,0:T(8,128)S(1)}, u32[]{:S(2)}, u32[]{:S(2)}) collective-permute-start(f32[2,8,128]{2,1,0:T(8,128)S(1)} %slice.29), channel_id=1, source_target_pairs={{0,6},{1,7},{2,4},{3,5},{4,2},{5,3},{6,0},{7,1},{8,14},{9,15},{10,... | collective-permute-start | bytes 24584 | tf_op jit(solution)/shard_map/ppermute | solution.py:141
  27.8 4.0 %collective-permute-start.11 = (f32[8,128]{1,0:T(8,128)S(1)}, f32[8,128]{1,0:T(8,128)S(1)}, u32[]{:S(2)}, u32[]{:S(2)}) collective-permute-start(f32[8,128]{1,0:T(8,128)S(1)} %slice_bitcast_fusion), channel_id=1, source_target_pairs={{0,10},{1,11},{2,8},{3,9},{4,14},{5,15},{6,12},{7,13},{8,2},{9,3},... | collective-permute-start | bytes 12296 | tf_op jit(solution)/shard_map/ppermute | solution.py:141

commit v7 on v6

--- a/solution.py
+++ b/solution.py
@@ -93,17 +93,18 @@
     for g in range(groups):
         total[g, pl.ds(pl.multiple_of(x * size, size), size), :] = (own_ref[g] + own_add[g]).reshape(size, -1)
         total[g, pl.ds(pl.multiple_of((1 - x) * size, size), size), :] = (far_ref[g] + far_add[g]).reshape(size, -1)
-    for g in range(groups):
-        for s in range(tile):
-            rows = total[g, pl.ds(s, 2 * depth, stride=tile), :]
-            own = total[g, pl.ds(x * size + s, depth, stride=tile), :]
-            value = value + lax.dot_general(
-                rows,
-                own,
-                (((1,), (1,)), ((), ())),
-                precision=lax.Precision.HIGHEST,
-                preferred_element_type=jnp.float32,
-            )
+    picks = [(g, s) for g in range(groups) for s in range(tile)]
+    for n in range(0, len(picks), 16):
+        part = picks[n : n + 16]
+        rows = jnp.concatenate([total[g, pl.ds(s, 2 * depth, stride=tile), :] for g, s in part], axis=1)
+        own = jnp.concatenate([total[g, pl.ds(x * size + s, depth, stride=tile), :] for g, s in part], axis=1)
+        value = value + lax.dot_general(
+            rows,
+            own,
+            (((1,), (1,)), ((), ())),
+            precision=lax.Precision.HIGHEST,
+            preferred_element_type=jnp.float32,
+        )
     gram[:, 0:depth] = value * scale
     for slot, hops in enumerate(((), (SECOND,), (FIRST,), (FIRST, SECOND))):
         to_z = z

time: 32.5 us -> 32.4 us (level)
  no operation moved by 1% of the time
where the time goes in v7:
time: 32.4 us; the launch traced here: 32.2 us
  waiting for transfers between devices  14.3 us (44%)
  starting transfers between devices  13.5 us (42%)
  Pallas kernels  3.69 us (11%)
  other arithmetic  0.7 us (2%)
    ppermute x6, waiting for transfers between devices, hop(): return lax.ppermute(value, ('z', 'core', 'col'), pairs)  12.7 us
    ppermute x6, starting transfers between devices, hop(): return lax.ppermute(value, ('z', 'core', 'col'), pairs)  11.5 us
    pallas_call x1, Pallas kernels, project(): pl.pallas_call(functools.partial(project_kernel, chunk, starts), out_shap...  3.31 us
    ppermute x6, starting transfers between devices, swap(): return lax.ppermute(value, axis, [(0, 1), (1, 0)])  1.96 us
    ppermute x6, waiting for transfers between devices, swap(): return lax.ppermute(value, axis, [(0, 1), (1, 0)])  1.58 us
  transfers between devices with their start and end apart: 12, of which 7 were waited for; matrix products, arithmetic and copies ran while one was open for 0% of the time, Pallas kernels for 0%

profile of v7, /device:TPU:0, one launch (start us, length us, event | category | flops | bytes accessed | tf_op | source)
XLA Modules:
  0.0 32.2 jit_solution(5315153250419078851)
XLA Ops:
  0.0 3.3 %shard_map.37 = (f32[2,16,8,128]{3,2,1,0:T(8,128)S(1)}, f32[2,16,8,128]{3,2,1,0:T(8,128)S(1)}, f32[2,16,8,128]{3,2,1,0:T(8,128)S(1)}, f32[2,16,8,128]{3,2,1,0:T(...) custom-call(bf16[16,64,2048]{2,1,0:T(8,128)(2,1)} %slab_ref.1, ...), custom_call_target="tpu_custom_call" | custom-call | flops 570425344 | bytes 5767168 | tf_op jit(solution)/shard_map/pallas_call | solution.py:66
  3.3 0.5 %collective-permute-start.2 = (f32[2,16,8,128]{3,2,1,0:T(8,128)S(1)}, f32[2,16,8,128]{3,2,1,0:T(8,128)S(1)}, u32[]{:S(2)}, u32[]{:S(2)}) collective-permute-start(f32[2,16,8,128]{3,2,1,0:T(8,128)S(1)} %get-tuple-element.21), channel_id=1, source_target_pairs={{0,2},{2,0},{1,3},{3,1},{4,6},{6,4},{5,7},{7,5},{8,10},{10,8},{9,1... | collective-permute-start | bytes 393224 | tf_op jit(solution)/shard_map/ppermute | solution.py:146
  3.8 0.1 collective-permute-start.4
  3.9 0.4 %collective-permute-start = (f32[2,16,8,128]{3,2,1,0:T(8,128)S(1)}, f32[2,16,8,128]{3,2,1,0:T(8,128)S(1)}, u32[]{:S(2)}, u32[]{:S(2)}) collective-permute-start(f32[2,16,8,128]{3,2,1,0:T(8,128)S(1)} %get-tuple-element.17), channel_id=1, source_target_pairs={{0,2},{2,0},{1,3},{3,1},{4,6},{6,4},{5,7},{7,5},{8,10},{10,8},{9,1... | collective-permute-start | bytes 393224 | tf_op jit(solution)/shard_map/ppermute | solution.py:146
  4.3 0.1 collective-permute-start.1
  4.4 0.4 %collective-permute-done.2 = f32[2,16,8,128]{3,2,1,0:T(8,128)S(1)} collective-permute-done((f32[2,16,8,128]{3,2,1,0:T(8,128)S(1)}, f32[2,16,8,128]{3,2,1,0:T(8,128)S(1)}, u32[]{:S(2)}, u32[]{:S(2)}) %collective-permute-start.2) | collective-permute-done | bytes 131104 | tf_op jit(solution)/shard_map/ppermute | solution.py:146
  4.8 3.0 %collective-permute-start.3 = (f32[2,16,8,128]{3,2,1,0:T(8,128)S(1)}, f32[2,16,8,128]{3,2,1,0:T(8,128)S(1)}, u32[]{:S(2)}, u32[]{:S(2)}) collective-permute-start(f32[2,16,8,128]{3,2,1,0:T(8,128)S(1)} %add.29), channel_id=1, source_target_pairs={{0,4},{1,5},{2,10},{3,11},{4,0},{5,1},{6,14},{7,15},{8,12},{9,13},... | collective-permute-start | bytes 393224 | tf_op jit(solution)/shard_map/ppermute | solution.py:142
  7.8 0.0 collective-permute-done.4
  7.9 0.2 collective-permute-start.5
  8.0 0.0 collective-permute-done
  8.0 0.0 collective-permute-done.1
  8.1 3.8 %collective-permute-done.3 = f32[2,16,8,128]{3,2,1,0:T(8,128)S(1)} collective-permute-done((f32[2,16,8,128]{3,2,1,0:T(8,128)S(1)}, f32[2,16,8,128]{3,2,1,0:T(8,128)S(1)}, u32[]{:S(2)}, u32[]{:S(2)}) %collective-permute-start.3) | collective-permute-done | bytes 131104 | tf_op jit(solution)/shard_map/ppermute | solution.py:142
  11.9 3.7 %collective-permute-start.8 = (f32[2,16,8,128]{3,2,1,0:T(8,128)S(1)}, f32[2,16,8,128]{3,2,1,0:T(8,128)S(1)}, u32[]{:S(2)}, u32[]{:S(2)}) collective-permute-start(f32[2,16,8,128]{3,2,1,0:T(8,128)S(1)} %add_add_fusion), channel_id=1, source_target_pairs={{0,9},{1,8},{2,7},{3,6},{4,13},{5,12},{6,3},{7,2},{8,1},{9,0},{10,... | collective-permute-start | bytes 393224 | tf_op jit(solution)/shard_map/ppermute | solution.py:142
  15.7 0.8 %collective-permute-start.6 = (f32[2,16,8,128]{3,2,1,0:T(8,128)S(1)}, f32[2,16,8,128]{3,2,1,0:T(8,128)S(1)}, u32[]{:S(2)}, u32[]{:S(2)}) collective-permute-start(f32[2,16,8,128]{3,2,1,0:T(8,128)S(1)} %add_add_fusion), channel_id=1, source_target_pairs={{0,8},{1,9},{2,6},{3,7},{4,12},{5,13},{6,2},{7,3},{8,0},{9,1},{10,... | collective-permute-start | bytes 393224 | tf_op jit(solution)/shard_map/ppermute | solution.py:142
  16.5 0.0 collective-permute-done.5
  16.5 0.8 %collective-permute-start.7 = (f32[2,16,8,128]{3,2,1,0:T(8,128)S(1)}, f32[2,16,8,128]{3,2,1,0:T(8,128)S(1)}, u32[]{:S(2)}, u32[]{:S(2)}) collective-permute-start(f32[2,16,8,128]{3,2,1,0:T(8,128)S(1)} %add.32.own_ref), channel_id=1, source_target_pairs={{0,1},{1,0},{2,3},{3,2},{4,5},{5,4},{6,7},{7,6},{8,9},{9,8},{10,11... | collective-permute-start | bytes 393224 | tf_op jit(solution)/shard_map/ppermute | solution.py:146
  17.3 1.7 %collective-permute-done.8.far_add = f32[2,16,8,128]{3,2,1,0:T(8,128)S(1)} collective-permute-done((f32[2,16,8,128]{3,2,1,0:T(8,128)S(1)}, f32[2,16,8,128]{3,2,1,0:T(8,128)S(1)}, u32[]{:S(2)}, u32[]{:S(2)}) %collective-permute-start.8) | collective-permute-done | bytes 131104 | tf_op jit(solution)/shard_map/ppermute | solution.py:142
  19.0 4.0 %collective-permute-done.6.own_add = f32[2,16,8,128]{3,2,1,0:T(8,128)S(1)} collective-permute-done((f32[2,16,8,128]{3,2,1,0:T(8,128)S(1)}, f32[2,16,8,128]{3,2,1,0:T(8,128)S(1)}, u32[]{:S(2)}, u32[]{:S(2)}) %collective-permute-start.6) | collective-permute-done | bytes 131104 | tf_op jit(solution)/shard_map/ppermute | solution.py:142
  22.9 0.0 collective-permute-done.7.far_ref
  22.9 0.4 %shard_map.38 = (f32[4,8,128]{2,1,0:T(8,128)S(1)}, s32[8,128]{1,0:T(8,128)S(1)}) custom-call(f32[2,16,8,128]{3,2,1,0:T(8,128)S(1)} %add.32.own_ref, f32[2,16,8,128]{3,2,1,0:T(8,128)S(1)} %collective-permute-done.6.own_add, f32[2,16,8,128]{3,2,1,0:T(8,128)S(1)} %collective-permute-done.7.far_ref, f32[2,16,8,128]{3,2,1,0:T(8,128)S(1)} %collective-permute-done.8.far_add), custom_call_target="tpu_custom_call" | custom-call | flops 2097152 | bytes 524288 | tf_op jit(solution)/shard_map/pallas_call | solution.py:120
  23.3 0.1 collective-permute-start.9
  23.4 1.2 %collective-permute-done.9 = f32[4,8,128]{2,1,0:T(8,128)S(1)} collective-permute-done((f32[4,8,128]{2,1,0:T(8,128)S(1)}, f32[4,8,128]{2,1,0:T(8,128)S(1)}, u32[]{:S(2)}, u32[]{:S(2)}) %collective-permute-start.9) | collective-permute-done | bytes 16416 | tf_op jit(solution)/shard_map/ppermute | solution.py:146
  24.6 1.2 %collective-permute-start.10 = (f32[2,8,128]{2,1,0:T(8,128)S(1)}, f32[2,8,128]{2,1,0:T(8,128)S(1)}, u32[]{:S(2)}, u32[]{:S(2)}) collective-permute-start(f32[2,8,128]{2,1,0:T(8,128)S(1)} %slice.29), channel_id=1, source_target_pairs={{0,6},{1,7},{2,4},{3,5},{4,2},{5,3},{6,0},{7,1},{8,14},{9,15},{10,... | collective-permute-start | bytes 24584 | tf_op jit(solution)/shard_map/ppermute | solution.py:142
  25.8 1.9 %collective-permute-done.10 = f32[2,8,128]{2,1,0:T(8,128)S(1)} collective-permute-done((f32[2,8,128]{2,1,0:T(8,128)S(1)}, f32[2,8,128]{2,1,0:T(8,128)S(1)}, u32[]{:S(2)}, u32[]{:S(2)}) %collective-permute-start.10) | collective-permute-done | bytes 8224 | tf_op jit(solution)/shard_map/ppermute | solution.py:142
  27.7 2.6 %collective-permute-start.11 = (f32[8,128]{1,0:T(8,128)S(1)}, f32[8,128]{1,0:T(8,128)S(1)}, u32[]{:S(2)}, u32[]{:S(2)}) collective-permute-start(f32[8,128]{1,0:T(8,128)S(1)} %slice_bitcast_fusion), channel_id=1, source_target_pairs={{0,10},{1,11},{2,8},{3,9},{4,14},{5,15},{6,12},{7,13},{8,2},{9,3},... | collective-permute-start | bytes 12296 | tf_op jit(solution)/shard_map/ppermute | solution.py:142
  30.3 1.3 %collective-permute-done.11 = f32[8,128]{1,0:T(8,128)S(1)} collective-permute-done((f32[8,128]{1,0:T(8,128)S(1)}, f32[8,128]{1,0:T(8,128)S(1)}, u32[]{:S(2)}, u32[]{:S(2)}) %collective-permute-start.11) | collective-permute-done | bytes 4128 | tf_op jit(solution)/shard_map/ppermute | solution.py:142
  31.7 0.6 %select_bitcast_fusion = f32[16,4]{0,1:T(4,128)} fusion(f32[8,128]{1,0:T(8,128)S(1)} %fusion, s32[8,128]{1,0:T(8,128)S(1)} %get-tuple-element.25), kind=kLoop, calls=%fused_computation.5 | loop fusion | flops 128 | bytes 1024 | tf_op jit(solution)/shard_map/transpose | solution.py:179
  (10 shorter events, 0.1 us)
Async XLA Ops:
  3.3 1.5 %collective-permute-start.2 = (f32[2,16,8,128]{3,2,1,0:T(8,128)S(1)}, f32[2,16,8,128]{3,2,1,0:T(8,128)S(1)}, u32[]{:S(2)}, u32[]{:S(2)}) collective-permute-start(f32[2,16,8,128]{3,2,1,0:T(8,128)S(1)} %get-tuple-element.21), channel_id=1, source_target_pairs={{0,2},{2,0},{1,3},{3,1},{4,6},{6,4},{5,7},{7,5},{8,10},{10,8},{9,1... | collective-permute-start | bytes 393224 | tf_op jit(solution)/shard_map/ppermute | solution.py:146
  3.8 4.0 %collective-permute-start.4 = (f32[2,16,8,128]{3,2,1,0:T(8,128)S(1)}, f32[2,16,8,128]{3,2,1,0:T(8,128)S(1)}, u32[]{:S(2)}, u32[]{:S(2)}) collective-permute-start(f32[2,16,8,128]{3,2,1,0:T(8,128)S(1)} %get-tuple-element.24), channel_id=1, source_target_pairs={{0,2},{2,0},{1,3},{3,1},{4,6},{6,4},{5,7},{7,5},{8,10},{10,8},{9,1... | collective-permute-start | bytes 393224 | tf_op jit(solution)/shard_map/ppermute | solution.py:146
  3.9 4.1 %collective-permute-start = (f32[2,16,8,128]{3,2,1,0:T(8,128)S(1)}, f32[2,16,8,128]{3,2,1,0:T(8,128)S(1)}, u32[]{:S(2)}, u32[]{:S(2)}) collective-permute-start(f32[2,16,8,128]{3,2,1,0:T(8,128)S(1)} %get-tuple-element.17), channel_id=1, source_target_pairs={{0,2},{2,0},{1,3},{3,1},{4,6},{6,4},{5,7},{7,5},{8,10},{10,8},{9,1... | collective-permute-start | bytes 393224 | tf_op jit(solution)/shard_map/ppermute | solution.py:146
  4.3 3.7 %collective-permute-start.1 = (f32[2,16,8,128]{3,2,1,0:T(8,128)S(1)}, f32[2,16,8,128]{3,2,1,0:T(8,128)S(1)}, u32[]{:S(2)}, u32[]{:S(2)}) collective-permute-start(f32[2,16,8,128]{3,2,1,0:T(8,128)S(1)} %get-tuple-element.19), channel_id=1, source_target_pairs={{0,2},{2,0},{1,3},{3,1},{4,6},{6,4},{5,7},{7,5},{8,10},{10,8},{9,1... | collective-permute-start | bytes 393224 | tf_op jit(solution)/shard_map/ppermute | solution.py:146
  4.8 7.1 %collective-permute-start.3 = (f32[2,16,8,128]{3,2,1,0:T(8,128)S(1)}, f32[2,16,8,128]{3,2,1,0:T(8,128)S(1)}, u32[]{:S(2)}, u32[]{:S(2)}) collective-permute-start(f32[2,16,8,128]{3,2,1,0:T(8,128)S(1)} %add.29), channel_id=1, source_target_pairs={{0,4},{1,5},{2,10},{3,11},{4,0},{5,1},{6,14},{7,15},{8,12},{9,13},... | collective-permute-start | bytes 393224 | tf_op jit(solution)/shard_map/ppermute | solution.py:142
  7.9 8.6 %collective-permute-start.5 = (f32[2,16,8,128]{3,2,1,0:T(8,128)S(1)}, f32[2,16,8,128]{3,2,1,0:T(8,128)S(1)}, u32[]{:S(2)}, u32[]{:S(2)}) collective-permute-start(f32[2,16,8,128]{3,2,1,0:T(8,128)S(1)} %add.31), channel_id=1, source_target_pairs={{0,4},{1,5},{2,10},{3,11},{4,0},{5,1},{6,14},{7,15},{8,12},{9,13},... | collective-permute-start | bytes 393224 | tf_op jit(solution)/shard_map/ppermute | solution.py:142
  11.9 7.0 %collective-permute-start.8 = (f32[2,16,8,128]{3,2,1,0:T(8,128)S(1)}, f32[2,16,8,128]{3,2,1,0:T(8,128)S(1)}, u32[]{:S(2)}, u32[]{:S(2)}) collective-permute-start(f32[2,16,8,128]{3,2,1,0:T(8,128)S(1)} %add_add_fusion), channel_id=1, source_target_pairs={{0,9},{1,8},{2,7},{3,6},{4,13},{5,12},{6,3},{7,2},{8,1},{9,0},{10,... | collective-permute-start | bytes 393224 | tf_op jit(solution)/shard_map/ppermute | solution.py:142
  15.7 7.3 %collective-permute-start.6 = (f32[2,16,8,128]{3,2,1,0:T(8,128)S(1)}, f32[2,16,8,128]{3,2,1,0:T(8,128)S(1)}, u32[]{:S(2)}, u32[]{:S(2)}) collective-permute-start(f32[2,16,8,128]{3,2,1,0:T(8,128)S(1)} %add_add_fusion), channel_id=1, source_target_pairs={{0,8},{1,9},{2,6},{3,7},{4,12},{5,13},{6,2},{7,3},{8,0},{9,1},{10,... | collective-permute-start | bytes 393224 | tf_op jit(solution)/shard_map/ppermute | solution.py:142
  16.5 6.4 %collective-permute-start.7 = (f32[2,16,8,128]{3,2,1,0:T(8,128)S(1)}, f32[2,16,8,128]{3,2,1,0:T(8,128)S(1)}, u32[]{:S(2)}, u32[]{:S(2)}) collective-permute-start(f32[2,16,8,128]{3,2,1,0:T(8,128)S(1)} %add.32.own_ref), channel_id=1, source_target_pairs={{0,1},{1,0},{2,3},{3,2},{4,5},{5,4},{6,7},{7,6},{8,9},{9,8},{10,11... | collective-permute-start | bytes 393224 | tf_op jit(solution)/shard_map/ppermute | solution.py:146
  23.3 1.2 %collective-permute-start.9 = (f32[4,8,128]{2,1,0:T(8,128)S(1)}, f32[4,8,128]{2,1,0:T(8,128)S(1)}, u32[]{:S(2)}, u32[]{:S(2)}) collective-permute-start(f32[4,8,128]{2,1,0:T(8,128)S(1)} %get-tuple-element.26), channel_id=1, source_target_pairs={{0,2},{2,0},{1,3},{3,1},{4,6},{6,4},{5,7},{7,5},{8,10},{10,8},{9,1... | collective-permute-start | bytes 49160 | tf_op jit(solution)/shard_map/ppermute | solution.py:146
  24.6 3.1 %collective-permute-start.10 = (f32[2,8,128]{2,1,0:T(8,128)S(1)}, f32[2,8,128]{2,1,0:T(8,128)S(1)}, u32[]{:S(2)}, u32[]{:S(2)}) collective-permute-start(f32[2,8,128]{2,1,0:T(8,128)S(1)} %slice.29), channel_id=1, source_target_pairs={{0,6},{1,7},{2,4},{3,5},{4,2},{5,3},{6,0},{7,1},{8,14},{9,15},{10,... | collective-permute-start | bytes 24584 | tf_op jit(solution)/shard_map/ppermute | solution.py:142
  27.7 4.0 %collective-permute-start.11 = (f32[8,128]{1,0:T(8,128)S(1)}, f32[8,128]{1,0:T(8,128)S(1)}, u32[]{:S(2)}, u32[]{:S(2)}) collective-permute-start(f32[8,128]{1,0:T(8,128)S(1)} %slice_bitcast_fusion), channel_id=1, source_target_pairs={{0,10},{1,11},{2,8},{3,9},{4,14},{5,15},{6,12},{7,13},{8,2},{9,3},... | collective-permute-start | bytes 12296 | tf_op jit(solution)/shard_map/ppermute | solution.py:142

commit v8 on v7

--- a/solution.py
+++ b/solution.py
@@ -84,6 +84,12 @@
     )(*(pltpu.with_memory_space_constraint(a, pltpu.HBM) for a in (slab, factor_one, factor_two)))
 
 
+def halves(value):
+    high = value.astype(jnp.bfloat16)
+    low = (value - high.astype(jnp.float32)).astype(jnp.bfloat16)
+    return jnp.concatenate([high, low], axis=0)
+
+
 def gram_kernel(scale, own_ref, own_add, far_ref, far_add, out_ref, flag_ref, total, gram):
     groups, depth, tile, _ = own_ref.shape
     z, core, x = (lax.axis_index(name) for name in ("z", "core", "col"))
@@ -98,13 +104,11 @@
         part = picks[n : n + 16]
         rows = jnp.concatenate([total[g, pl.ds(s, 2 * depth, stride=tile), :] for g, s in part], axis=1)
         own = jnp.concatenate([total[g, pl.ds(x * size + s, depth, stride=tile), :] for g, s in part], axis=1)
-        value = value + lax.dot_general(
-            rows,
-            own,
-            (((1,), (1,)), ((), ())),
-            precision=lax.Precision.HIGHEST,
-            preferred_element_type=jnp.float32,
+        four = lax.dot_general(
+            halves(rows), halves(own), (((1,), (1,)), ((), ())), preferred_element_type=jnp.float32
         )
+        for at in (0, 2 * depth):
+            value = value + (four[at : at + 2 * depth, 0:depth] + four[at : at + 2 * depth, depth : 2 * depth])
     gram[:, 0:depth] = value * scale
     for slot, hops in enumerate(((), (SECOND,), (FIRST,), (FIRST, SECOND))):
         to_z = z

time: 32.4 us -> 32.3 us (level)
  no operation moved by 1% of the time
where the time goes in v8:
time: 32.3 us; the launch traced here: 32.2 us
  waiting for transfers between devices  14.3 us (44%)
  starting transfers between devices  13.5 us (42%)
  Pallas kernels  3.63 us (11%)
  other arithmetic  0.7 us (2%)
    ppermute x6, waiting for transfers between devices, hop(): return lax.ppermute(value, ('z', 'core', 'col'), pairs)  12.7 us
    ppermute x6, starting transfers between devices, hop(): return lax.ppermute(value, ('z', 'core', 'col'), pairs)  11.5 us
    pallas_call x1, Pallas kernels, project(): pl.pallas_call(functools.partial(project_kernel, chunk, starts), out_shap...  3.31 us
    ppermute x6, starting transfers between devices, swap(): return lax.ppermute(value, axis, [(0, 1), (1, 0)])  1.96 us
    ppermute x6, waiting for transfers between devices, swap(): return lax.ppermute(value, axis, [(0, 1), (1, 0)])  1.58 us
  transfers between devices with their start and end apart: 12, of which 7 were waited for; matrix products, arithmetic and copies ran while one was open for 0% of the time, Pallas kernels for 0%

profile of v8, /device:TPU:0, one launch (start us, length us, event | category | flops | bytes accessed | tf_op | source)
XLA Modules:
  0.0 32.2 jit_solution(2358861471739020674)
XLA Ops:
  0.0 3.3 %shard_map.37 = (f32[2,16,8,128]{3,2,1,0:T(8,128)S(1)}, f32[2,16,8,128]{3,2,1,0:T(8,128)S(1)}, f32[2,16,8,128]{3,2,1,0:T(8,128)S(1)}, f32[2,16,8,128]{3,2,1,0:T(...) custom-call(bf16[16,64,2048]{2,1,0:T(8,128)(2,1)} %slab_ref.1, ...), custom_call_target="tpu_custom_call" | custom-call | flops 570425344 | bytes 5767168 | tf_op jit(solution)/shard_map/pallas_call | solution.py:66
  3.3 0.5 %collective-permute-start.2 = (f32[2,16,8,128]{3,2,1,0:T(8,128)S(1)}, f32[2,16,8,128]{3,2,1,0:T(8,128)S(1)}, u32[]{:S(2)}, u32[]{:S(2)}) collective-permute-start(f32[2,16,8,128]{3,2,1,0:T(8,128)S(1)} %get-tuple-element.21), channel_id=1, source_target_pairs={{0,2},{2,0},{1,3},{3,1},{4,6},{6,4},{5,7},{7,5},{8,10},{10,8},{9,1... | collective-permute-start | bytes 393224 | tf_op jit(solution)/shard_map/ppermute | solution.py:150
  3.8 0.1 collective-permute-start.4
  3.9 0.4 %collective-permute-start = (f32[2,16,8,128]{3,2,1,0:T(8,128)S(1)}, f32[2,16,8,128]{3,2,1,0:T(8,128)S(1)}, u32[]{:S(2)}, u32[]{:S(2)}) collective-permute-start(f32[2,16,8,128]{3,2,1,0:T(8,128)S(1)} %get-tuple-element.17), channel_id=1, source_target_pairs={{0,2},{2,0},{1,3},{3,1},{4,6},{6,4},{5,7},{7,5},{8,10},{10,8},{9,1... | collective-permute-start | bytes 393224 | tf_op jit(solution)/shard_map/ppermute | solution.py:150
  4.3 0.1 collective-permute-start.1
  4.4 0.4 %collective-permute-done.2 = f32[2,16,8,128]{3,2,1,0:T(8,128)S(1)} collective-permute-done((f32[2,16,8,128]{3,2,1,0:T(8,128)S(1)}, f32[2,16,8,128]{3,2,1,0:T(8,128)S(1)}, u32[]{:S(2)}, u32[]{:S(2)}) %collective-permute-start.2) | collective-permute-done | bytes 131104 | tf_op jit(solution)/shard_map/ppermute | solution.py:150
  4.8 3.0 %collective-permute-start.3 = (f32[2,16,8,128]{3,2,1,0:T(8,128)S(1)}, f32[2,16,8,128]{3,2,1,0:T(8,128)S(1)}, u32[]{:S(2)}, u32[]{:S(2)}) collective-permute-start(f32[2,16,8,128]{3,2,1,0:T(8,128)S(1)} %add.29), channel_id=1, source_target_pairs={{0,4},{1,5},{2,10},{3,11},{4,0},{5,1},{6,14},{7,15},{8,12},{9,13},... | collective-permute-start | bytes 393224 | tf_op jit(solution)/shard_map/ppermute | solution.py:146
  7.8 0.0 collective-permute-done.4
  7.9 0.2 collective-permute-start.5
  8.0 0.0 collective-permute-done
  8.0 0.0 collective-permute-done.1
  8.1 3.8 %collective-permute-done.3 = f32[2,16,8,128]{3,2,1,0:T(8,128)S(1)} collective-permute-done((f32[2,16,8,128]{3,2,1,0:T(8,128)S(1)}, f32[2,16,8,128]{3,2,1,0:T(8,128)S(1)}, u32[]{:S(2)}, u32[]{:S(2)}) %collective-permute-start.3) | collective-permute-done | bytes 131104 | tf_op jit(solution)/shard_map/ppermute | solution.py:146
  11.9 3.7 %collective-permute-start.8 = (f32[2,16,8,128]{3,2,1,0:T(8,128)S(1)}, f32[2,16,8,128]{3,2,1,0:T(8,128)S(1)}, u32[]{:S(2)}, u32[]{:S(2)}) collective-permute-start(f32[2,16,8,128]{3,2,1,0:T(8,128)S(1)} %add_add_fusion), channel_id=1, source_target_pairs={{0,9},{1,8},{2,7},{3,6},{4,13},{5,12},{6,3},{7,2},{8,1},{9,0},{10,... | collective-permute-start | bytes 393224 | tf_op jit(solution)/shard_map/ppermute | solution.py:146
  15.7 0.8 %collective-permute-start.6 = (f32[2,16,8,128]{3,2,1,0:T(8,128)S(1)}, f32[2,16,8,128]{3,2,1,0:T(8,128)S(1)}, u32[]{:S(2)}, u32[]{:S(2)}) collective-permute-start(f32[2,16,8,128]{3,2,1,0:T(8,128)S(1)} %add_add_fusion), channel_id=1, source_target_pairs={{0,8},{1,9},{2,6},{3,7},{4,12},{5,13},{6,2},{7,3},{8,0},{9,1},{10,... | collective-permute-start | bytes 393224 | tf_op jit(solution)/shard_map/ppermute | solution.py:146
  16.5 0.0 collective-permute-done.5
  16.5 0.8 %collective-permute-start.7 = (f32[2,16,8,128]{3,2,1,0:T(8,128)S(1)}, f32[2,16,8,128]{3,2,1,0:T(8,128)S(1)}, u32[]{:S(2)}, u32[]{:S(2)}) collective-permute-start(f32[2,16,8,128]{3,2,1,0:T(8,128)S(1)} %add.32.own_ref), channel_id=1, source_target_pairs={{0,1},{1,0},{2,3},{3,2},{4,5},{5,4},{6,7},{7,6},{8,9},{9,8},{10,11... | collective-permute-start | bytes 393224 | tf_op jit(solution)/shard_map/ppermute | solution.py:150
  17.3 1.7 %collective-permute-done.8.far_add = f32[2,16,8,128]{3,2,1,0:T(8,128)S(1)} collective-permute-done((f32[2,16,8,128]{3,2,1,0:T(8,128)S(1)}, f32[2,16,8,128]{3,2,1,0:T(8,128)S(1)}, u32[]{:S(2)}, u32[]{:S(2)}) %collective-permute-start.8) | collective-permute-done | bytes 131104 | tf_op jit(solution)/shard_map/ppermute | solution.py:146
  19.0 4.0 %collective-permute-done.6.own_add = f32[2,16,8,128]{3,2,1,0:T(8,128)S(1)} collective-permute-done((f32[2,16,8,128]{3,2,1,0:T(8,128)S(1)}, f32[2,16,8,128]{3,2,1,0:T(8,128)S(1)}, u32[]{:S(2)}, u32[]{:S(2)}) %collective-permute-start.6) | collective-permute-done | bytes 131104 | tf_op jit(solution)/shard_map/ppermute | solution.py:146
  22.9 0.0 collective-permute-done.7.far_ref
  22.9 0.3 %shard_map.38 = (f32[4,8,128]{2,1,0:T(8,128)S(1)}, s32[8,128]{1,0:T(8,128)S(1)}) custom-call(f32[2,16,8,128]{3,2,1,0:T(8,128)S(1)} %add.32.own_ref, f32[2,16,8,128]{3,2,1,0:T(8,128)S(1)} %collective-permute-done.6.own_add, f32[2,16,8,128]{3,2,1,0:T(8,128)S(1)} %collective-permute-done.7.far_ref, f32[2,16,8,128]{3,2,1,0:T(8,128)S(1)} %collective-permute-done.8.far_add), custom_call_target="tpu_custom_call" | custom-call | flops 2097152 | bytes 524288 | tf_op jit(solution)/shard_map/pallas_call | solution.py:124
  23.3 0.1 collective-permute-start.9
  23.3 1.2 %collective-permute-done.9 = f32[4,8,128]{2,1,0:T(8,128)S(1)} collective-permute-done((f32[4,8,128]{2,1,0:T(8,128)S(1)}, f32[4,8,128]{2,1,0:T(8,128)S(1)}, u32[]{:S(2)}, u32[]{:S(2)}) %collective-permute-start.9) | collective-permute-done | bytes 16416 | tf_op jit(solution)/shard_map/ppermute | solution.py:150
  24.5 1.2 %collective-permute-start.10 = (f32[2,8,128]{2,1,0:T(8,128)S(1)}, f32[2,8,128]{2,1,0:T(8,128)S(1)}, u32[]{:S(2)}, u32[]{:S(2)}) collective-permute-start(f32[2,8,128]{2,1,0:T(8,128)S(1)} %slice.29), channel_id=1, source_target_pairs={{0,6},{1,7},{2,4},{3,5},{4,2},{5,3},{6,0},{7,1},{8,14},{9,15},{10,... | collective-permute-start | bytes 24584 | tf_op jit(solution)/shard_map/ppermute | solution.py:146
  25.7 1.9 %collective-permute-done.10 = f32[2,8,128]{2,1,0:T(8,128)S(1)} collective-permute-done((f32[2,8,128]{2,1,0:T(8,128)S(1)}, f32[2,8,128]{2,1,0:T(8,128)S(1)}, u32[]{:S(2)}, u32[]{:S(2)}) %collective-permute-start.10) | collective-permute-done | bytes 8224 | tf_op jit(solution)/shard_map/ppermute | solution.py:146
  27.6 2.6 %collective-permute-start.11 = (f32[8,128]{1,0:T(8,128)S(1)}, f32[8,128]{1,0:T(8,128)S(1)}, u32[]{:S(2)}, u32[]{:S(2)}) collective-permute-start(f32[8,128]{1,0:T(8,128)S(1)} %slice_bitcast_fusion), channel_id=1, source_target_pairs={{0,10},{1,11},{2,8},{3,9},{4,14},{5,15},{6,12},{7,13},{8,2},{9,3},... | collective-permute-start | bytes 12296 | tf_op jit(solution)/shard_map/ppermute | solution.py:146
  30.3 1.3 %collective-permute-done.11 = f32[8,128]{1,0:T(8,128)S(1)} collective-permute-done((f32[8,128]{1,0:T(8,128)S(1)}, f32[8,128]{1,0:T(8,128)S(1)}, u32[]{:S(2)}, u32[]{:S(2)}) %collective-permute-start.11) | collective-permute-done | bytes 4128 | tf_op jit(solution)/shard_map/ppermute | solution.py:146
  31.6 0.6 %select_bitcast_fusion = f32[16,4]{0,1:T(4,128)} fusion(f32[8,128]{1,0:T(8,128)S(1)} %fusion, s32[8,128]{1,0:T(8,128)S(1)} %get-tuple-element.25), kind=kLoop, calls=%fused_computation.5 | loop fusion | flops 128 | bytes 1024 | tf_op jit(solution)/shard_map/transpose | solution.py:183
  (10 shorter events, 0.1 us)
Async XLA Ops:
  3.3 1.5 %collective-permute-start.2 = (f32[2,16,8,128]{3,2,1,0:T(8,128)S(1)}, f32[2,16,8,128]{3,2,1,0:T(8,128)S(1)}, u32[]{:S(2)}, u32[]{:S(2)}) collective-permute-start(f32[2,16,8,128]{3,2,1,0:T(8,128)S(1)} %get-tuple-element.21), channel_id=1, source_target_pairs={{0,2},{2,0},{1,3},{3,1},{4,6},{6,4},{5,7},{7,5},{8,10},{10,8},{9,1... | collective-permute-start | bytes 393224 | tf_op jit(solution)/shard_map/ppermute | solution.py:150
  3.8 4.0 %collective-permute-start.4 = (f32[2,16,8,128]{3,2,1,0:T(8,128)S(1)}, f32[2,16,8,128]{3,2,1,0:T(8,128)S(1)}, u32[]{:S(2)}, u32[]{:S(2)}) collective-permute-start(f32[2,16,8,128]{3,2,1,0:T(8,128)S(1)} %get-tuple-element.24), channel_id=1, source_target_pairs={{0,2},{2,0},{1,3},{3,1},{4,6},{6,4},{5,7},{7,5},{8,10},{10,8},{9,1... | collective-permute-start | bytes 393224 | tf_op jit(solution)/shard_map/ppermute | solution.py:150
  3.9 4.1 %collective-permute-start = (f32[2,16,8,128]{3,2,1,0:T(8,128)S(1)}, f32[2,16,8,128]{3,2,1,0:T(8,128)S(1)}, u32[]{:S(2)}, u32[]{:S(2)}) collective-permute-start(f32[2,16,8,128]{3,2,1,0:T(8,128)S(1)} %get-tuple-element.17), channel_id=1, source_target_pairs={{0,2},{2,0},{1,3},{3,1},{4,6},{6,4},{5,7},{7,5},{8,10},{10,8},{9,1... | collective-permute-start | bytes 393224 | tf_op jit(solution)/shard_map/ppermute | solution.py:150
  4.3 3.7 %collective-permute-start.1 = (f32[2,16,8,128]{3,2,1,0:T(8,128)S(1)}, f32[2,16,8,128]{3,2,1,0:T(8,128)S(1)}, u32[]{:S(2)}, u32[]{:S(2)}) collective-permute-start(f32[2,16,8,128]{3,2,1,0:T(8,128)S(1)} %get-tuple-element.19), channel_id=1, source_target_pairs={{0,2},{2,0},{1,3},{3,1},{4,6},{6,4},{5,7},{7,5},{8,10},{10,8},{9,1... | collective-permute-start | bytes 393224 | tf_op jit(solution)/shard_map/ppermute | solution.py:150
  4.8 7.1 %collective-permute-start.3 = (f32[2,16,8,128]{3,2,1,0:T(8,128)S(1)}, f32[2,16,8,128]{3,2,1,0:T(8,128)S(1)}, u32[]{:S(2)}, u32[]{:S(2)}) collective-permute-start(f32[2,16,8,128]{3,2,1,0:T(8,128)S(1)} %add.29), channel_id=1, source_target_pairs={{0,4},{1,5},{2,10},{3,11},{4,0},{5,1},{6,14},{7,15},{8,12},{9,13},... | collective-permute-start | bytes 393224 | tf_op jit(solution)/shard_map/ppermute | solution.py:146
  7.9 8.6 %collective-permute-start.5 = (f32[2,16,8,128]{3,2,1,0:T(8,128)S(1)}, f32[2,16,8,128]{3,2,1,0:T(8,128)S(1)}, u32[]{:S(2)}, u32[]{:S(2)}) collective-permute-start(f32[2,16,8,128]{3,2,1,0:T(8,128)S(1)} %add.31), channel_id=1, source_target_pairs={{0,4},{1,5},{2,10},{3,11},{4,0},{5,1},{6,14},{7,15},{8,12},{9,13},... | collective-permute-start | bytes 393224 | tf_op jit(solution)/shard_map/ppermute | solution.py:146
  11.9 7.0 %collective-permute-start.8 = (f32[2,16,8,128]{3,2,1,0:T(8,128)S(1)}, f32[2,16,8,128]{3,2,1,0:T(8,128)S(1)}, u32[]{:S(2)}, u32[]{:S(2)}) collective-permute-start(f32[2,16,8,128]{3,2,1,0:T(8,128)S(1)} %add_add_fusion), channel_id=1, source_target_pairs={{0,9},{1,8},{2,7},{3,6},{4,13},{5,12},{6,3},{7,2},{8,1},{9,0},{10,... | collective-permute-start | bytes 393224 | tf_op jit(solution)/shard_map/ppermute | solution.py:146
  15.7 7.3 %collective-permute-start.6 = (f32[2,16,8,128]{3,2,1,0:T(8,128)S(1)}, f32[2,16,8,128]{3,2,1,0:T(8,128)S(1)}, u32[]{:S(2)}, u32[]{:S(2)}) collective-permute-start(f32[2,16,8,128]{3,2,1,0:T(8,128)S(1)} %add_add_fusion), channel_id=1, source_target_pairs={{0,8},{1,9},{2,6},{3,7},{4,12},{5,13},{6,2},{7,3},{8,0},{9,1},{10,... | collective-permute-start | bytes 393224 | tf_op jit(solution)/shard_map/ppermute | solution.py:146
  16.5 6.4 %collective-permute-start.7 = (f32[2,16,8,128]{3,2,1,0:T(8,128)S(1)}, f32[2,16,8,128]{3,2,1,0:T(8,128)S(1)}, u32[]{:S(2)}, u32[]{:S(2)}) collective-permute-start(f32[2,16,8,128]{3,2,1,0:T(8,128)S(1)} %add.32.own_ref), channel_id=1, source_target_pairs={{0,1},{1,0},{2,3},{3,2},{4,5},{5,4},{6,7},{7,6},{8,9},{9,8},{10,11... | collective-permute-start | bytes 393224 | tf_op jit(solution)/shard_map/ppermute | solution.py:150
  23.3 1.2 %collective-permute-start.9 = (f32[4,8,128]{2,1,0:T(8,128)S(1)}, f32[4,8,128]{2,1,0:T(8,128)S(1)}, u32[]{:S(2)}, u32[]{:S(2)}) collective-permute-start(f32[4,8,128]{2,1,0:T(8,128)S(1)} %get-tuple-element.26), channel_id=1, source_target_pairs={{0,2},{2,0},{1,3},{3,1},{4,6},{6,4},{5,7},{7,5},{8,10},{10,8},{9,1... | collective-permute-start | bytes 49160 | tf_op jit(solution)/shard_map/ppermute | solution.py:150
  24.5 3.1 %collective-permute-start.10 = (f32[2,8,128]{2,1,0:T(8,128)S(1)}, f32[2,8,128]{2,1,0:T(8,128)S(1)}, u32[]{:S(2)}, u32[]{:S(2)}) collective-permute-start(f32[2,8,128]{2,1,0:T(8,128)S(1)} %slice.29), channel_id=1, source_target_pairs={{0,6},{1,7},{2,4},{3,5},{4,2},{5,3},{6,0},{7,1},{8,14},{9,15},{10,... | collective-permute-start | bytes 24584 | tf_op jit(solution)/shard_map/ppermute | solution.py:146
  27.6 4.0 %collective-permute-start.11 = (f32[8,128]{1,0:T(8,128)S(1)}, f32[8,128]{1,0:T(8,128)S(1)}, u32[]{:S(2)}, u32[]{:S(2)}) collective-permute-start(f32[8,128]{1,0:T(8,128)S(1)} %slice_bitcast_fusion), channel_id=1, source_target_pairs={{0,10},{1,11},{2,8},{3,9},{4,14},{5,15},{6,12},{7,13},{8,2},{9,3},... | collective-permute-start | bytes 12296 | tf_op jit(solution)/shard_map/ppermute | solution.py:146

commit v9 on v8

--- a/solution.py
+++ b/solution.py
@@ -176,9 +176,9 @@
     own_add = hop(onward, zs, SECOND_HOP)
     own = lax.optimization_barrier((own, onward))[0] + beside
     blocks, flag = gram_blocks((own, own_add), (swap(own, "col"), far_add), zs, scale)
-    blocks = blocks + swap(blocks, "core")
-    pair = blocks[:2] + hop(blocks[2:], zs, (FIRST, FIRST), cross=1)
-    last = pair[0] + hop(pair[1], zs, (SECOND, SECOND), cross=1)
+    pair = blocks[0::2] + hop(blocks[1::2], zs, (SECOND, SECOND), cross=1)
+    pair = pair + swap(pair, "core")
+    last = pair[0] + hop(pair[1], zs, (FIRST, FIRST), cross=1)
     depth, rows = slab.shape[0], last.shape[0] // CORES
     return jnp.where(flag[:rows, :depth] == 1, last[rows:, :depth], last[:rows, :depth]).T
 

time: 32.3 us -> 32.3 us (level)
  starting transfers between devices: 13.5 us -> 12.1 us
  waiting for transfers between devices: 14.3 us -> 15.7 us
    ppermute x6, waiting for transfers between devices: 12.7 us -> 14.1 us  [hop(): return lax.ppermute(value, ('z', 'core', 'col'), pairs)]
    ppermute x6, starting transfers between devices: 11.5 us -> 10.2 us  [hop(): return lax.ppermute(value, ('z', 'core', 'col'), pairs)]
where the time goes in v9:
time: 32.3 us; the launch traced here: 32.2 us
  waiting for transfers between devices  15.7 us (49%)
  starting transfers between devices  12.1 us (37%)
  Pallas kernels  3.63 us (11%)
  other arithmetic  0.7 us (2%)
    ppermute x6, waiting for transfers between devices, hop(): return lax.ppermute(value, ('z', 'core', 'col'), pairs)  14.1 us
    ppermute x6, starting transfers between devices, hop(): return lax.ppermute(value, ('z', 'core', 'col'), pairs)  10.2 us
    pallas_call x1, Pallas kernels, project(): pl.pallas_call(functools.partial(project_kernel, chunk, starts), out_shap...  3.31 us
    ppermute x6, starting transfers between devices, swap(): return lax.ppermute(value, axis, [(0, 1), (1, 0)])  1.9 us
    ppermute x6, waiting for transfers between devices, swap(): return lax.ppermute(value, axis, [(0, 1), (1, 0)])  1.58 us
  transfers between devices with their start and end apart: 12, of which 7 were waited for; matrix products, arithmetic and copies ran while one was open for 0% of the time, Pallas kernels for 0%

profile of v9, /device:TPU:0, one launch (start us, length us, event | category | flops | bytes accessed | tf_op | source)
XLA Modules:
  0.0 32.2 jit_solution(18349186938810081249)
XLA Ops:
  0.0 3.3 %shard_map.37 = (f32[2,16,8,128]{3,2,1,0:T(8,128)S(1)}, f32[2,16,8,128]{3,2,1,0:T(8,128)S(1)}, f32[2,16,8,128]{3,2,1,0:T(8,128)S(1)}, f32[2,16,8,128]{3,2,1,0:T(...) custom-call(bf16[16,64,2048]{2,1,0:T(8,128)(2,1)} %slab_ref.1, ...), custom_call_target="tpu_custom_call" | custom-call | flops 570425344 | bytes 5767168 | tf_op jit(solution)/shard_map/pallas_call | solution.py:66
  3.3 0.5 %collective-permute-start.2 = (f32[2,16,8,128]{3,2,1,0:T(8,128)S(1)}, f32[2,16,8,128]{3,2,1,0:T(8,128)S(1)}, u32[]{:S(2)}, u32[]{:S(2)}) collective-permute-start(f32[2,16,8,128]{3,2,1,0:T(8,128)S(1)} %get-tuple-element.21), channel_id=1, source_target_pairs={{0,2},{2,0},{1,3},{3,1},{4,6},{6,4},{5,7},{7,5},{8,10},{10,8},{9,1... | collective-permute-start | bytes 393224 | tf_op jit(solution)/shard_map/ppermute | solution.py:150
  3.8 0.1 collective-permute-start.4
  3.9 0.4 %collective-permute-start = (f32[2,16,8,128]{3,2,1,0:T(8,128)S(1)}, f32[2,16,8,128]{3,2,1,0:T(8,128)S(1)}, u32[]{:S(2)}, u32[]{:S(2)}) collective-permute-start(f32[2,16,8,128]{3,2,1,0:T(8,128)S(1)} %get-tuple-element.17), channel_id=1, source_target_pairs={{0,2},{2,0},{1,3},{3,1},{4,6},{6,4},{5,7},{7,5},{8,10},{10,8},{9,1... | collective-permute-start | bytes 393224 | tf_op jit(solution)/shard_map/ppermute | solution.py:150
  4.3 0.1 collective-permute-start.1
  4.4 0.4 %collective-permute-done.2 = f32[2,16,8,128]{3,2,1,0:T(8,128)S(1)} collective-permute-done((f32[2,16,8,128]{3,2,1,0:T(8,128)S(1)}, f32[2,16,8,128]{3,2,1,0:T(8,128)S(1)}, u32[]{:S(2)}, u32[]{:S(2)}) %collective-permute-start.2) | collective-permute-done | bytes 131104 | tf_op jit(solution)/shard_map/ppermute | solution.py:150
  4.8 3.0 %collective-permute-start.3 = (f32[2,16,8,128]{3,2,1,0:T(8,128)S(1)}, f32[2,16,8,128]{3,2,1,0:T(8,128)S(1)}, u32[]{:S(2)}, u32[]{:S(2)}) collective-permute-start(f32[2,16,8,128]{3,2,1,0:T(8,128)S(1)} %add.29), channel_id=1, source_target_pairs={{0,4},{1,5},{2,10},{3,11},{4,0},{5,1},{6,14},{7,15},{8,12},{9,13},... | collective-permute-start | bytes 393224 | tf_op jit(solution)/shard_map/ppermute | solution.py:146
  7.8 0.0 collective-permute-done.4
  7.9 0.2 collective-permute-start.5
  8.0 0.0 collective-permute-done
  8.0 0.0 collective-permute-done.1
  8.1 3.8 %collective-permute-done.3 = f32[2,16,8,128]{3,2,1,0:T(8,128)S(1)} collective-permute-done((f32[2,16,8,128]{3,2,1,0:T(8,128)S(1)}, f32[2,16,8,128]{3,2,1,0:T(8,128)S(1)}, u32[]{:S(2)}, u32[]{:S(2)}) %collective-permute-start.3) | collective-permute-done | bytes 131104 | tf_op jit(solution)/shard_map/ppermute | solution.py:146
  11.9 3.7 %collective-permute-start.8 = (f32[2,16,8,128]{3,2,1,0:T(8,128)S(1)}, f32[2,16,8,128]{3,2,1,0:T(8,128)S(1)}, u32[]{:S(2)}, u32[]{:S(2)}) collective-permute-start(f32[2,16,8,128]{3,2,1,0:T(8,128)S(1)} %add_add_fusion), channel_id=1, source_target_pairs={{0,9},{1,8},{2,7},{3,6},{4,13},{5,12},{6,3},{7,2},{8,1},{9,0},{10,... | collective-permute-start | bytes 393224 | tf_op jit(solution)/shard_map/ppermute | solution.py:146
  15.7 0.8 %collective-permute-start.6 = (f32[2,16,8,128]{3,2,1,0:T(8,128)S(1)}, f32[2,16,8,128]{3,2,1,0:T(8,128)S(1)}, u32[]{:S(2)}, u32[]{:S(2)}) collective-permute-start(f32[2,16,8,128]{3,2,1,0:T(8,128)S(1)} %add_add_fusion), channel_id=1, source_target_pairs={{0,8},{1,9},{2,6},{3,7},{4,12},{5,13},{6,2},{7,3},{8,0},{9,1},{10,... | collective-permute-start | bytes 393224 | tf_op jit(solution)/shard_map/ppermute | solution.py:146
  16.5 0.0 collective-permute-done.5
  16.5 0.8 %collective-permute-start.7 = (f32[2,16,8,128]{3,2,1,0:T(8,128)S(1)}, f32[2,16,8,128]{3,2,1,0:T(8,128)S(1)}, u32[]{:S(2)}, u32[]{:S(2)}) collective-permute-start(f32[2,16,8,128]{3,2,1,0:T(8,128)S(1)} %add.32.own_ref), channel_id=1, source_target_pairs={{0,1},{1,0},{2,3},{3,2},{4,5},{5,4},{6,7},{7,6},{8,9},{9,8},{10,11... | collective-permute-start | bytes 393224 | tf_op jit(solution)/shard_map/ppermute | solution.py:150
  17.3 1.7 %collective-permute-done.8.far_add = f32[2,16,8,128]{3,2,1,0:T(8,128)S(1)} collective-permute-done((f32[2,16,8,128]{3,2,1,0:T(8,128)S(1)}, f32[2,16,8,128]{3,2,1,0:T(8,128)S(1)}, u32[]{:S(2)}, u32[]{:S(2)}) %collective-permute-start.8) | collective-permute-done | bytes 131104 | tf_op jit(solution)/shard_map/ppermute | solution.py:146
  19.0 4.0 %collective-permute-done.6.own_add = f32[2,16,8,128]{3,2,1,0:T(8,128)S(1)} collective-permute-done((f32[2,16,8,128]{3,2,1,0:T(8,128)S(1)}, f32[2,16,8,128]{3,2,1,0:T(8,128)S(1)}, u32[]{:S(2)}, u32[]{:S(2)}) %collective-permute-start.6) | collective-permute-done | bytes 131104 | tf_op jit(solution)/shard_map/ppermute | solution.py:146
  22.9 0.0 collective-permute-done.7.far_ref
  22.9 0.3 %shard_map.38 = (f32[4,8,128]{2,1,0:T(8,128)S(1)}, s32[8,128]{1,0:T(8,128)S(1)}) custom-call(f32[2,16,8,128]{3,2,1,0:T(8,128)S(1)} %add.32.own_ref, f32[2,16,8,128]{3,2,1,0:T(8,128)S(1)} %collective-permute-done.6.own_add, f32[2,16,8,128]{3,2,1,0:T(8,128)S(1)} %collective-permute-done.7.far_ref, f32[2,16,8,128]{3,2,1,0:T(8,128)S(1)} %collective-permute-done.8.far_add), custom_call_target="tpu_custom_call" | custom-call | flops 2097152 | bytes 524288 | tf_op jit(solution)/shard_map/pallas_call | solution.py:124
  23.3 0.7 %collective-permute-start.9 = (f32[2,8,128]{2,1,0:T(8,128)S(1)}, f32[2,8,128]{2,1,0:T(8,128)S(1)}, u32[]{:S(2)}, u32[]{:S(2)}) collective-permute-start(f32[2,8,128]{2,1,0:T(8,128)S(1)} %slice.23), channel_id=1, source_target_pairs={{0,10},{1,11},{2,8},{3,9},{4,14},{5,15},{6,12},{7,13},{8,2},{9,3},... | collective-permute-start | bytes 24584 | tf_op jit(solution)/shard_map/ppermute | solution.py:146
  24.0 3.3 %collective-permute-done.9 = f32[2,8,128]{2,1,0:T(8,128)S(1)} collective-permute-done((f32[2,8,128]{2,1,0:T(8,128)S(1)}, f32[2,8,128]{2,1,0:T(8,128)S(1)}, u32[]{:S(2)}, u32[]{:S(2)}) %collective-permute-start.9) | collective-permute-done | bytes 8224 | tf_op jit(solution)/shard_map/ppermute | solution.py:146
  27.3 0.0 collective-permute-start.10
  27.3 1.2 %collective-permute-done.10 = f32[2,8,128]{2,1,0:T(8,128)S(1)} collective-permute-done((f32[2,8,128]{2,1,0:T(8,128)S(1)}, f32[2,8,128]{2,1,0:T(8,128)S(1)}, u32[]{:S(2)}, u32[]{:S(2)}) %collective-permute-start.10) | collective-permute-done | bytes 8224 | tf_op jit(solution)/shard_map/ppermute | solution.py:150
  28.5 1.7 %collective-permute-start.11 = (f32[8,128]{1,0:T(8,128)S(1)}, f32[8,128]{1,0:T(8,128)S(1)}, u32[]{:S(2)}, u32[]{:S(2)}) collective-permute-start(f32[8,128]{1,0:T(8,128)S(1)} %slice_bitcast_fusion), channel_id=1, source_target_pairs={{0,6},{1,7},{2,4},{3,5},{4,2},{5,3},{6,0},{7,1},{8,14},{9,15},{10,... | collective-permute-start | bytes 12296 | tf_op jit(solution)/shard_map/ppermute | solution.py:146
  30.2 1.3 %collective-permute-done.11 = f32[8,128]{1,0:T(8,128)S(1)} collective-permute-done((f32[8,128]{1,0:T(8,128)S(1)}, f32[8,128]{1,0:T(8,128)S(1)}, u32[]{:S(2)}, u32[]{:S(2)}) %collective-permute-start.11) | collective-permute-done | bytes 4128 | tf_op jit(solution)/shard_map/ppermute | solution.py:146
  31.6 0.6 %select_bitcast_fusion = f32[16,4]{0,1:T(4,128)} fusion(f32[8,128]{1,0:T(8,128)S(1)} %fusion, s32[8,128]{1,0:T(8,128)S(1)} %get-tuple-element.25), kind=kLoop, calls=%fused_computation.5 | loop fusion | flops 128 | bytes 1024 | tf_op jit(solution)/shard_map/transpose | solution.py:183
  (10 shorter events, 0.1 us)
Async XLA Ops:
  3.3 1.5 %collective-permute-start.2 = (f32[2,16,8,128]{3,2,1,0:T(8,128)S(1)}, f32[2,16,8,128]{3,2,1,0:T(8,128)S(1)}, u32[]{:S(2)}, u32[]{:S(2)}) collective-permute-start(f32[2,16,8,128]{3,2,1,0:T(8,128)S(1)} %get-tuple-element.21), channel_id=1, source_target_pairs={{0,2},{2,0},{1,3},{3,1},{4,6},{6,4},{5,7},{7,5},{8,10},{10,8},{9,1... | collective-permute-start | bytes 393224 | tf_op jit(solution)/shard_map/ppermute | solution.py:150
  3.8 4.0 %collective-permute-start.4 = (f32[2,16,8,128]{3,2,1,0:T(8,128)S(1)}, f32[2,16,8,128]{3,2,1,0:T(8,128)S(1)}, u32[]{:S(2)}, u32[]{:S(2)}) collective-permute-start(f32[2,16,8,128]{3,2,1,0:T(8,128)S(1)} %get-tuple-element.24), channel_id=1, source_target_pairs={{0,2},{2,0},{1,3},{3,1},{4,6},{6,4},{5,7},{7,5},{8,10},{10,8},{9,1... | collective-permute-start | bytes 393224 | tf_op jit(solution)/shard_map/ppermute | solution.py:150
  3.9 4.1 %collective-permute-start = (f32[2,16,8,128]{3,2,1,0:T(8,128)S(1)}, f32[2,16,8,128]{3,2,1,0:T(8,128)S(1)}, u32[]{:S(2)}, u32[]{:S(2)}) collective-permute-start(f32[2,16,8,128]{3,2,1,0:T(8,128)S(1)} %get-tuple-element.17), channel_id=1, source_target_pairs={{0,2},{2,0},{1,3},{3,1},{4,6},{6,4},{5,7},{7,5},{8,10},{10,8},{9,1... | collective-permute-start | bytes 393224 | tf_op jit(solution)/shard_map/ppermute | solution.py:150
  4.3 3.7 %collective-permute-start.1 = (f32[2,16,8,128]{3,2,1,0:T(8,128)S(1)}, f32[2,16,8,128]{3,2,1,0:T(8,128)S(1)}, u32[]{:S(2)}, u32[]{:S(2)}) collective-permute-start(f32[2,16,8,128]{3,2,1,0:T(8,128)S(1)} %get-tuple-element.19), channel_id=1, source_target_pairs={{0,2},{2,0},{1,3},{3,1},{4,6},{6,4},{5,7},{7,5},{8,10},{10,8},{9,1... | collective-permute-start | bytes 393224 | tf_op jit(solution)/shard_map/ppermute | solution.py:150
  4.8 7.1 %collective-permute-start.3 = (f32[2,16,8,128]{3,2,1,0:T(8,128)S(1)}, f32[2,16,8,128]{3,2,1,0:T(8,128)S(1)}, u32[]{:S(2)}, u32[]{:S(2)}) collective-permute-start(f32[2,16,8,128]{3,2,1,0:T(8,128)S(1)} %add.29), channel_id=1, source_target_pairs={{0,4},{1,5},{2,10},{3,11},{4,0},{5,1},{6,14},{7,15},{8,12},{9,13},... | collective-permute-start | bytes 393224 | tf_op jit(solution)/shard_map/ppermute | solution.py:146
  7.9 8.6 %collective-permute-start.5 = (f32[2,16,8,128]{3,2,1,0:T(8,128)S(1)}, f32[2,16,8,128]{3,2,1,0:T(8,128)S(1)}, u32[]{:S(2)}, u32[]{:S(2)}) collective-permute-start(f32[2,16,8,128]{3,2,1,0:T(8,128)S(1)} %add.31), channel_id=1, source_target_pairs={{0,4},{1,5},{2,10},{3,11},{4,0},{5,1},{6,14},{7,15},{8,12},{9,13},... | collective-permute-start | bytes 393224 | tf_op jit(solution)/shard_map/ppermute | solution.py:146
  11.9 7.0 %collective-permute-start.8 = (f32[2,16,8,128]{3,2,1,0:T(8,128)S(1)}, f32[2,16,8,128]{3,2,1,0:T(8,128)S(1)}, u32[]{:S(2)}, u32[]{:S(2)}) collective-permute-start(f32[2,16,8,128]{3,2,1,0:T(8,128)S(1)} %add_add_fusion), channel_id=1, source_target_pairs={{0,9},{1,8},{2,7},{3,6},{4,13},{5,12},{6,3},{7,2},{8,1},{9,0},{10,... | collective-permute-start | bytes 393224 | tf_op jit(solution)/shard_map/ppermute | solution.py:146
  15.7 7.3 %collective-permute-start.6 = (f32[2,16,8,128]{3,2,1,0:T(8,128)S(1)}, f32[2,16,8,128]{3,2,1,0:T(8,128)S(1)}, u32[]{:S(2)}, u32[]{:S(2)}) collective-permute-start(f32[2,16,8,128]{3,2,1,0:T(8,128)S(1)} %add_add_fusion), channel_id=1, source_target_pairs={{0,8},{1,9},{2,6},{3,7},{4,12},{5,13},{6,2},{7,3},{8,0},{9,1},{10,... | collective-permute-start | bytes 393224 | tf_op jit(solution)/shard_map/ppermute | solution.py:146
  16.5 6.4 %collective-permute-start.7 = (f32[2,16,8,128]{3,2,1,0:T(8,128)S(1)}, f32[2,16,8,128]{3,2,1,0:T(8,128)S(1)}, u32[]{:S(2)}, u32[]{:S(2)}) collective-permute-start(f32[2,16,8,128]{3,2,1,0:T(8,128)S(1)} %add.32.own_ref), channel_id=1, source_target_pairs={{0,1},{1,0},{2,3},{3,2},{4,5},{5,4},{6,7},{7,6},{8,9},{9,8},{10,11... | collective-permute-start | bytes 393224 | tf_op jit(solution)/shard_map/ppermute | solution.py:150
  23.3 4.0 %collective-permute-start.9 = (f32[2,8,128]{2,1,0:T(8,128)S(1)}, f32[2,8,128]{2,1,0:T(8,128)S(1)}, u32[]{:S(2)}, u32[]{:S(2)}) collective-permute-start(f32[2,8,128]{2,1,0:T(8,128)S(1)} %slice.23), channel_id=1, source_target_pairs={{0,10},{1,11},{2,8},{3,9},{4,14},{5,15},{6,12},{7,13},{8,2},{9,3},... | collective-permute-start | bytes 24584 | tf_op jit(solution)/shard_map/ppermute | solution.py:146
  27.3 1.2 %collective-permute-start.10 = (f32[2,8,128]{2,1,0:T(8,128)S(1)}, f32[2,8,128]{2,1,0:T(8,128)S(1)}, u32[]{:S(2)}, u32[]{:S(2)}) collective-permute-start(f32[2,8,128]{2,1,0:T(8,128)S(1)} %slice_add_fusion), channel_id=1, source_target_pairs={{0,2},{2,0},{1,3},{3,1},{4,6},{6,4},{5,7},{7,5},{8,10},{10,8},{9,1... | collective-permute-start | bytes 24584 | tf_op jit(solution)/shard_map/ppermute | solution.py:150
  28.5 3.1 %collective-permute-start.11 = (f32[8,128]{1,0:T(8,128)S(1)}, f32[8,128]{1,0:T(8,128)S(1)}, u32[]{:S(2)}, u32[]{:S(2)}) collective-permute-start(f32[8,128]{1,0:T(8,128)S(1)} %slice_bitcast_fusion), channel_id=1, source_target_pairs={{0,6},{1,7},{2,4},{3,5},{4,2},{5,3},{6,0},{7,1},{8,14},{9,15},{10,... | collective-permute-start | bytes 12296 | tf_op jit(solution)/shard_map/ppermute | solution.py:146

commit v10 on v9

--- a/solution.py
+++ b/solution.py
@@ -84,37 +84,33 @@
     )(*(pltpu.with_memory_space_constraint(a, pltpu.HBM) for a in (slab, factor_one, factor_two)))
 
 
-def halves(value):
-    high = value.astype(jnp.bfloat16)
-    low = (value - high.astype(jnp.float32)).astype(jnp.bfloat16)
-    return jnp.concatenate([high, low], axis=0)
-
-
-def gram_kernel(scale, own_ref, own_add, far_ref, far_add, out_ref, flag_ref, total, gram):
+def gram_kernel(scale, own_ref, own_add, far_ref, far_add, out_ref, flag_ref, total):
     groups, depth, tile, _ = own_ref.shape
     z, core, x = (lax.axis_index(name) for name in ("z", "core", "col"))
     chips, share, _ = out_ref.shape
     size = depth * tile
-    value = jnp.zeros((2 * depth, depth), jnp.float32)
     for g in range(groups):
-        total[g, pl.ds(pl.multiple_of(x * size, size), size), :] = (own_ref[g] + own_add[g]).reshape(size, -1)
-        total[g, pl.ds(pl.multiple_of((1 - x) * size, size), size), :] = (far_ref[g] + far_add[g]).reshape(size, -1)
-    picks = [(g, s) for g in range(groups) for s in range(tile)]
-    for n in range(0, len(picks), 16):
-        part = picks[n : n + 16]
-        rows = jnp.concatenate([total[g, pl.ds(s, 2 * depth, stride=tile), :] for g, s in part], axis=1)
-        own = jnp.concatenate([total[g, pl.ds(x * size + s, depth, stride=tile), :] for g, s in part], axis=1)
-        four = lax.dot_general(
-            halves(rows), halves(own), (((1,), (1,)), ((), ())), preferred_element_type=jnp.float32
-        )
-        for at in (0, 2 * depth):
-            value = value + (four[at : at + 2 * depth, 0:depth] + four[at : at + 2 * depth, depth : 2 * depth])
-    gram[:, 0:depth] = value * scale
-    for slot, hops in enumerate(((), (SECOND,), (FIRST,), (FIRST, SECOND))):
-        to_z = z
-        for hop in hops:
-            to_z = jnp.bitwise_xor(to_z, hop)
-        out_ref[slot] = gram[pl.ds(pl.multiple_of(to_z * share, TILE), share), :]
+        total[g, 0:size, :] = (own_ref[g] + own_add[g]).reshape(size, -1)
+        total[g, size : 2 * size, :] = (far_ref[g] + far_add[g]).reshape(size, -1)
+    picks = [total[g, pl.ds(s, 2 * depth, stride=tile), :] for g in range(groups) for s in range(tile)]
+    rows = jnp.concatenate(picks, axis=1)
+    high = rows.astype(jnp.bfloat16)
+    low = (rows - high.astype(jnp.float32)).astype(jnp.bfloat16)
+    four = lax.dot_general(
+        jnp.concatenate([high, low], axis=0),
+        jnp.concatenate([high[0:depth], low[0:depth]], axis=0),
+        (((1,), (1,)), ((), ())),
+        preferred_element_type=jnp.float32,
+    )
+    value = (four[0 : 2 * depth, 0:depth] + four[0 : 2 * depth, depth : 2 * depth]) + (
+        four[2 * depth : 4 * depth, 0:depth] + four[2 * depth : 4 * depth, depth : 2 * depth]
+    )
+    value = value * scale
+    for n in range(chips):
+        half, part = n // 2, n % 2
+        mask = jnp.bitwise_xor(z, 2 * (x if half == 0 else 1 - x) + part)
+        slot = mask // SECOND + 2 * (mask % SECOND)
+        out_ref[slot, :, 0:depth] = value[n * share : (n + 1) * share]
     flag_ref[...] = jnp.full(flag_ref.shape, core, jnp.int32)
 
 
@@ -128,7 +124,6 @@
         out_specs=[pl.BlockSpec(memory_space=pltpu.VMEM)] * 2,
         scratch_shapes=[
             pltpu.VMEM((groups, full * tile, r1), jnp.float32),
-            pltpu.VMEM((full, 128), jnp.float32),
         ],
         cost_estimate=pl.CostEstimate(
             flops=2 * groups * full * depth * tile * r1, bytes_accessed=16 * own[0].size, transcendentals=0
@@ -172,8 +167,8 @@
     arrived = hop(passed, zs, FIRST_HOP)
     beside = hop(given, zs, FIRST_HOP)
     onward = across + arrived
+    own_add = hop(onward, zs, SECOND_HOP)
     far_add = hop(onward, zs, SECOND_HOP, flip=1)
-    own_add = hop(onward, zs, SECOND_HOP)
     own = lax.optimization_barrier((own, onward))[0] + beside
     blocks, flag = gram_blocks((own, own_add), (swap(own, "col"), far_add), zs, scale)
     pair = blocks[0::2] + hop(blocks[1::2], zs, (SECOND, SECOND), cross=1)

time: 32.3 us -> 32.3 us (level)
  no operation moved by 1% of the time
where the time goes in v10:
time: 32.3 us; the launch traced here: 32.1 us
  waiting for transfers between devices  15.7 us (49%)
  starting transfers between devices  12.1 us (37%)
  Pallas kernels  3.62 us (11%)
  other arithmetic  0.7 us (2%)
    ppermute x6, waiting for transfers between devices, hop(): return lax.ppermute(value, ('z', 'core', 'col'), pairs)  14.1 us
    ppermute x6, starting transfers between devices, hop(): return lax.ppermute(value, ('z', 'core', 'col'), pairs)  10.2 us
    pallas_call x1, Pallas kernels, project(): pl.pallas_call(functools.partial(project_kernel, chunk, starts), out_shap...  3.31 us
    ppermute x6, starting transfers between devices, swap(): return lax.ppermute(value, axis, [(0, 1), (1, 0)])  1.9 us
    ppermute x6, waiting for transfers between devices, swap(): return lax.ppermute(value, axis, [(0, 1), (1, 0)])  1.58 us
  transfers between devices with their start and end apart: 12, of which 7 were waited for; matrix products, arithmetic and copies ran while one was open for 0% of the time, Pallas kernels for 0%

profile of v10, /device:TPU:0, one launch (start us, length us, event | category | flops | bytes accessed | tf_op | source)
XLA Modules:
  0.0 32.1 jit_solution(7971817590057887800)
XLA Ops:
  0.0 3.3 %shard_map.37 = (f32[2,16,8,128]{3,2,1,0:T(8,128)S(1)}, f32[2,16,8,128]{3,2,1,0:T(8,128)S(1)}, f32[2,16,8,128]{3,2,1,0:T(8,128)S(1)}, f32[2,16,8,128]{3,2,1,0:T(...) custom-call(bf16[16,64,2048]{2,1,0:T(8,128)(2,1)} %slab_ref.1, ...), custom_call_target="tpu_custom_call" | custom-call | flops 570425344 | bytes 5767168 | tf_op jit(solution)/shard_map/pallas_call | solution.py:66
  3.3 0.5 %collective-permute-start.2 = (f32[2,16,8,128]{3,2,1,0:T(8,128)S(1)}, f32[2,16,8,128]{3,2,1,0:T(8,128)S(1)}, u32[]{:S(2)}, u32[]{:S(2)}) collective-permute-start(f32[2,16,8,128]{3,2,1,0:T(8,128)S(1)} %get-tuple-element.21), channel_id=1, source_target_pairs={{0,2},{2,0},{1,3},{3,1},{4,6},{6,4},{5,7},{7,5},{8,10},{10,8},{9,1... | collective-permute-start | bytes 393224 | tf_op jit(solution)/shard_map/ppermute | solution.py:145
  3.8 0.1 collective-permute-start.4
  3.9 0.4 %collective-permute-start = (f32[2,16,8,128]{3,2,1,0:T(8,128)S(1)}, f32[2,16,8,128]{3,2,1,0:T(8,128)S(1)}, u32[]{:S(2)}, u32[]{:S(2)}) collective-permute-start(f32[2,16,8,128]{3,2,1,0:T(8,128)S(1)} %get-tuple-element.17), channel_id=1, source_target_pairs={{0,2},{2,0},{1,3},{3,1},{4,6},{6,4},{5,7},{7,5},{8,10},{10,8},{9,1... | collective-permute-start | bytes 393224 | tf_op jit(solution)/shard_map/ppermute | solution.py:145
  4.3 0.1 collective-permute-start.1
  4.4 0.4 %collective-permute-done.2 = f32[2,16,8,128]{3,2,1,0:T(8,128)S(1)} collective-permute-done((f32[2,16,8,128]{3,2,1,0:T(8,128)S(1)}, f32[2,16,8,128]{3,2,1,0:T(8,128)S(1)}, u32[]{:S(2)}, u32[]{:S(2)}) %collective-permute-start.2) | collective-permute-done | bytes 131104 | tf_op jit(solution)/shard_map/ppermute | solution.py:145
  4.8 3.0 %collective-permute-start.3 = (f32[2,16,8,128]{3,2,1,0:T(8,128)S(1)}, f32[2,16,8,128]{3,2,1,0:T(8,128)S(1)}, u32[]{:S(2)}, u32[]{:S(2)}) collective-permute-start(f32[2,16,8,128]{3,2,1,0:T(8,128)S(1)} %add.29), channel_id=1, source_target_pairs={{0,4},{1,5},{2,10},{3,11},{4,0},{5,1},{6,14},{7,15},{8,12},{9,13},... | collective-permute-start | bytes 393224 | tf_op jit(solution)/shard_map/ppermute | solution.py:141
  7.8 0.0 collective-permute-done.4
  7.9 0.2 collective-permute-start.5
  8.0 0.0 collective-permute-done
  8.0 0.0 collective-permute-done.1
  8.1 3.8 %collective-permute-done.3 = f32[2,16,8,128]{3,2,1,0:T(8,128)S(1)} collective-permute-done((f32[2,16,8,128]{3,2,1,0:T(8,128)S(1)}, f32[2,16,8,128]{3,2,1,0:T(8,128)S(1)}, u32[]{:S(2)}, u32[]{:S(2)}) %collective-permute-start.3) | collective-permute-done | bytes 131104 | tf_op jit(solution)/shard_map/ppermute | solution.py:141
  11.9 3.7 %collective-permute-start.8 = (f32[2,16,8,128]{3,2,1,0:T(8,128)S(1)}, f32[2,16,8,128]{3,2,1,0:T(8,128)S(1)}, u32[]{:S(2)}, u32[]{:S(2)}) collective-permute-start(f32[2,16,8,128]{3,2,1,0:T(8,128)S(1)} %add_add_fusion), channel_id=1, source_target_pairs={{0,9},{1,8},{2,7},{3,6},{4,13},{5,12},{6,3},{7,2},{8,1},{9,0},{10,... | collective-permute-start | bytes 393224 | tf_op jit(solution)/shard_map/ppermute | solution.py:141
  15.7 0.8 %collective-permute-start.6 = (f32[2,16,8,128]{3,2,1,0:T(8,128)S(1)}, f32[2,16,8,128]{3,2,1,0:T(8,128)S(1)}, u32[]{:S(2)}, u32[]{:S(2)}) collective-permute-start(f32[2,16,8,128]{3,2,1,0:T(8,128)S(1)} %add_add_fusion), channel_id=1, source_target_pairs={{0,8},{1,9},{2,6},{3,7},{4,12},{5,13},{6,2},{7,3},{8,0},{9,1},{10,... | collective-permute-start | bytes 393224 | tf_op jit(solution)/shard_map/ppermute | solution.py:141
  16.5 0.0 collective-permute-done.5
  16.5 0.8 %collective-permute-start.7 = (f32[2,16,8,128]{3,2,1,0:T(8,128)S(1)}, f32[2,16,8,128]{3,2,1,0:T(8,128)S(1)}, u32[]{:S(2)}, u32[]{:S(2)}) collective-permute-start(f32[2,16,8,128]{3,2,1,0:T(8,128)S(1)} %add.32.own_ref), channel_id=1, source_target_pairs={{0,1},{1,0},{2,3},{3,2},{4,5},{5,4},{6,7},{7,6},{8,9},{9,8},{10,11... | collective-permute-start | bytes 393224 | tf_op jit(solution)/shard_map/ppermute | solution.py:145
  17.3 1.7 %collective-permute-done.8.far_add = f32[2,16,8,128]{3,2,1,0:T(8,128)S(1)} collective-permute-done((f32[2,16,8,128]{3,2,1,0:T(8,128)S(1)}, f32[2,16,8,128]{3,2,1,0:T(8,128)S(1)}, u32[]{:S(2)}, u32[]{:S(2)}) %collective-permute-start.8) | collective-permute-done | bytes 131104 | tf_op jit(solution)/shard_map/ppermute | solution.py:141
  19.0 4.0 %collective-permute-done.6.own_add = f32[2,16,8,128]{3,2,1,0:T(8,128)S(1)} collective-permute-done((f32[2,16,8,128]{3,2,1,0:T(8,128)S(1)}, f32[2,16,8,128]{3,2,1,0:T(8,128)S(1)}, u32[]{:S(2)}, u32[]{:S(2)}) %collective-permute-start.6) | collective-permute-done | bytes 131104 | tf_op jit(solution)/shard_map/ppermute | solution.py:141
  22.9 0.0 collective-permute-done.7.far_ref
  22.9 0.3 shard_map.38
  23.3 0.7 %collective-permute-start.9 = (f32[2,8,128]{2,1,0:T(8,128)S(1)}, f32[2,8,128]{2,1,0:T(8,128)S(1)}, u32[]{:S(2)}, u32[]{:S(2)}) collective-permute-start(f32[2,8,128]{2,1,0:T(8,128)S(1)} %slice.23), channel_id=1, source_target_pairs={{0,10},{1,11},{2,8},{3,9},{4,14},{5,15},{6,12},{7,13},{8,2},{9,3},... | collective-permute-start | bytes 24584 | tf_op jit(solution)/shard_map/ppermute | solution.py:141
  24.0 3.3 %collective-permute-done.9 = f32[2,8,128]{2,1,0:T(8,128)S(1)} collective-permute-done((f32[2,8,128]{2,1,0:T(8,128)S(1)}, f32[2,8,128]{2,1,0:T(8,128)S(1)}, u32[]{:S(2)}, u32[]{:S(2)}) %collective-permute-start.9) | collective-permute-done | bytes 8224 | tf_op jit(solution)/shard_map/ppermute | solution.py:141
  27.3 0.0 collective-permute-start.10
  27.3 1.2 %collective-permute-done.10 = f32[2,8,128]{2,1,0:T(8,128)S(1)} collective-permute-done((f32[2,8,128]{2,1,0:T(8,128)S(1)}, f32[2,8,128]{2,1,0:T(8,128)S(1)}, u32[]{:S(2)}, u32[]{:S(2)}) %collective-permute-start.10) | collective-permute-done | bytes 8224 | tf_op jit(solution)/shard_map/ppermute | solution.py:145
  28.5 1.7 %collective-permute-start.11 = (f32[8,128]{1,0:T(8,128)S(1)}, f32[8,128]{1,0:T(8,128)S(1)}, u32[]{:S(2)}, u32[]{:S(2)}) collective-permute-start(f32[8,128]{1,0:T(8,128)S(1)} %slice_bitcast_fusion), channel_id=1, source_target_pairs={{0,6},{1,7},{2,4},{3,5},{4,2},{5,3},{6,0},{7,1},{8,14},{9,15},{10,... | collective-permute-start | bytes 12296 | tf_op jit(solution)/shard_map/ppermute | solution.py:141
  30.2 1.3 %collective-permute-done.11 = f32[8,128]{1,0:T(8,128)S(1)} collective-permute-done((f32[8,128]{1,0:T(8,128)S(1)}, f32[8,128]{1,0:T(8,128)S(1)}, u32[]{:S(2)}, u32[]{:S(2)}) %collective-permute-start.11) | collective-permute-done | bytes 4128 | tf_op jit(solution)/shard_map/ppermute | solution.py:141
  31.6 0.6 %select_bitcast_fusion = f32[16,4]{0,1:T(4,128)} fusion(f32[8,128]{1,0:T(8,128)S(1)} %fusion, s32[8,128]{1,0:T(8,128)S(1)} %get-tuple-element.25), kind=kLoop, calls=%fused_computation.5 | loop fusion | flops 128 | bytes 1024 | tf_op jit(solution)/shard_map/transpose | solution.py:178
  (10 shorter events, 0.1 us)
Async XLA Ops:
  3.3 1.5 %collective-permute-start.2 = (f32[2,16,8,128]{3,2,1,0:T(8,128)S(1)}, f32[2,16,8,128]{3,2,1,0:T(8,128)S(1)}, u32[]{:S(2)}, u32[]{:S(2)}) collective-permute-start(f32[2,16,8,128]{3,2,1,0:T(8,128)S(1)} %get-tuple-element.21), channel_id=1, source_target_pairs={{0,2},{2,0},{1,3},{3,1},{4,6},{6,4},{5,7},{7,5},{8,10},{10,8},{9,1... | collective-permute-start | bytes 393224 | tf_op jit(solution)/shard_map/ppermute | solution.py:145
  3.8 4.0 %collective-permute-start.4 = (f32[2,16,8,128]{3,2,1,0:T(8,128)S(1)}, f32[2,16,8,128]{3,2,1,0:T(8,128)S(1)}, u32[]{:S(2)}, u32[]{:S(2)}) collective-permute-start(f32[2,16,8,128]{3,2,1,0:T(8,128)S(1)} %get-tuple-element.24), channel_id=1, source_target_pairs={{0,2},{2,0},{1,3},{3,1},{4,6},{6,4},{5,7},{7,5},{8,10},{10,8},{9,1... | collective-permute-start | bytes 393224 | tf_op jit(solution)/shard_map/ppermute | solution.py:145
  3.9 4.1 %collective-permute-start = (f32[2,16,8,128]{3,2,1,0:T(8,128)S(1)}, f32[2,16,8,128]{3,2,1,0:T(8,128)S(1)}, u32[]{:S(2)}, u32[]{:S(2)}) collective-permute-start(f32[2,16,8,128]{3,2,1,0:T(8,128)S(1)} %get-tuple-element.17), channel_id=1, source_target_pairs={{0,2},{2,0},{1,3},{3,1},{4,6},{6,4},{5,7},{7,5},{8,10},{10,8},{9,1... | collective-permute-start | bytes 393224 | tf_op jit(solution)/shard_map/ppermute | solution.py:145
  4.3 3.7 %collective-permute-start.1 = (f32[2,16,8,128]{3,2,1,0:T(8,128)S(1)}, f32[2,16,8,128]{3,2,1,0:T(8,128)S(1)}, u32[]{:S(2)}, u32[]{:S(2)}) collective-permute-start(f32[2,16,8,128]{3,2,1,0:T(8,128)S(1)} %get-tuple-element.19), channel_id=1, source_target_pairs={{0,2},{2,0},{1,3},{3,1},{4,6},{6,4},{5,7},{7,5},{8,10},{10,8},{9,1... | collective-permute-start | bytes 393224 | tf_op jit(solution)/shard_map/ppermute | solution.py:145
  4.8 7.1 %collective-permute-start.3 = (f32[2,16,8,128]{3,2,1,0:T(8,128)S(1)}, f32[2,16,8,128]{3,2,1,0:T(8,128)S(1)}, u32[]{:S(2)}, u32[]{:S(2)}) collective-permute-start(f32[2,16,8,128]{3,2,1,0:T(8,128)S(1)} %add.29), channel_id=1, source_target_pairs={{0,4},{1,5},{2,10},{3,11},{4,0},{5,1},{6,14},{7,15},{8,12},{9,13},... | collective-permute-start | bytes 393224 | tf_op jit(solution)/shard_map/ppermute | solution.py:141
  7.9 8.6 %collective-permute-start.5 = (f32[2,16,8,128]{3,2,1,0:T(8,128)S(1)}, f32[2,16,8,128]{3,2,1,0:T(8,128)S(1)}, u32[]{:S(2)}, u32[]{:S(2)}) collective-permute-start(f32[2,16,8,128]{3,2,1,0:T(8,128)S(1)} %add.31), channel_id=1, source_target_pairs={{0,4},{1,5},{2,10},{3,11},{4,0},{5,1},{6,14},{7,15},{8,12},{9,13},... | collective-permute-start | bytes 393224 | tf_op jit(solution)/shard_map/ppermute | solution.py:141
  11.9 7.0 %collective-permute-start.8 = (f32[2,16,8,128]{3,2,1,0:T(8,128)S(1)}, f32[2,16,8,128]{3,2,1,0:T(8,128)S(1)}, u32[]{:S(2)}, u32[]{:S(2)}) collective-permute-start(f32[2,16,8,128]{3,2,1,0:T(8,128)S(1)} %add_add_fusion), channel_id=1, source_target_pairs={{0,9},{1,8},{2,7},{3,6},{4,13},{5,12},{6,3},{7,2},{8,1},{9,0},{10,... | collective-permute-start | bytes 393224 | tf_op jit(solution)/shard_map/ppermute | solution.py:141
  15.7 7.3 %collective-permute-start.6 = (f32[2,16,8,128]{3,2,1,0:T(8,128)S(1)}, f32[2,16,8,128]{3,2,1,0:T(8,128)S(1)}, u32[]{:S(2)}, u32[]{:S(2)}) collective-permute-start(f32[2,16,8,128]{3,2,1,0:T(8,128)S(1)} %add_add_fusion), channel_id=1, source_target_pairs={{0,8},{1,9},{2,6},{3,7},{4,12},{5,13},{6,2},{7,3},{8,0},{9,1},{10,... | collective-permute-start | bytes 393224 | tf_op jit(solution)/shard_map/ppermute | solution.py:141
  16.5 6.4 %collective-permute-start.7 = (f32[2,16,8,128]{3,2,1,0:T(8,128)S(1)}, f32[2,16,8,128]{3,2,1,0:T(8,128)S(1)}, u32[]{:S(2)}, u32[]{:S(2)}) collective-permute-start(f32[2,16,8,128]{3,2,1,0:T(8,128)S(1)} %add.32.own_ref), channel_id=1, source_target_pairs={{0,1},{1,0},{2,3},{3,2},{4,5},{5,4},{6,7},{7,6},{8,9},{9,8},{10,11... | collective-permute-start | bytes 393224 | tf_op jit(solution)/shard_map/ppermute | solution.py:145
  23.3 4.0 %collective-permute-start.9 = (f32[2,8,128]{2,1,0:T(8,128)S(1)}, f32[2,8,128]{2,1,0:T(8,128)S(1)}, u32[]{:S(2)}, u32[]{:S(2)}) collective-permute-start(f32[2,8,128]{2,1,0:T(8,128)S(1)} %slice.23), channel_id=1, source_target_pairs={{0,10},{1,11},{2,8},{3,9},{4,14},{5,15},{6,12},{7,13},{8,2},{9,3},... | collective-permute-start | bytes 24584 | tf_op jit(solution)/shard_map/ppermute | solution.py:141
  27.3 1.2 %collective-permute-start.10 = (f32[2,8,128]{2,1,0:T(8,128)S(1)}, f32[2,8,128]{2,1,0:T(8,128)S(1)}, u32[]{:S(2)}, u32[]{:S(2)}) collective-permute-start(f32[2,8,128]{2,1,0:T(8,128)S(1)} %slice_add_fusion), channel_id=1, source_target_pairs={{0,2},{2,0},{1,3},{3,1},{4,6},{6,4},{5,7},{7,5},{8,10},{10,8},{9,1... | collective-permute-start | bytes 24584 | tf_op jit(solution)/shard_map/ppermute | solution.py:145
  28.5 3.1 %collective-permute-start.11 = (f32[8,128]{1,0:T(8,128)S(1)}, f32[8,128]{1,0:T(8,128)S(1)}, u32[]{:S(2)}, u32[]{:S(2)}) collective-permute-start(f32[8,128]{1,0:T(8,128)S(1)} %slice_bitcast_fusion), channel_id=1, source_target_pairs={{0,6},{1,7},{2,4},{3,5},{4,2},{5,3},{6,0},{7,1},{8,14},{9,15},{10,... | collective-permute-start | bytes 12296 | tf_op jit(solution)/shard_map/ppermute | solution.py:141

commit v11 on v8

--- a/solution.py
+++ b/solution.py
@@ -18,6 +18,7 @@
 def project_kernel(chunk, starts, slab_ref, one_ref, two_ref, *rest):
     outs, (slab_buf, one_buf, two_buf, turned, sems) = rest[:-5], rest[-5:]
     depth, width, _ = slab_ref.shape
+    r1 = one_ref.shape[1]
     chunks = depth // chunk
     copies = []
     for c in range(chunks):
@@ -37,11 +38,13 @@
     share = two.shape[0] // len(outs)
 
     def second(c, first):
-        for q in range(chunk):
-            core_part = jnp.dot(two, first[q * width : (q + 1) * width], preferred_element_type=jnp.float32)
+        for q in range(0, chunk, 2):
+            pieces = [first[k * width : (k + 1) * width] for k in range(q, q + 2)]
+            wide = jnp.dot(two, jnp.concatenate(pieces, axis=1), preferred_element_type=jnp.float32)
             for o, out in enumerate(outs):
-                piece = core_part[o * share : (o + 1) * share]
-                out[:, c * chunk + q] = piece.reshape(share // TILE, TILE, -1)
+                for k in range(2):
+                    piece = wide[o * share : (o + 1) * share, k * r1 : (k + 1) * r1]
+                    out[:, c * chunk + q + k] = piece.reshape(share // TILE, TILE, -1)
 
     one_copy.wait()
     late = None

time: 32.3 us -> 32.3 us (level)
  no operation moved by 1% of the time
where the time goes in v11:
time: 32.3 us; the launch traced here: 32.2 us
  waiting for transfers between devices  14.3 us (44%)
  starting transfers between devices  13.5 us (42%)
  Pallas kernels  3.65 us (11%)
  other arithmetic  0.7 us (2%)
    ppermute x6, waiting for transfers between devices, hop(): return lax.ppermute(value, ('z', 'core', 'col'), pairs)  12.7 us
    ppermute x6, starting transfers between devices, hop(): return lax.ppermute(value, ('z', 'core', 'col'), pairs)  11.5 us
    pallas_call x1, Pallas kernels, project(): pl.pallas_call(functools.partial(project_kernel, chunk, starts), out_shap...  3.32 us
    ppermute x6, starting transfers between devices, swap(): return lax.ppermute(value, axis, [(0, 1), (1, 0)])  1.96 us
    ppermute x6, waiting for transfers between devices, swap(): return lax.ppermute(value, axis, [(0, 1), (1, 0)])  1.58 us
  transfers between devices with their start and end apart: 12, of which 7 were waited for; matrix products, arithmetic and copies ran while one was open for 0% of the time, Pallas kernels for 0%

profile of v11, /device:TPU:0, one launch (start us, length us, event | category | flops | bytes accessed | tf_op | source)
XLA Modules:
  0.0 32.2 jit_solution(13116062535771842990)
XLA Ops:
  0.0 3.3 %shard_map.37 = (f32[2,16,8,128]{3,2,1,0:T(8,128)S(1)}, f32[2,16,8,128]{3,2,1,0:T(8,128)S(1)}, f32[2,16,8,128]{3,2,1,0:T(8,128)S(1)}, f32[2,16,8,128]{3,2,1,0:T(...) custom-call(bf16[16,64,2048]{2,1,0:T(8,128)(2,1)} %slab_ref.1, ...), custom_call_target="tpu_custom_call" | custom-call | flops 570425344 | bytes 5767168 | tf_op jit(solution)/shard_map/pallas_call | solution.py:69
  3.3 0.5 %collective-permute-start.2 = (f32[2,16,8,128]{3,2,1,0:T(8,128)S(1)}, f32[2,16,8,128]{3,2,1,0:T(8,128)S(1)}, u32[]{:S(2)}, u32[]{:S(2)}) collective-permute-start(f32[2,16,8,128]{3,2,1,0:T(8,128)S(1)} %get-tuple-element.21), channel_id=1, source_target_pairs={{0,2},{2,0},{1,3},{3,1},{4,6},{6,4},{5,7},{7,5},{8,10},{10,8},{9,1... | collective-permute-start | bytes 393224 | tf_op jit(solution)/shard_map/ppermute | solution.py:153
  3.8 0.1 collective-permute-start.4
  3.9 0.4 %collective-permute-start = (f32[2,16,8,128]{3,2,1,0:T(8,128)S(1)}, f32[2,16,8,128]{3,2,1,0:T(8,128)S(1)}, u32[]{:S(2)}, u32[]{:S(2)}) collective-permute-start(f32[2,16,8,128]{3,2,1,0:T(8,128)S(1)} %get-tuple-element.17), channel_id=1, source_target_pairs={{0,2},{2,0},{1,3},{3,1},{4,6},{6,4},{5,7},{7,5},{8,10},{10,8},{9,1... | collective-permute-start | bytes 393224 | tf_op jit(solution)/shard_map/ppermute | solution.py:153
  4.4 0.1 collective-permute-start.1
  4.4 0.4 %collective-permute-done.2 = f32[2,16,8,128]{3,2,1,0:T(8,128)S(1)} collective-permute-done((f32[2,16,8,128]{3,2,1,0:T(8,128)S(1)}, f32[2,16,8,128]{3,2,1,0:T(8,128)S(1)}, u32[]{:S(2)}, u32[]{:S(2)}) %collective-permute-start.2) | collective-permute-done | bytes 131104 | tf_op jit(solution)/shard_map/ppermute | solution.py:153
  4.9 3.0 %collective-permute-start.3 = (f32[2,16,8,128]{3,2,1,0:T(8,128)S(1)}, f32[2,16,8,128]{3,2,1,0:T(8,128)S(1)}, u32[]{:S(2)}, u32[]{:S(2)}) collective-permute-start(f32[2,16,8,128]{3,2,1,0:T(8,128)S(1)} %add.29), channel_id=1, source_target_pairs={{0,4},{1,5},{2,10},{3,11},{4,0},{5,1},{6,14},{7,15},{8,12},{9,13},... | collective-permute-start | bytes 393224 | tf_op jit(solution)/shard_map/ppermute | solution.py:149
  7.8 0.0 collective-permute-done.4
  7.9 0.2 collective-permute-start.5
  8.0 0.0 collective-permute-done
  8.1 0.0 collective-permute-done.1
  8.1 3.8 %collective-permute-done.3 = f32[2,16,8,128]{3,2,1,0:T(8,128)S(1)} collective-permute-done((f32[2,16,8,128]{3,2,1,0:T(8,128)S(1)}, f32[2,16,8,128]{3,2,1,0:T(8,128)S(1)}, u32[]{:S(2)}, u32[]{:S(2)}) %collective-permute-start.3) | collective-permute-done | bytes 131104 | tf_op jit(solution)/shard_map/ppermute | solution.py:149
  11.9 3.7 %collective-permute-start.8 = (f32[2,16,8,128]{3,2,1,0:T(8,128)S(1)}, f32[2,16,8,128]{3,2,1,0:T(8,128)S(1)}, u32[]{:S(2)}, u32[]{:S(2)}) collective-permute-start(f32[2,16,8,128]{3,2,1,0:T(8,128)S(1)} %add_add_fusion), channel_id=1, source_target_pairs={{0,9},{1,8},{2,7},{3,6},{4,13},{5,12},{6,3},{7,2},{8,1},{9,0},{10,... | collective-permute-start | bytes 393224 | tf_op jit(solution)/shard_map/ppermute | solution.py:149
  15.7 0.8 %collective-permute-start.6 = (f32[2,16,8,128]{3,2,1,0:T(8,128)S(1)}, f32[2,16,8,128]{3,2,1,0:T(8,128)S(1)}, u32[]{:S(2)}, u32[]{:S(2)}) collective-permute-start(f32[2,16,8,128]{3,2,1,0:T(8,128)S(1)} %add_add_fusion), channel_id=1, source_target_pairs={{0,8},{1,9},{2,6},{3,7},{4,12},{5,13},{6,2},{7,3},{8,0},{9,1},{10,... | collective-permute-start | bytes 393224 | tf_op jit(solution)/shard_map/ppermute | solution.py:149
  16.5 0.0 collective-permute-done.5
  16.5 0.8 %collective-permute-start.7 = (f32[2,16,8,128]{3,2,1,0:T(8,128)S(1)}, f32[2,16,8,128]{3,2,1,0:T(8,128)S(1)}, u32[]{:S(2)}, u32[]{:S(2)}) collective-permute-start(f32[2,16,8,128]{3,2,1,0:T(8,128)S(1)} %add.32.own_ref), channel_id=1, source_target_pairs={{0,1},{1,0},{2,3},{3,2},{4,5},{5,4},{6,7},{7,6},{8,9},{9,8},{10,11... | collective-permute-start | bytes 393224 | tf_op jit(solution)/shard_map/ppermute | solution.py:153
  17.3 1.7 %collective-permute-done.8.far_add = f32[2,16,8,128]{3,2,1,0:T(8,128)S(1)} collective-permute-done((f32[2,16,8,128]{3,2,1,0:T(8,128)S(1)}, f32[2,16,8,128]{3,2,1,0:T(8,128)S(1)}, u32[]{:S(2)}, u32[]{:S(2)}) %collective-permute-start.8) | collective-permute-done | bytes 131104 | tf_op jit(solution)/shard_map/ppermute | solution.py:149
  19.0 4.0 %collective-permute-done.6.own_add = f32[2,16,8,128]{3,2,1,0:T(8,128)S(1)} collective-permute-done((f32[2,16,8,128]{3,2,1,0:T(8,128)S(1)}, f32[2,16,8,128]{3,2,1,0:T(8,128)S(1)}, u32[]{:S(2)}, u32[]{:S(2)}) %collective-permute-start.6) | collective-permute-done | bytes 131104 | tf_op jit(solution)/shard_map/ppermute | solution.py:149
  23.0 0.0 collective-permute-done.7.far_ref
  23.0 0.3 %shard_map.38 = (f32[4,8,128]{2,1,0:T(8,128)S(1)}, s32[8,128]{1,0:T(8,128)S(1)}) custom-call(f32[2,16,8,128]{3,2,1,0:T(8,128)S(1)} %add.32.own_ref, f32[2,16,8,128]{3,2,1,0:T(8,128)S(1)} %collective-permute-done.6.own_add, f32[2,16,8,128]{3,2,1,0:T(8,128)S(1)} %collective-permute-done.7.far_ref, f32[2,16,8,128]{3,2,1,0:T(8,128)S(1)} %collective-permute-done.8.far_add), custom_call_target="tpu_custom_call" | custom-call | flops 2097152 | bytes 524288 | tf_op jit(solution)/shard_map/pallas_call | solution.py:127
  23.3 0.1 collective-permute-start.9
  23.4 1.2 %collective-permute-done.9 = f32[4,8,128]{2,1,0:T(8,128)S(1)} collective-permute-done((f32[4,8,128]{2,1,0:T(8,128)S(1)}, f32[4,8,128]{2,1,0:T(8,128)S(1)}, u32[]{:S(2)}, u32[]{:S(2)}) %collective-permute-start.9) | collective-permute-done | bytes 16416 | tf_op jit(solution)/shard_map/ppermute | solution.py:153
  24.5 1.2 %collective-permute-start.10 = (f32[2,8,128]{2,1,0:T(8,128)S(1)}, f32[2,8,128]{2,1,0:T(8,128)S(1)}, u32[]{:S(2)}, u32[]{:S(2)}) collective-permute-start(f32[2,8,128]{2,1,0:T(8,128)S(1)} %slice.29), channel_id=1, source_target_pairs={{0,6},{1,7},{2,4},{3,5},{4,2},{5,3},{6,0},{7,1},{8,14},{9,15},{10,... | collective-permute-start | bytes 24584 | tf_op jit(solution)/shard_map/ppermute | solution.py:149
  25.7 1.9 %collective-permute-done.10 = f32[2,8,128]{2,1,0:T(8,128)S(1)} collective-permute-done((f32[2,8,128]{2,1,0:T(8,128)S(1)}, f32[2,8,128]{2,1,0:T(8,128)S(1)}, u32[]{:S(2)}, u32[]{:S(2)}) %collective-permute-start.10) | collective-permute-done | bytes 8224 | tf_op jit(solution)/shard_map/ppermute | solution.py:149
  27.6 2.6 %collective-permute-start.11 = (f32[8,128]{1,0:T(8,128)S(1)}, f32[8,128]{1,0:T(8,128)S(1)}, u32[]{:S(2)}, u32[]{:S(2)}) collective-permute-start(f32[8,128]{1,0:T(8,128)S(1)} %slice_bitcast_fusion), channel_id=1, source_target_pairs={{0,10},{1,11},{2,8},{3,9},{4,14},{5,15},{6,12},{7,13},{8,2},{9,3},... | collective-permute-start | bytes 12296 | tf_op jit(solution)/shard_map/ppermute | solution.py:149
  30.3 1.3 %collective-permute-done.11 = f32[8,128]{1,0:T(8,128)S(1)} collective-permute-done((f32[8,128]{1,0:T(8,128)S(1)}, f32[8,128]{1,0:T(8,128)S(1)}, u32[]{:S(2)}, u32[]{:S(2)}) %collective-permute-start.11) | collective-permute-done | bytes 4128 | tf_op jit(solution)/shard_map/ppermute | solution.py:149
  31.6 0.6 %select_bitcast_fusion = f32[16,4]{0,1:T(4,128)} fusion(f32[8,128]{1,0:T(8,128)S(1)} %fusion, s32[8,128]{1,0:T(8,128)S(1)} %get-tuple-element.25), kind=kLoop, calls=%fused_computation.5 | loop fusion | flops 128 | bytes 1024 | tf_op jit(solution)/shard_map/transpose | solution.py:186
  (10 shorter events, 0.1 us)
Async XLA Ops:
  3.3 1.5 %collective-permute-start.2 = (f32[2,16,8,128]{3,2,1,0:T(8,128)S(1)}, f32[2,16,8,128]{3,2,1,0:T(8,128)S(1)}, u32[]{:S(2)}, u32[]{:S(2)}) collective-permute-start(f32[2,16,8,128]{3,2,1,0:T(8,128)S(1)} %get-tuple-element.21), channel_id=1, source_target_pairs={{0,2},{2,0},{1,3},{3,1},{4,6},{6,4},{5,7},{7,5},{8,10},{10,8},{9,1... | collective-permute-start | bytes 393224 | tf_op jit(solution)/shard_map/ppermute | solution.py:153
  3.8 4.0 %collective-permute-start.4 = (f32[2,16,8,128]{3,2,1,0:T(8,128)S(1)}, f32[2,16,8,128]{3,2,1,0:T(8,128)S(1)}, u32[]{:S(2)}, u32[]{:S(2)}) collective-permute-start(f32[2,16,8,128]{3,2,1,0:T(8,128)S(1)} %get-tuple-element.24), channel_id=1, source_target_pairs={{0,2},{2,0},{1,3},{3,1},{4,6},{6,4},{5,7},{7,5},{8,10},{10,8},{9,1... | collective-permute-start | bytes 393224 | tf_op jit(solution)/shard_map/ppermute | solution.py:153
  3.9 4.1 %collective-permute-start = (f32[2,16,8,128]{3,2,1,0:T(8,128)S(1)}, f32[2,16,8,128]{3,2,1,0:T(8,128)S(1)}, u32[]{:S(2)}, u32[]{:S(2)}) collective-permute-start(f32[2,16,8,128]{3,2,1,0:T(8,128)S(1)} %get-tuple-element.17), channel_id=1, source_target_pairs={{0,2},{2,0},{1,3},{3,1},{4,6},{6,4},{5,7},{7,5},{8,10},{10,8},{9,1... | collective-permute-start | bytes 393224 | tf_op jit(solution)/shard_map/ppermute | solution.py:153
  4.4 3.7 %collective-permute-start.1 = (f32[2,16,8,128]{3,2,1,0:T(8,128)S(1)}, f32[2,16,8,128]{3,2,1,0:T(8,128)S(1)}, u32[]{:S(2)}, u32[]{:S(2)}) collective-permute-start(f32[2,16,8,128]{3,2,1,0:T(8,128)S(1)} %get-tuple-element.19), channel_id=1, source_target_pairs={{0,2},{2,0},{1,3},{3,1},{4,6},{6,4},{5,7},{7,5},{8,10},{10,8},{9,1... | collective-permute-start | bytes 393224 | tf_op jit(solution)/shard_map/ppermute | solution.py:153
  4.9 7.1 %collective-permute-start.3 = (f32[2,16,8,128]{3,2,1,0:T(8,128)S(1)}, f32[2,16,8,128]{3,2,1,0:T(8,128)S(1)}, u32[]{:S(2)}, u32[]{:S(2)}) collective-permute-start(f32[2,16,8,128]{3,2,1,0:T(8,128)S(1)} %add.29), channel_id=1, source_target_pairs={{0,4},{1,5},{2,10},{3,11},{4,0},{5,1},{6,14},{7,15},{8,12},{9,13},... | collective-permute-start | bytes 393224 | tf_op jit(solution)/shard_map/ppermute | solution.py:149
  7.9 8.6 %collective-permute-start.5 = (f32[2,16,8,128]{3,2,1,0:T(8,128)S(1)}, f32[2,16,8,128]{3,2,1,0:T(8,128)S(1)}, u32[]{:S(2)}, u32[]{:S(2)}) collective-permute-start(f32[2,16,8,128]{3,2,1,0:T(8,128)S(1)} %add.31), channel_id=1, source_target_pairs={{0,4},{1,5},{2,10},{3,11},{4,0},{5,1},{6,14},{7,15},{8,12},{9,13},... | collective-permute-start | bytes 393224 | tf_op jit(solution)/shard_map/ppermute | solution.py:149
  11.9 7.0 %collective-permute-start.8 = (f32[2,16,8,128]{3,2,1,0:T(8,128)S(1)}, f32[2,16,8,128]{3,2,1,0:T(8,128)S(1)}, u32[]{:S(2)}, u32[]{:S(2)}) collective-permute-start(f32[2,16,8,128]{3,2,1,0:T(8,128)S(1)} %add_add_fusion), channel_id=1, source_target_pairs={{0,9},{1,8},{2,7},{3,6},{4,13},{5,12},{6,3},{7,2},{8,1},{9,0},{10,... | collective-permute-start | bytes 393224 | tf_op jit(solution)/shard_map/ppermute | solution.py:149
  15.7 7.3 %collective-permute-start.6 = (f32[2,16,8,128]{3,2,1,0:T(8,128)S(1)}, f32[2,16,8,128]{3,2,1,0:T(8,128)S(1)}, u32[]{:S(2)}, u32[]{:S(2)}) collective-permute-start(f32[2,16,8,128]{3,2,1,0:T(8,128)S(1)} %add_add_fusion), channel_id=1, source_target_pairs={{0,8},{1,9},{2,6},{3,7},{4,12},{5,13},{6,2},{7,3},{8,0},{9,1},{10,... | collective-permute-start | bytes 393224 | tf_op jit(solution)/shard_map/ppermute | solution.py:149
  16.5 6.4 %collective-permute-start.7 = (f32[2,16,8,128]{3,2,1,0:T(8,128)S(1)}, f32[2,16,8,128]{3,2,1,0:T(8,128)S(1)}, u32[]{:S(2)}, u32[]{:S(2)}) collective-permute-start(f32[2,16,8,128]{3,2,1,0:T(8,128)S(1)} %add.32.own_ref), channel_id=1, source_target_pairs={{0,1},{1,0},{2,3},{3,2},{4,5},{5,4},{6,7},{7,6},{8,9},{9,8},{10,11... | collective-permute-start | bytes 393224 | tf_op jit(solution)/shard_map/ppermute | solution.py:153
  23.3 1.2 %collective-permute-start.9 = (f32[4,8,128]{2,1,0:T(8,128)S(1)}, f32[4,8,128]{2,1,0:T(8,128)S(1)}, u32[]{:S(2)}, u32[]{:S(2)}) collective-permute-start(f32[4,8,128]{2,1,0:T(8,128)S(1)} %get-tuple-element.26), channel_id=1, source_target_pairs={{0,2},{2,0},{1,3},{3,1},{4,6},{6,4},{5,7},{7,5},{8,10},{10,8},{9,1... | collective-permute-start | bytes 49160 | tf_op jit(solution)/shard_map/ppermute | solution.py:153
  24.5 3.1 %collective-permute-start.10 = (f32[2,8,128]{2,1,0:T(8,128)S(1)}, f32[2,8,128]{2,1,0:T(8,128)S(1)}, u32[]{:S(2)}, u32[]{:S(2)}) collective-permute-start(f32[2,8,128]{2,1,0:T(8,128)S(1)} %slice.29), channel_id=1, source_target_pairs={{0,6},{1,7},{2,4},{3,5},{4,2},{5,3},{6,0},{7,1},{8,14},{9,15},{10,... | collective-permute-start | bytes 24584 | tf_op jit(solution)/shard_map/ppermute | solution.py:149
  27.6 4.0 %collective-permute-start.11 = (f32[8,128]{1,0:T(8,128)S(1)}, f32[8,128]{1,0:T(8,128)S(1)}, u32[]{:S(2)}, u32[]{:S(2)}) collective-permute-start(f32[8,128]{1,0:T(8,128)S(1)} %slice_bitcast_fusion), channel_id=1, source_target_pairs={{0,10},{1,11},{2,8},{3,9},{4,14},{5,15},{6,12},{7,13},{8,2},{9,3},... | collective-permute-start | bytes 12296 | tf_op jit(solution)/shard_map/ppermute | solution.py:149

commit v12 on v10

--- a/solution.py
+++ b/solution.py
@@ -167,13 +167,13 @@
     arrived = hop(passed, zs, FIRST_HOP)
     beside = hop(given, zs, FIRST_HOP)
     onward = across + arrived
+    far_add = hop(onward, zs, SECOND_HOP, flip=1)
     own_add = hop(onward, zs, SECOND_HOP)
-    far_add = hop(onward, zs, SECOND_HOP, flip=1)
     own = lax.optimization_barrier((own, onward))[0] + beside
     blocks, flag = gram_blocks((own, own_add), (swap(own, "col"), far_add), zs, scale)
-    pair = blocks[0::2] + hop(blocks[1::2], zs, (SECOND, SECOND), cross=1)
-    pair = pair + swap(pair, "core")
-    last = pair[0] + hop(pair[1], zs, (FIRST, FIRST), cross=1)
+    blocks = blocks + swap(blocks, "core")
+    pair = blocks[:2] + hop(blocks[2:], zs, (FIRST, FIRST), cross=1)
+    last = pair[0] + hop(pair[1], zs, (SECOND, SECOND), cross=1)
     depth, rows = slab.shape[0], last.shape[0] // CORES
     return jnp.where(flag[:rows, :depth] == 1, last[rows:, :depth], last[:rows, :depth]).T
 

time: 32.3 us -> 32.3 us (level)
  starting transfers between devices: 12.1 us -> 13.5 us
  waiting for transfers between devices: 15.7 us -> 14.3 us
    ppermute x6, waiting for transfers between devices: 14.1 us -> 12.7 us  [hop(): return lax.ppermute(value, ('z', 'core', 'col'), pairs)]
    ppermute x6, starting transfers between devices: 10.2 us -> 11.5 us  [hop(): return lax.ppermute(value, ('z', 'core', 'col'), pairs)]
where the time goes in v12:
time: 32.3 us; the launch traced here: 32.2 us
  waiting for transfers between devices  14.3 us (44%)
  starting transfers between devices  13.5 us (42%)
  Pallas kernels  3.62 us (11%)
  other arithmetic  0.7 us (2%)
    ppermute x6, waiting for transfers between devices, hop(): return lax.ppermute(value, ('z', 'core', 'col'), pairs)  12.7 us
    ppermute x6, starting transfers between devices, hop(): return lax.ppermute(value, ('z', 'core', 'col'), pairs)  11.5 us
    pallas_call x1, Pallas kernels, project(): pl.pallas_call(functools.partial(project_kernel, chunk, starts), out_shap...  3.31 us
    ppermute x6, starting transfers between devices, swap(): return lax.ppermute(value, axis, [(0, 1), (1, 0)])  1.96 us
    ppermute x6, waiting for transfers between devices, swap(): return lax.ppermute(value, axis, [(0, 1), (1, 0)])  1.58 us
  transfers between devices with their start and end apart: 12, of which 7 were waited for; matrix products, arithmetic and copies ran while one was open for 0% of the time, Pallas kernels for 0%

profile of v12, /device:TPU:0, one launch (start us, length us, event | category | flops | bytes accessed | tf_op | source)
XLA Modules:
  0.0 32.2 jit_solution(2628212485863980810)
XLA Ops:
  0.0 3.3 %shard_map.37 = (f32[2,16,8,128]{3,2,1,0:T(8,128)S(1)}, f32[2,16,8,128]{3,2,1,0:T(8,128)S(1)}, f32[2,16,8,128]{3,2,1,0:T(8,128)S(1)}, f32[2,16,8,128]{3,2,1,0:T(...) custom-call(bf16[16,64,2048]{2,1,0:T(8,128)(2,1)} %slab_ref.1, ...), custom_call_target="tpu_custom_call" | custom-call | flops 570425344 | bytes 5767168 | tf_op jit(solution)/shard_map/pallas_call | solution.py:66
  3.3 0.5 %collective-permute-start.2 = (f32[2,16,8,128]{3,2,1,0:T(8,128)S(1)}, f32[2,16,8,128]{3,2,1,0:T(8,128)S(1)}, u32[]{:S(2)}, u32[]{:S(2)}) collective-permute-start(f32[2,16,8,128]{3,2,1,0:T(8,128)S(1)} %get-tuple-element.21), channel_id=1, source_target_pairs={{0,2},{2,0},{1,3},{3,1},{4,6},{6,4},{5,7},{7,5},{8,10},{10,8},{9,1... | collective-permute-start | bytes 393224 | tf_op jit(solution)/shard_map/ppermute | solution.py:145
  3.8 0.1 collective-permute-start.4
  3.9 0.4 %collective-permute-start = (f32[2,16,8,128]{3,2,1,0:T(8,128)S(1)}, f32[2,16,8,128]{3,2,1,0:T(8,128)S(1)}, u32[]{:S(2)}, u32[]{:S(2)}) collective-permute-start(f32[2,16,8,128]{3,2,1,0:T(8,128)S(1)} %get-tuple-element.17), channel_id=1, source_target_pairs={{0,2},{2,0},{1,3},{3,1},{4,6},{6,4},{5,7},{7,5},{8,10},{10,8},{9,1... | collective-permute-start | bytes 393224 | tf_op jit(solution)/shard_map/ppermute | solution.py:145
  4.3 0.1 collective-permute-start.1
  4.4 0.4 %collective-permute-done.2 = f32[2,16,8,128]{3,2,1,0:T(8,128)S(1)} collective-permute-done((f32[2,16,8,128]{3,2,1,0:T(8,128)S(1)}, f32[2,16,8,128]{3,2,1,0:T(8,128)S(1)}, u32[]{:S(2)}, u32[]{:S(2)}) %collective-permute-start.2) | collective-permute-done | bytes 131104 | tf_op jit(solution)/shard_map/ppermute | solution.py:145
  4.8 3.0 %collective-permute-start.3 = (f32[2,16,8,128]{3,2,1,0:T(8,128)S(1)}, f32[2,16,8,128]{3,2,1,0:T(8,128)S(1)}, u32[]{:S(2)}, u32[]{:S(2)}) collective-permute-start(f32[2,16,8,128]{3,2,1,0:T(8,128)S(1)} %add.29), channel_id=1, source_target_pairs={{0,4},{1,5},{2,10},{3,11},{4,0},{5,1},{6,14},{7,15},{8,12},{9,13},... | collective-permute-start | bytes 393224 | tf_op jit(solution)/shard_map/ppermute | solution.py:141
  7.8 0.0 collective-permute-done.4
  7.9 0.2 collective-permute-start.5
  8.0 0.0 collective-permute-done
  8.0 0.0 collective-permute-done.1
  8.1 3.8 %collective-permute-done.3 = f32[2,16,8,128]{3,2,1,0:T(8,128)S(1)} collective-permute-done((f32[2,16,8,128]{3,2,1,0:T(8,128)S(1)}, f32[2,16,8,128]{3,2,1,0:T(8,128)S(1)}, u32[]{:S(2)}, u32[]{:S(2)}) %collective-permute-start.3) | collective-permute-done | bytes 131104 | tf_op jit(solution)/shard_map/ppermute | solution.py:141
  11.9 3.7 %collective-permute-start.8 = (f32[2,16,8,128]{3,2,1,0:T(8,128)S(1)}, f32[2,16,8,128]{3,2,1,0:T(8,128)S(1)}, u32[]{:S(2)}, u32[]{:S(2)}) collective-permute-start(f32[2,16,8,128]{3,2,1,0:T(8,128)S(1)} %add_add_fusion), channel_id=1, source_target_pairs={{0,9},{1,8},{2,7},{3,6},{4,13},{5,12},{6,3},{7,2},{8,1},{9,0},{10,... | collective-permute-start | bytes 393224 | tf_op jit(solution)/shard_map/ppermute | solution.py:141
  15.7 0.8 %collective-permute-start.6 = (f32[2,16,8,128]{3,2,1,0:T(8,128)S(1)}, f32[2,16,8,128]{3,2,1,0:T(8,128)S(1)}, u32[]{:S(2)}, u32[]{:S(2)}) collective-permute-start(f32[2,16,8,128]{3,2,1,0:T(8,128)S(1)} %add_add_fusion), channel_id=1, source_target_pairs={{0,8},{1,9},{2,6},{3,7},{4,12},{5,13},{6,2},{7,3},{8,0},{9,1},{10,... | collective-permute-start | bytes 393224 | tf_op jit(solution)/shard_map/ppermute | solution.py:141
  16.5 0.0 collective-permute-done.5
  16.5 0.8 %collective-permute-start.7 = (f32[2,16,8,128]{3,2,1,0:T(8,128)S(1)}, f32[2,16,8,128]{3,2,1,0:T(8,128)S(1)}, u32[]{:S(2)}, u32[]{:S(2)}) collective-permute-start(f32[2,16,8,128]{3,2,1,0:T(8,128)S(1)} %add.32.own_ref), channel_id=1, source_target_pairs={{0,1},{1,0},{2,3},{3,2},{4,5},{5,4},{6,7},{7,6},{8,9},{9,8},{10,11... | collective-permute-start | bytes 393224 | tf_op jit(solution)/shard_map/ppermute | solution.py:145
  17.3 1.7 %collective-permute-done.8.far_add = f32[2,16,8,128]{3,2,1,0:T(8,128)S(1)} collective-permute-done((f32[2,16,8,128]{3,2,1,0:T(8,128)S(1)}, f32[2,16,8,128]{3,2,1,0:T(8,128)S(1)}, u32[]{:S(2)}, u32[]{:S(2)}) %collective-permute-start.8) | collective-permute-done | bytes 131104 | tf_op jit(solution)/shard_map/ppermute | solution.py:141
  19.0 4.0 %collective-permute-done.6.own_add = f32[2,16,8,128]{3,2,1,0:T(8,128)S(1)} collective-permute-done((f32[2,16,8,128]{3,2,1,0:T(8,128)S(1)}, f32[2,16,8,128]{3,2,1,0:T(8,128)S(1)}, u32[]{:S(2)}, u32[]{:S(2)}) %collective-permute-start.6) | collective-permute-done | bytes 131104 | tf_op jit(solution)/shard_map/ppermute | solution.py:141
  22.9 0.0 collective-permute-done.7.far_ref
  22.9 0.3 shard_map.38
  23.3 0.1 collective-permute-start.9
  23.3 1.2 %collective-permute-done.9 = f32[4,8,128]{2,1,0:T(8,128)S(1)} collective-permute-done((f32[4,8,128]{2,1,0:T(8,128)S(1)}, f32[4,8,128]{2,1,0:T(8,128)S(1)}, u32[]{:S(2)}, u32[]{:S(2)}) %collective-permute-start.9) | collective-permute-done | bytes 16416 | tf_op jit(solution)/shard_map/ppermute | solution.py:145
  24.5 1.2 %collective-permute-start.10 = (f32[2,8,128]{2,1,0:T(8,128)S(1)}, f32[2,8,128]{2,1,0:T(8,128)S(1)}, u32[]{:S(2)}, u32[]{:S(2)}) collective-permute-start(f32[2,8,128]{2,1,0:T(8,128)S(1)} %slice.29), channel_id=1, source_target_pairs={{0,6},{1,7},{2,4},{3,5},{4,2},{5,3},{6,0},{7,1},{8,14},{9,15},{10,... | collective-permute-start | bytes 24584 | tf_op jit(solution)/shard_map/ppermute | solution.py:141
  25.7 1.9 %collective-permute-done.10 = f32[2,8,128]{2,1,0:T(8,128)S(1)} collective-permute-done((f32[2,8,128]{2,1,0:T(8,128)S(1)}, f32[2,8,128]{2,1,0:T(8,128)S(1)}, u32[]{:S(2)}, u32[]{:S(2)}) %collective-permute-start.10) | collective-permute-done | bytes 8224 | tf_op jit(solution)/shard_map/ppermute | solution.py:141
  27.6 2.6 %collective-permute-start.11 = (f32[8,128]{1,0:T(8,128)S(1)}, f32[8,128]{1,0:T(8,128)S(1)}, u32[]{:S(2)}, u32[]{:S(2)}) collective-permute-start(f32[8,128]{1,0:T(8,128)S(1)} %slice_bitcast_fusion), channel_id=1, source_target_pairs={{0,10},{1,11},{2,8},{3,9},{4,14},{5,15},{6,12},{7,13},{8,2},{9,3},... | collective-permute-start | bytes 12296 | tf_op jit(solution)/shard_map/ppermute | solution.py:141
  30.2 1.3 %collective-permute-done.11 = f32[8,128]{1,0:T(8,128)S(1)} collective-permute-done((f32[8,128]{1,0:T(8,128)S(1)}, f32[8,128]{1,0:T(8,128)S(1)}, u32[]{:S(2)}, u32[]{:S(2)}) %collective-permute-start.11) | collective-permute-done | bytes 4128 | tf_op jit(solution)/shard_map/ppermute | solution.py:141
  31.6 0.6 %select_bitcast_fusion = f32[16,4]{0,1:T(4,128)} fusion(f32[8,128]{1,0:T(8,128)S(1)} %fusion, s32[8,128]{1,0:T(8,128)S(1)} %get-tuple-element.25), kind=kLoop, calls=%fused_computation.5 | loop fusion | flops 128 | bytes 1024 | tf_op jit(solution)/shard_map/transpose | solution.py:178
  (10 shorter events, 0.1 us)
Async XLA Ops:
  3.3 1.5 %collective-permute-start.2 = (f32[2,16,8,128]{3,2,1,0:T(8,128)S(1)}, f32[2,16,8,128]{3,2,1,0:T(8,128)S(1)}, u32[]{:S(2)}, u32[]{:S(2)}) collective-permute-start(f32[2,16,8,128]{3,2,1,0:T(8,128)S(1)} %get-tuple-element.21), channel_id=1, source_target_pairs={{0,2},{2,0},{1,3},{3,1},{4,6},{6,4},{5,7},{7,5},{8,10},{10,8},{9,1... | collective-permute-start | bytes 393224 | tf_op jit(solution)/shard_map/ppermute | solution.py:145
  3.8 4.0 %collective-permute-start.4 = (f32[2,16,8,128]{3,2,1,0:T(8,128)S(1)}, f32[2,16,8,128]{3,2,1,0:T(8,128)S(1)}, u32[]{:S(2)}, u32[]{:S(2)}) collective-permute-start(f32[2,16,8,128]{3,2,1,0:T(8,128)S(1)} %get-tuple-element.24), channel_id=1, source_target_pairs={{0,2},{2,0},{1,3},{3,1},{4,6},{6,4},{5,7},{7,5},{8,10},{10,8},{9,1... | collective-permute-start | bytes 393224 | tf_op jit(solution)/shard_map/ppermute | solution.py:145
  3.9 4.1 %collective-permute-start = (f32[2,16,8,128]{3,2,1,0:T(8,128)S(1)}, f32[2,16,8,128]{3,2,1,0:T(8,128)S(1)}, u32[]{:S(2)}, u32[]{:S(2)}) collective-permute-start(f32[2,16,8,128]{3,2,1,0:T(8,128)S(1)} %get-tuple-element.17), channel_id=1, source_target_pairs={{0,2},{2,0},{1,3},{3,1},{4,6},{6,4},{5,7},{7,5},{8,10},{10,8},{9,1... | collective-permute-start | bytes 393224 | tf_op jit(solution)/shard_map/ppermute | solution.py:145
  4.3 3.7 %collective-permute-start.1 = (f32[2,16,8,128]{3,2,1,0:T(8,128)S(1)}, f32[2,16,8,128]{3,2,1,0:T(8,128)S(1)}, u32[]{:S(2)}, u32[]{:S(2)}) collective-permute-start(f32[2,16,8,128]{3,2,1,0:T(8,128)S(1)} %get-tuple-element.19), channel_id=1, source_target_pairs={{0,2},{2,0},{1,3},{3,1},{4,6},{6,4},{5,7},{7,5},{8,10},{10,8},{9,1... | collective-permute-start | bytes 393224 | tf_op jit(solution)/shard_map/ppermute | solution.py:145
  4.8 7.1 %collective-permute-start.3 = (f32[2,16,8,128]{3,2,1,0:T(8,128)S(1)}, f32[2,16,8,128]{3,2,1,0:T(8,128)S(1)}, u32[]{:S(2)}, u32[]{:S(2)}) collective-permute-start(f32[2,16,8,128]{3,2,1,0:T(8,128)S(1)} %add.29), channel_id=1, source_target_pairs={{0,4},{1,5},{2,10},{3,11},{4,0},{5,1},{6,14},{7,15},{8,12},{9,13},... | collective-permute-start | bytes 393224 | tf_op jit(solution)/shard_map/ppermute | solution.py:141
  7.9 8.6 %collective-permute-start.5 = (f32[2,16,8,128]{3,2,1,0:T(8,128)S(1)}, f32[2,16,8,128]{3,2,1,0:T(8,128)S(1)}, u32[]{:S(2)}, u32[]{:S(2)}) collective-permute-start(f32[2,16,8,128]{3,2,1,0:T(8,128)S(1)} %add.31), channel_id=1, source_target_pairs={{0,4},{1,5},{2,10},{3,11},{4,0},{5,1},{6,14},{7,15},{8,12},{9,13},... | collective-permute-start | bytes 393224 | tf_op jit(solution)/shard_map/ppermute | solution.py:141
  11.9 7.0 %collective-permute-start.8 = (f32[2,16,8,128]{3,2,1,0:T(8,128)S(1)}, f32[2,16,8,128]{3,2,1,0:T(8,128)S(1)}, u32[]{:S(2)}, u32[]{:S(2)}) collective-permute-start(f32[2,16,8,128]{3,2,1,0:T(8,128)S(1)} %add_add_fusion), channel_id=1, source_target_pairs={{0,9},{1,8},{2,7},{3,6},{4,13},{5,12},{6,3},{7,2},{8,1},{9,0},{10,... | collective-permute-start | bytes 393224 | tf_op jit(solution)/shard_map/ppermute | solution.py:141
  15.7 7.3 %collective-permute-start.6 = (f32[2,16,8,128]{3,2,1,0:T(8,128)S(1)}, f32[2,16,8,128]{3,2,1,0:T(8,128)S(1)}, u32[]{:S(2)}, u32[]{:S(2)}) collective-permute-start(f32[2,16,8,128]{3,2,1,0:T(8,128)S(1)} %add_add_fusion), channel_id=1, source_target_pairs={{0,8},{1,9},{2,6},{3,7},{4,12},{5,13},{6,2},{7,3},{8,0},{9,1},{10,... | collective-permute-start | bytes 393224 | tf_op jit(solution)/shard_map/ppermute | solution.py:141
  16.5 6.4 %collective-permute-start.7 = (f32[2,16,8,128]{3,2,1,0:T(8,128)S(1)}, f32[2,16,8,128]{3,2,1,0:T(8,128)S(1)}, u32[]{:S(2)}, u32[]{:S(2)}) collective-permute-start(f32[2,16,8,128]{3,2,1,0:T(8,128)S(1)} %add.32.own_ref), channel_id=1, source_target_pairs={{0,1},{1,0},{2,3},{3,2},{4,5},{5,4},{6,7},{7,6},{8,9},{9,8},{10,11... | collective-permute-start | bytes 393224 | tf_op jit(solution)/shard_map/ppermute | solution.py:145
  23.3 1.2 %collective-permute-start.9 = (f32[4,8,128]{2,1,0:T(8,128)S(1)}, f32[4,8,128]{2,1,0:T(8,128)S(1)}, u32[]{:S(2)}, u32[]{:S(2)}) collective-permute-start(f32[4,8,128]{2,1,0:T(8,128)S(1)} %get-tuple-element.26), channel_id=1, source_target_pairs={{0,2},{2,0},{1,3},{3,1},{4,6},{6,4},{5,7},{7,5},{8,10},{10,8},{9,1... | collective-permute-start | bytes 49160 | tf_op jit(solution)/shard_map/ppermute | solution.py:145
  24.5 3.1 %collective-permute-start.10 = (f32[2,8,128]{2,1,0:T(8,128)S(1)}, f32[2,8,128]{2,1,0:T(8,128)S(1)}, u32[]{:S(2)}, u32[]{:S(2)}) collective-permute-start(f32[2,8,128]{2,1,0:T(8,128)S(1)} %slice.29), channel_id=1, source_target_pairs={{0,6},{1,7},{2,4},{3,5},{4,2},{5,3},{6,0},{7,1},{8,14},{9,15},{10,... | collective-permute-start | bytes 24584 | tf_op jit(solution)/shard_map/ppermute | solution.py:141
  27.6 4.0 %collective-permute-start.11 = (f32[8,128]{1,0:T(8,128)S(1)}, f32[8,128]{1,0:T(8,128)S(1)}, u32[]{:S(2)}, u32[]{:S(2)}) collective-permute-start(f32[8,128]{1,0:T(8,128)S(1)} %slice_bitcast_fusion), channel_id=1, source_target_pairs={{0,10},{1,11},{2,8},{3,9},{4,14},{5,15},{6,12},{7,13},{8,2},{9,3},... | collective-permute-start | bytes 12296 | tf_op jit(solution)/shard_map/ppermute | solution.py:141

commit v13 on v8

--- a/solution.py
+++ b/solution.py
@@ -100,8 +100,8 @@
         total[g, pl.ds(pl.multiple_of(x * size, size), size), :] = (own_ref[g] + own_add[g]).reshape(size, -1)
         total[g, pl.ds(pl.multiple_of((1 - x) * size, size), size), :] = (far_ref[g] + far_add[g]).reshape(size, -1)
     picks = [(g, s) for g in range(groups) for s in range(tile)]
-    for n in range(0, len(picks), 16):
-        part = picks[n : n + 16]
+    for n in range(0, len(picks), 4):
+        part = picks[n : n + 4]
         rows = jnp.concatenate([total[g, pl.ds(s, 2 * depth, stride=tile), :] for g, s in part], axis=1)
         own = jnp.concatenate([total[g, pl.ds(x * size + s, depth, stride=tile), :] for g, s in part], axis=1)
         four = lax.dot_general(

time: 32.3 us -> 32.3 us (level)
  no operation moved by 1% of the time
where the time goes in v13:
time: 32.3 us; the launch traced here: 32.2 us
  waiting for transfers between devices  14.3 us (44%)
  starting transfers between devices  13.5 us (42%)
  Pallas kernels  3.64 us (11%)
  other arithmetic  0.7 us (2%)
    ppermute x6, waiting for transfers between devices, hop(): return lax.ppermute(value, ('z', 'core', 'col'), pairs)  12.7 us
    ppermute x6, starting transfers between devices, hop(): return lax.ppermute(value, ('z', 'core', 'col'), pairs)  11.5 us
    pallas_call x1, Pallas kernels, project(): pl.pallas_call(functools.partial(project_kernel, chunk, starts), out_shap...  3.31 us
    ppermute x6, starting transfers between devices, swap(): return lax.ppermute(value, axis, [(0, 1), (1, 0)])  1.96 us
    ppermute x6, waiting for transfers between devices, swap(): return lax.ppermute(value, axis, [(0, 1), (1, 0)])  1.58 us
  transfers between devices with their start and end apart: 12, of which 7 were waited for; matrix products, arithmetic and copies ran while one was open for 0% of the time, Pallas kernels for 0%

profile of v13, /device:TPU:0, one launch (start us, length us, event | category | flops | bytes accessed | tf_op | source)
XLA Modules:
  0.0 32.2 jit_solution(7631974697118030561)
XLA Ops:
  0.0 3.3 %shard_map.37 = (f32[2,16,8,128]{3,2,1,0:T(8,128)S(1)}, f32[2,16,8,128]{3,2,1,0:T(8,128)S(1)}, f32[2,16,8,128]{3,2,1,0:T(8,128)S(1)}, f32[2,16,8,128]{3,2,1,0:T(...) custom-call(bf16[16,64,2048]{2,1,0:T(8,128)(2,1)} %slab_ref.1, ...), custom_call_target="tpu_custom_call" | custom-call | flops 570425344 | bytes 5767168 | tf_op jit(solution)/shard_map/pallas_call | solution.py:66
  3.3 0.5 %collective-permute-start.2 = (f32[2,16,8,128]{3,2,1,0:T(8,128)S(1)}, f32[2,16,8,128]{3,2,1,0:T(8,128)S(1)}, u32[]{:S(2)}, u32[]{:S(2)}) collective-permute-start(f32[2,16,8,128]{3,2,1,0:T(8,128)S(1)} %get-tuple-element.21), channel_id=1, source_target_pairs={{0,2},{2,0},{1,3},{3,1},{4,6},{6,4},{5,7},{7,5},{8,10},{10,8},{9,1... | collective-permute-start | bytes 393224 | tf_op jit(solution)/shard_map/ppermute | solution.py:150
  3.8 0.1 collective-permute-start.4
  3.9 0.4 %collective-permute-start = (f32[2,16,8,128]{3,2,1,0:T(8,128)S(1)}, f32[2,16,8,128]{3,2,1,0:T(8,128)S(1)}, u32[]{:S(2)}, u32[]{:S(2)}) collective-permute-start(f32[2,16,8,128]{3,2,1,0:T(8,128)S(1)} %get-tuple-element.17), channel_id=1, source_target_pairs={{0,2},{2,0},{1,3},{3,1},{4,6},{6,4},{5,7},{7,5},{8,10},{10,8},{9,1... | collective-permute-start | bytes 393224 | tf_op jit(solution)/shard_map/ppermute | solution.py:150
  4.3 0.1 collective-permute-start.1
  4.4 0.4 %collective-permute-done.2 = f32[2,16,8,128]{3,2,1,0:T(8,128)S(1)} collective-permute-done((f32[2,16,8,128]{3,2,1,0:T(8,128)S(1)}, f32[2,16,8,128]{3,2,1,0:T(8,128)S(1)}, u32[]{:S(2)}, u32[]{:S(2)}) %collective-permute-start.2) | collective-permute-done | bytes 131104 | tf_op jit(solution)/shard_map/ppermute | solution.py:150
  4.8 3.0 %collective-permute-start.3 = (f32[2,16,8,128]{3,2,1,0:T(8,128)S(1)}, f32[2,16,8,128]{3,2,1,0:T(8,128)S(1)}, u32[]{:S(2)}, u32[]{:S(2)}) collective-permute-start(f32[2,16,8,128]{3,2,1,0:T(8,128)S(1)} %add.29), channel_id=1, source_target_pairs={{0,4},{1,5},{2,10},{3,11},{4,0},{5,1},{6,14},{7,15},{8,12},{9,13},... | collective-permute-start | bytes 393224 | tf_op jit(solution)/shard_map/ppermute | solution.py:146
  7.8 0.0 collective-permute-done.4
  7.9 0.2 collective-permute-start.5
  8.0 0.0 collective-permute-done
  8.0 0.0 collective-permute-done.1
  8.1 3.8 %collective-permute-done.3 = f32[2,16,8,128]{3,2,1,0:T(8,128)S(1)} collective-permute-done((f32[2,16,8,128]{3,2,1,0:T(8,128)S(1)}, f32[2,16,8,128]{3,2,1,0:T(8,128)S(1)}, u32[]{:S(2)}, u32[]{:S(2)}) %collective-permute-start.3) | collective-permute-done | bytes 131104 | tf_op jit(solution)/shard_map/ppermute | solution.py:146
  11.9 3.7 %collective-permute-start.8 = (f32[2,16,8,128]{3,2,1,0:T(8,128)S(1)}, f32[2,16,8,128]{3,2,1,0:T(8,128)S(1)}, u32[]{:S(2)}, u32[]{:S(2)}) collective-permute-start(f32[2,16,8,128]{3,2,1,0:T(8,128)S(1)} %add_add_fusion), channel_id=1, source_target_pairs={{0,9},{1,8},{2,7},{3,6},{4,13},{5,12},{6,3},{7,2},{8,1},{9,0},{10,... | collective-permute-start | bytes 393224 | tf_op jit(solution)/shard_map/ppermute | solution.py:146
  15.7 0.8 %collective-permute-start.6 = (f32[2,16,8,128]{3,2,1,0:T(8,128)S(1)}, f32[2,16,8,128]{3,2,1,0:T(8,128)S(1)}, u32[]{:S(2)}, u32[]{:S(2)}) collective-permute-start(f32[2,16,8,128]{3,2,1,0:T(8,128)S(1)} %add_add_fusion), channel_id=1, source_target_pairs={{0,8},{1,9},{2,6},{3,7},{4,12},{5,13},{6,2},{7,3},{8,0},{9,1},{10,... | collective-permute-start | bytes 393224 | tf_op jit(solution)/shard_map/ppermute | solution.py:146
  16.5 0.0 collective-permute-done.5
  16.5 0.8 %collective-permute-start.7 = (f32[2,16,8,128]{3,2,1,0:T(8,128)S(1)}, f32[2,16,8,128]{3,2,1,0:T(8,128)S(1)}, u32[]{:S(2)}, u32[]{:S(2)}) collective-permute-start(f32[2,16,8,128]{3,2,1,0:T(8,128)S(1)} %add.32.own_ref), channel_id=1, source_target_pairs={{0,1},{1,0},{2,3},{3,2},{4,5},{5,4},{6,7},{7,6},{8,9},{9,8},{10,11... | collective-permute-start | bytes 393224 | tf_op jit(solution)/shard_map/ppermute | solution.py:150
  17.3 1.7 %collective-permute-done.8.far_add = f32[2,16,8,128]{3,2,1,0:T(8,128)S(1)} collective-permute-done((f32[2,16,8,128]{3,2,1,0:T(8,128)S(1)}, f32[2,16,8,128]{3,2,1,0:T(8,128)S(1)}, u32[]{:S(2)}, u32[]{:S(2)}) %collective-permute-start.8) | collective-permute-done | bytes 131104 | tf_op jit(solution)/shard_map/ppermute | solution.py:146
  19.0 4.0 %collective-permute-done.6.own_add = f32[2,16,8,128]{3,2,1,0:T(8,128)S(1)} collective-permute-done((f32[2,16,8,128]{3,2,1,0:T(8,128)S(1)}, f32[2,16,8,128]{3,2,1,0:T(8,128)S(1)}, u32[]{:S(2)}, u32[]{:S(2)}) %collective-permute-start.6) | collective-permute-done | bytes 131104 | tf_op jit(solution)/shard_map/ppermute | solution.py:146
  22.9 0.0 collective-permute-done.7.far_ref
  22.9 0.3 %shard_map.38 = (f32[4,8,128]{2,1,0:T(8,128)S(1)}, s32[8,128]{1,0:T(8,128)S(1)}) custom-call(f32[2,16,8,128]{3,2,1,0:T(8,128)S(1)} %add.32.own_ref, f32[2,16,8,128]{3,2,1,0:T(8,128)S(1)} %collective-permute-done.6.own_add, f32[2,16,8,128]{3,2,1,0:T(8,128)S(1)} %collective-permute-done.7.far_ref, f32[2,16,8,128]{3,2,1,0:T(8,128)S(1)} %collective-permute-done.8.far_add), custom_call_target="tpu_custom_call" | custom-call | flops 2097152 | bytes 524288 | tf_op jit(solution)/shard_map/pallas_call | solution.py:124
  23.3 0.1 collective-permute-start.9
  23.4 1.2 %collective-permute-done.9 = f32[4,8,128]{2,1,0:T(8,128)S(1)} collective-permute-done((f32[4,8,128]{2,1,0:T(8,128)S(1)}, f32[4,8,128]{2,1,0:T(8,128)S(1)}, u32[]{:S(2)}, u32[]{:S(2)}) %collective-permute-start.9) | collective-permute-done | bytes 16416 | tf_op jit(solution)/shard_map/ppermute | solution.py:150
  24.5 1.2 %collective-permute-start.10 = (f32[2,8,128]{2,1,0:T(8,128)S(1)}, f32[2,8,128]{2,1,0:T(8,128)S(1)}, u32[]{:S(2)}, u32[]{:S(2)}) collective-permute-start(f32[2,8,128]{2,1,0:T(8,128)S(1)} %slice.29), channel_id=1, source_target_pairs={{0,6},{1,7},{2,4},{3,5},{4,2},{5,3},{6,0},{7,1},{8,14},{9,15},{10,... | collective-permute-start | bytes 24584 | tf_op jit(solution)/shard_map/ppermute | solution.py:146
  25.7 1.9 %collective-permute-done.10 = f32[2,8,128]{2,1,0:T(8,128)S(1)} collective-permute-done((f32[2,8,128]{2,1,0:T(8,128)S(1)}, f32[2,8,128]{2,1,0:T(8,128)S(1)}, u32[]{:S(2)}, u32[]{:S(2)}) %collective-permute-start.10) | collective-permute-done | bytes 8224 | tf_op jit(solution)/shard_map/ppermute | solution.py:146
  27.6 2.6 %collective-permute-start.11 = (f32[8,128]{1,0:T(8,128)S(1)}, f32[8,128]{1,0:T(8,128)S(1)}, u32[]{:S(2)}, u32[]{:S(2)}) collective-permute-start(f32[8,128]{1,0:T(8,128)S(1)} %slice_bitcast_fusion), channel_id=1, source_target_pairs={{0,10},{1,11},{2,8},{3,9},{4,14},{5,15},{6,12},{7,13},{8,2},{9,3},... | collective-permute-start | bytes 12296 | tf_op jit(solution)/shard_map/ppermute | solution.py:146
  30.3 1.3 %collective-permute-done.11 = f32[8,128]{1,0:T(8,128)S(1)} collective-permute-done((f32[8,128]{1,0:T(8,128)S(1)}, f32[8,128]{1,0:T(8,128)S(1)}, u32[]{:S(2)}, u32[]{:S(2)}) %collective-permute-start.11) | collective-permute-done | bytes 4128 | tf_op jit(solution)/shard_map/ppermute | solution.py:146
  31.6 0.6 %select_bitcast_fusion = f32[16,4]{0,1:T(4,128)} fusion(f32[8,128]{1,0:T(8,128)S(1)} %fusion, s32[8,128]{1,0:T(8,128)S(1)} %get-tuple-element.25), kind=kLoop, calls=%fused_computation.5 | loop fusion | flops 128 | bytes 1024 | tf_op jit(solution)/shard_map/transpose | solution.py:183
  (10 shorter events, 0.1 us)
Async XLA Ops:
  3.3 1.5 %collective-permute-start.2 = (f32[2,16,8,128]{3,2,1,0:T(8,128)S(1)}, f32[2,16,8,128]{3,2,1,0:T(8,128)S(1)}, u32[]{:S(2)}, u32[]{:S(2)}) collective-permute-start(f32[2,16,8,128]{3,2,1,0:T(8,128)S(1)} %get-tuple-element.21), channel_id=1, source_target_pairs={{0,2},{2,0},{1,3},{3,1},{4,6},{6,4},{5,7},{7,5},{8,10},{10,8},{9,1... | collective-permute-start | bytes 393224 | tf_op jit(solution)/shard_map/ppermute | solution.py:150
  3.8 4.0 %collective-permute-start.4 = (f32[2,16,8,128]{3,2,1,0:T(8,128)S(1)}, f32[2,16,8,128]{3,2,1,0:T(8,128)S(1)}, u32[]{:S(2)}, u32[]{:S(2)}) collective-permute-start(f32[2,16,8,128]{3,2,1,0:T(8,128)S(1)} %get-tuple-element.24), channel_id=1, source_target_pairs={{0,2},{2,0},{1,3},{3,1},{4,6},{6,4},{5,7},{7,5},{8,10},{10,8},{9,1... | collective-permute-start | bytes 393224 | tf_op jit(solution)/shard_map/ppermute | solution.py:150
  3.9 4.1 %collective-permute-start = (f32[2,16,8,128]{3,2,1,0:T(8,128)S(1)}, f32[2,16,8,128]{3,2,1,0:T(8,128)S(1)}, u32[]{:S(2)}, u32[]{:S(2)}) collective-permute-start(f32[2,16,8,128]{3,2,1,0:T(8,128)S(1)} %get-tuple-element.17), channel_id=1, source_target_pairs={{0,2},{2,0},{1,3},{3,1},{4,6},{6,4},{5,7},{7,5},{8,10},{10,8},{9,1... | collective-permute-start | bytes 393224 | tf_op jit(solution)/shard_map/ppermute | solution.py:150
  4.3 3.7 %collective-permute-start.1 = (f32[2,16,8,128]{3,2,1,0:T(8,128)S(1)}, f32[2,16,8,128]{3,2,1,0:T(8,128)S(1)}, u32[]{:S(2)}, u32[]{:S(2)}) collective-permute-start(f32[2,16,8,128]{3,2,1,0:T(8,128)S(1)} %get-tuple-element.19), channel_id=1, source_target_pairs={{0,2},{2,0},{1,3},{3,1},{4,6},{6,4},{5,7},{7,5},{8,10},{10,8},{9,1... | collective-permute-start | bytes 393224 | tf_op jit(solution)/shard_map/ppermute | solution.py:150
  4.8 7.1 %collective-permute-start.3 = (f32[2,16,8,128]{3,2,1,0:T(8,128)S(1)}, f32[2,16,8,128]{3,2,1,0:T(8,128)S(1)}, u32[]{:S(2)}, u32[]{:S(2)}) collective-permute-start(f32[2,16,8,128]{3,2,1,0:T(8,128)S(1)} %add.29), channel_id=1, source_target_pairs={{0,4},{1,5},{2,10},{3,11},{4,0},{5,1},{6,14},{7,15},{8,12},{9,13},... | collective-permute-start | bytes 393224 | tf_op jit(solution)/shard_map/ppermute | solution.py:146
  7.9 8.6 %collective-permute-start.5 = (f32[2,16,8,128]{3,2,1,0:T(8,128)S(1)}, f32[2,16,8,128]{3,2,1,0:T(8,128)S(1)}, u32[]{:S(2)}, u32[]{:S(2)}) collective-permute-start(f32[2,16,8,128]{3,2,1,0:T(8,128)S(1)} %add.31), channel_id=1, source_target_pairs={{0,4},{1,5},{2,10},{3,11},{4,0},{5,1},{6,14},{7,15},{8,12},{9,13},... | collective-permute-start | bytes 393224 | tf_op jit(solution)/shard_map/ppermute | solution.py:146
  11.9 7.0 %collective-permute-start.8 = (f32[2,16,8,128]{3,2,1,0:T(8,128)S(1)}, f32[2,16,8,128]{3,2,1,0:T(8,128)S(1)}, u32[]{:S(2)}, u32[]{:S(2)}) collective-permute-start(f32[2,16,8,128]{3,2,1,0:T(8,128)S(1)} %add_add_fusion), channel_id=1, source_target_pairs={{0,9},{1,8},{2,7},{3,6},{4,13},{5,12},{6,3},{7,2},{8,1},{9,0},{10,... | collective-permute-start | bytes 393224 | tf_op jit(solution)/shard_map/ppermute | solution.py:146
  15.7 7.3 %collective-permute-start.6 = (f32[2,16,8,128]{3,2,1,0:T(8,128)S(1)}, f32[2,16,8,128]{3,2,1,0:T(8,128)S(1)}, u32[]{:S(2)}, u32[]{:S(2)}) collective-permute-start(f32[2,16,8,128]{3,2,1,0:T(8,128)S(1)} %add_add_fusion), channel_id=1, source_target_pairs={{0,8},{1,9},{2,6},{3,7},{4,12},{5,13},{6,2},{7,3},{8,0},{9,1},{10,... | collective-permute-start | bytes 393224 | tf_op jit(solution)/shard_map/ppermute | solution.py:146
  16.5 6.4 %collective-permute-start.7 = (f32[2,16,8,128]{3,2,1,0:T(8,128)S(1)}, f32[2,16,8,128]{3,2,1,0:T(8,128)S(1)}, u32[]{:S(2)}, u32[]{:S(2)}) collective-permute-start(f32[2,16,8,128]{3,2,1,0:T(8,128)S(1)} %add.32.own_ref), channel_id=1, source_target_pairs={{0,1},{1,0},{2,3},{3,2},{4,5},{5,4},{6,7},{7,6},{8,9},{9,8},{10,11... | collective-permute-start | bytes 393224 | tf_op jit(solution)/shard_map/ppermute | solution.py:150
  23.3 1.2 %collective-permute-start.9 = (f32[4,8,128]{2,1,0:T(8,128)S(1)}, f32[4,8,128]{2,1,0:T(8,128)S(1)}, u32[]{:S(2)}, u32[]{:S(2)}) collective-permute-start(f32[4,8,128]{2,1,0:T(8,128)S(1)} %get-tuple-element.26), channel_id=1, source_target_pairs={{0,2},{2,0},{1,3},{3,1},{4,6},{6,4},{5,7},{7,5},{8,10},{10,8},{9,1... | collective-permute-start | bytes 49160 | tf_op jit(solution)/shard_map/ppermute | solution.py:150
  24.5 3.1 %collective-permute-start.10 = (f32[2,8,128]{2,1,0:T(8,128)S(1)}, f32[2,8,128]{2,1,0:T(8,128)S(1)}, u32[]{:S(2)}, u32[]{:S(2)}) collective-permute-start(f32[2,8,128]{2,1,0:T(8,128)S(1)} %slice.29), channel_id=1, source_target_pairs={{0,6},{1,7},{2,4},{3,5},{4,2},{5,3},{6,0},{7,1},{8,14},{9,15},{10,... | collective-permute-start | bytes 24584 | tf_op jit(solution)/shard_map/ppermute | solution.py:146
  27.6 4.0 %collective-permute-start.11 = (f32[8,128]{1,0:T(8,128)S(1)}, f32[8,128]{1,0:T(8,128)S(1)}, u32[]{:S(2)}, u32[]{:S(2)}) collective-permute-start(f32[8,128]{1,0:T(8,128)S(1)} %slice_bitcast_fusion), channel_id=1, source_target_pairs={{0,10},{1,11},{2,8},{3,9},{4,14},{5,15},{6,12},{7,13},{8,2},{9,3},... | collective-permute-start | bytes 12296 | tf_op jit(solution)/shard_map/ppermute | solution.py:146
